TPU v7x, 32 devices: a whole 2x2x4 slice. The times are simulated.
32 devices in a mesh: dp: 4 (over y, x), expert: 8 (over z, core).
Axes of the slice: x: 2, y: 2, z: 4, core: 2. Of those that a mesh axis runs over, the one named last changes fastest.
Arguments:
- tokens: bfloat16 [16384, 768], P(('dp', 'expert')), may hold values from -6 to 6
- cotangent: bfloat16 [16384, 768], P(('dp', 'expert')), may hold values from -6 to 6
- routes: int32 [16384, 2], P(('dp', 'expert')), may hold values from 0 to 3, all different within a row; in each aligned block of 512 rows (0 to 511, 512 to 1023, ...) at most 512 rows name the same one
- attention_weight: float32 [768, 3072], P('expert'), may hold values from -0.57735027 to 0.57735027
- attention_first: float32 [768, 3072], P('expert'), may hold values from -40 to 40
- attention_second: float32 [768, 3072], P('expert'), may hold values from 2.048 to 32.768
- router_weight: float32 [768, 4], P('expert'), may hold values from -0.375 to 0.375
- router_first: float32 [768, 4], P('expert'), may hold values from -768 to 768
- router_second: float32 [768, 4], P('expert'), may hold values from 566.231 to 9122.611
- norm_vectors: float32 [4, 768], P(None, 'expert'), may hold values from -0.3 to 1.3
- norm_first: float32 [4, 768], P(None, 'expert'), may hold values from -64 to 64
- norm_second: float32 [4, 768], P(None, 'expert'), may hold values from 4.096 to 65.536
- widen_weight: float32 [8, 768, 1536], P('expert', 'dp'), may hold values from -0.21875 to 0.21875
- widen_first: float32 [8, 768, 1536], P('expert', 'dp'), may hold values from -16 to 16
- widen_second: float32 [8, 768, 1536], P('expert', 'dp'), may hold values from 0.24576 to 4.096
- narrow_weight: float32 [8, 1536, 768], P('expert', 'dp'), may hold values from -0.21875 to 0.21875
- narrow_first: float32 [8, 1536, 768], P('expert', 'dp'), may hold values from -16 to 16
- narrow_second: float32 [8, 1536, 768], P('expert', 'dp'), may hold values from 0.36864 to 5.7344
Outputs:
- mixed: bfloat16 [16384, 768], P(('dp', 'expert'))
- tokens_grad: float32 [16384, 768], P(('dp', 'expert'))
- attention_mean: float32 [768, 3072], P('expert')
- attention_square: float32 [768, 3072], P('expert')
- attention_updated: float32 [768, 3072], P('expert')
- router_mean: float32 [768, 4], P('expert')
- router_square: float32 [768, 4], P('expert')
- router_updated: float32 [768, 4], P('expert')
- norm_mean: float32 [4, 768], P(None, 'expert')
- norm_square: float32 [4, 768], P(None, 'expert')
- norm_updated: float32 [4, 768], P(None, 'expert')
- widen_mean: float32 [8, 768, 1536], P('expert', 'dp')
- widen_square: float32 [8, 768, 1536], P('expert', 'dp')
- widen_updated: float32 [8, 768, 1536], P('expert', 'dp')
- narrow_mean: float32 [8, 1536, 768], P('expert', 'dp')
- narrow_square: float32 [8, 1536, 768], P('expert', 'dp')
- narrow_updated: float32 [8, 1536, 768], P('expert', 'dp')
Inputs may be any that keep to these rules, and one draw needn't show every extreme that they name: `routes`: each row names two different experts; the rows of one device name one expert at most 512 times, a bound that some block reaches.
All inputs are finite; a program needn't handle non-finite values.
Results may differ from a plain program's by a relative error of at most 0.023.
Values may be sent and summed in bfloat16 or wider, within the bound.
No kernel may reach another device: no remote copies, remote signals or barrier semaphores. Data moves between devices by JAX's collectives and lax.ppermute only.
A program may use at most 256 MiB of HBM per device.

v0:
```python
import jax
import jax.numpy as jnp
from jax import lax
from jax.sharding import PartitionSpec as P

HEADS = 12
HEAD_DIM = 64
SEQ = 197
STEP = 5


HIGHEST = lax.Precision.HIGHEST
NORM_EPS = 1e-06
SCORE_SCALE = 0.125
MASKED = -1000000000.0
BETA_ONE = 0.9
BETA_TWO = 0.999
ADAM_EPS = 1e-08
MATRIX_RATE = 0.04
VECTOR_RATE = 0.2
DECAY = 0.1


def with_halo(block, sides, width):
    for axis, dim in sides:
        count = lax.axis_size(axis)
        forward = [(i, i + 1) for i in range(count - 1)]
        backward = [(target, source) for source, target in forward]
        low = lax.ppermute(
            lax.slice_in_dim(block, block.shape[dim] - width, None, axis=dim), axis, forward
        )
        high = lax.ppermute(lax.slice_in_dim(block, 0, width, axis=dim), axis, backward)
        block = jnp.concatenate([low, block, high], axis=dim)
    return block


def shifted(block, axis, distance):
    devices = range(lax.axis_size(axis))
    route = [(i - distance, i) for i in devices if i - distance in devices]
    return lax.ppermute(block, axis, route)


def layer_norm(values, norm_gain, norm_shift):
    center = values - jnp.mean(values, axis=-1, keepdims=True)
    spread = jnp.mean(center * center, axis=-1, keepdims=True)
    return center * lax.rsqrt(spread + NORM_EPS) * norm_gain + norm_shift


def exact_gelu(values):
    return jax.nn.gelu(values, approximate=False)


def adam_step(weight, first, second, grad, rate, decay):
    new_first = BETA_ONE * first + (1.0 - BETA_ONE) * grad
    new_second = BETA_TWO * second + (1.0 - BETA_TWO) * grad * grad
    mean_hat = new_first / (1.0 - BETA_ONE**STEP)
    square_hat = new_second / (1.0 - BETA_TWO**STEP)
    updated = weight - rate * (mean_hat / (jnp.sqrt(square_hat) + ADAM_EPS) + decay * weight)
    return (new_first, new_second, updated)


def slot_layout(routes, expert_count):
    flat = routes.reshape(-1)
    table = (flat[:, None] == jnp.arange(expert_count, dtype=jnp.int32)[None, :]).astype(jnp.int32)
    before = jnp.cumsum(table, axis=0) - table
    return (flat, jnp.sum(before * table, axis=1))


def to_experts(buffer):
    doubled = jnp.repeat(buffer, 2, axis=0)
    return lax.all_to_all(doubled, "expert", split_axis=0, concat_axis=0, tiled=True)


def both_halves(received, expert_ids, slot_ids):
    slices, capacity, width = received.shape
    summed = jnp.sum(received.astype(jnp.float32).reshape(slices // 2, 2, capacity, width), axis=1)
    return summed[expert_ids, slot_ids]


def masked_scores(queries, all_keys, allowed):
    scores = (
        jnp.einsum("qhd,khd->hqk", queries, all_keys, preferred_element_type=jnp.float32)
        * SCORE_SCALE
    )
    return jnp.where(allowed[None], scores, MASKED)


def local(
    tokens,
    cotangent,
    routes,
    attention_weight,
    attention_first,
    attention_second,
    router_weight,
    router_first,
    router_second,
    norm_vectors,
    norm_first,
    norm_second,
    widen_weight,
    widen_first,
    widen_second,
    narrow_weight,
    narrow_first,
    narrow_second,
):
    device_count = lax.axis_size("expert")
    expert_count = device_count // 2
    rows_dev = tokens.shape[0]
    width = tokens.shape[1]
    capacity = 4 * rows_dev // expert_count
    rim = SEQ - 1
    span = rows_dev + 2 * rim
    attention_low, router_low, norm_low = (
        lax.all_gather(attention_weight.astype(jnp.bfloat16), "expert", axis=0, tiled=True),
        lax.all_gather(router_weight.astype(jnp.bfloat16), "expert", axis=0, tiled=True),
        lax.all_gather(norm_vectors.astype(jnp.bfloat16), "expert", axis=1, tiled=True),
    )
    widen_all, narrow_all = (
        lax.all_gather(widen_weight.astype(jnp.bfloat16), "dp", axis=1, tiled=True),
        lax.all_gather(narrow_weight.astype(jnp.bfloat16), "dp", axis=1, tiled=True),
    )
    widen_low = widen_all[0]
    narrow_low = narrow_all[0]
    norm_float = norm_low.astype(jnp.float32)
    router_float = router_low.astype(jnp.float32)
    triple_weight = attention_low[:, : 3 * width]
    proj_weight = attention_low[:, 3 * width :]
    tokens_float = tokens.astype(jnp.float32)
    hidden_one = layer_norm(tokens_float, norm_float[0], norm_float[1]).astype(jnp.bfloat16)
    triple = jnp.dot(hidden_one, triple_weight, preferred_element_type=jnp.float32).astype(
        jnp.bfloat16
    )
    queries = triple[:, :width].reshape(rows_dev, HEADS, HEAD_DIM)
    extended = with_halo(triple[:, width:], (("expert", 0),), rim)
    all_keys = extended[:, :width].reshape(span, HEADS, HEAD_DIM)
    all_values = extended[:, width:].reshape(span, HEADS, HEAD_DIM)
    group_rows = rows_dev * device_count
    first_row = lax.axis_index("expert") * rows_dev
    query_rows = first_row + jnp.arange(rows_dev, dtype=jnp.int32)
    key_rows = first_row - rim + jnp.arange(span, dtype=jnp.int32)
    allowed = (
        (query_rows[:, None] // SEQ == key_rows[None, :] // SEQ)
        & (key_rows[None, :] >= 0)
        & (key_rows[None, :] < group_rows)
    )
    scores = masked_scores(queries, all_keys, allowed)
    peak = jnp.max(scores, axis=-1, keepdims=True)
    log_total = peak + jnp.log(jnp.sum(jnp.exp(scores - peak), axis=-1, keepdims=True))
    attend_low = jnp.exp(scores - log_total).astype(jnp.bfloat16)
    heads_low = (
        jnp.einsum("hqk,khd->qhd", attend_low, all_values, preferred_element_type=jnp.float32)
        .reshape(rows_dev, width)
        .astype(jnp.bfloat16)
    )
    resid = tokens_float + jnp.dot(heads_low, proj_weight, preferred_element_type=jnp.float32)
    hidden_two = layer_norm(resid, norm_float[2], norm_float[3]).astype(jnp.bfloat16)
    logits = jnp.dot(hidden_two, router_low, preferred_element_type=jnp.float32)
    chooser = (
        routes[:, :, None] == jnp.arange(expert_count, dtype=jnp.int32)[None, None, :]
    ).astype(jnp.float32)
    chosen = jnp.sum(chooser * logits[:, None, :], axis=-1)
    chosen_peak = jnp.max(chosen, axis=-1, keepdims=True)
    raised = jnp.exp(chosen - chosen_peak)
    gates = raised / jnp.sum(raised, axis=-1, keepdims=True)
    expert_ids, slot_ids = slot_layout(routes, expert_count)
    dispatch = (
        jnp.zeros((expert_count, capacity, width), jnp.bfloat16)
        .at[expert_ids, slot_ids]
        .set(jnp.repeat(hidden_two, 2, axis=0))
    )
    expert_rows = to_experts(dispatch).reshape(device_count * capacity, width)
    before_act = jnp.dot(expert_rows, widen_low, preferred_element_type=jnp.float32)
    act_low = exact_gelu(before_act).astype(jnp.bfloat16)
    parts_low = (
        jnp.dot(act_low, narrow_low, preferred_element_type=jnp.float32)
        .astype(jnp.bfloat16)
        .reshape(device_count, capacity, width)
    )
    returned = lax.all_to_all(parts_low, "expert", split_axis=0, concat_axis=0, tiled=True)
    combined = both_halves(returned, expert_ids, slot_ids).reshape(rows_dev, 2, width)
    mixed = (resid + jnp.sum(gates[:, :, None] * combined, axis=1)).astype(jnp.bfloat16)
    grad_output = cotangent.astype(jnp.float32)
    grad_parts = (
        (gates[:, :, None] * grad_output[:, None, :])
        .astype(jnp.bfloat16)
        .reshape(2 * rows_dev, width)
    )
    grad_dispatch = (
        jnp.zeros((expert_count, capacity, width), jnp.bfloat16)
        .at[expert_ids, slot_ids]
        .set(grad_parts)
    )
    grad_rows = to_experts(grad_dispatch).reshape(device_count * capacity, width)
    grad_act = jnp.einsum("rd,fd->rf", grad_rows, narrow_low, preferred_element_type=jnp.float32)
    gelu_pull = jax.vjp(exact_gelu, before_act)[1]
    grad_before = gelu_pull(grad_act)[0].astype(jnp.bfloat16)
    grad_narrow = jnp.einsum("rf,rd->fd", act_low, grad_rows, preferred_element_type=jnp.float32)
    grad_widen = jnp.einsum(
        "rd,rf->df", expert_rows, grad_before, preferred_element_type=jnp.float32
    )
    grad_back = jnp.einsum(
        "rf,df->rd", grad_before, widen_low, preferred_element_type=jnp.float32
    ).reshape(device_count, capacity, width)
    grad_returned = lax.all_to_all(
        grad_back.astype(jnp.bfloat16), "expert", split_axis=0, concat_axis=0, tiled=True
    ).astype(grad_back.dtype)
    grad_hidden = jnp.sum(
        both_halves(grad_returned, expert_ids, slot_ids).reshape(rows_dev, 2, width), axis=1
    )
    grad_gates = jnp.sum(grad_output[:, None, :] * combined, axis=-1)
    grad_chosen = gates * (grad_gates - jnp.sum(gates * grad_gates, axis=-1, keepdims=True))
    grad_logits = jnp.sum(grad_chosen[:, :, None] * chooser, axis=1)
    grad_router = jnp.einsum(
        "rd,re->de", hidden_two.astype(jnp.float32), grad_logits, precision=HIGHEST
    )
    grad_hidden = grad_hidden + jnp.einsum(
        "re,de->rd", grad_logits, router_float, precision=HIGHEST
    )
    pull_two = jax.vjp(layer_norm, resid, norm_float[2], norm_float[3])[1]
    grad_resid_norm, grad_gain_two, grad_shift_two = pull_two(grad_hidden)
    grad_resid = grad_output + grad_resid_norm
    grad_branch = grad_resid.astype(jnp.bfloat16)
    grad_proj = jnp.einsum("rd,re->de", heads_low, grad_branch, preferred_element_type=jnp.float32)
    grad_heads = (
        jnp.einsum("re,de->rd", grad_branch, proj_weight, preferred_element_type=jnp.float32)
        .astype(jnp.bfloat16)
        .reshape(rows_dev, HEADS, HEAD_DIM)
    )
    scores = masked_scores(queries, all_keys, allowed)
    attend = jnp.exp(scores - log_total)
    attend_again = attend.astype(jnp.bfloat16)
    grad_values = jnp.einsum(
        "hqk,qhd->khd", attend_again, grad_heads, preferred_element_type=jnp.float32
    )
    grad_attend = jnp.einsum(
        "qhd,khd->hqk", grad_heads, all_values, preferred_element_type=jnp.float32
    )
    inner = jnp.sum(attend * grad_attend, axis=-1, keepdims=True)
    grad_scores = (attend * (grad_attend - inner)).astype(jnp.bfloat16)
    grad_queries = (
        jnp.einsum("hqk,khd->qhd", grad_scores, all_keys, preferred_element_type=jnp.float32)
        * SCORE_SCALE
    )
    grad_keys = (
        jnp.einsum("hqk,qhd->khd", grad_scores, queries, preferred_element_type=jnp.float32)
        * SCORE_SCALE
    )
    grad_extended = jnp.concatenate(
        [grad_keys.reshape(span, width), grad_values.reshape(span, width)], axis=1
    )
    from_above = shifted(grad_extended[:rim].astype(jnp.bfloat16), "expert", -1).astype(jnp.float32)
    from_below = shifted(grad_extended[rows_dev + rim :].astype(jnp.bfloat16), "expert", 1).astype(
        jnp.float32
    )
    grad_pairs = grad_extended[rim : rim + rows_dev]
    grad_pairs = grad_pairs.at[rows_dev - rim :].add(from_above).at[:rim].add(from_below)
    grad_triple = jnp.concatenate(
        [grad_queries.reshape(rows_dev, width), grad_pairs], axis=1
    ).astype(jnp.bfloat16)
    grad_triple_weight = jnp.einsum(
        "rd,re->de", hidden_one, grad_triple, preferred_element_type=jnp.float32
    )
    grad_hidden_one = jnp.einsum(
        "re,de->rd", grad_triple, triple_weight, preferred_element_type=jnp.float32
    )
    pull_one = jax.vjp(layer_norm, tokens_float, norm_float[0], norm_float[1])[1]
    grad_tokens_norm, grad_gain_one, grad_shift_one = pull_one(grad_hidden_one)
    tokens_grad = grad_resid + grad_tokens_norm
    grad_attention = jnp.concatenate([grad_triple_weight, grad_proj], axis=1)
    grad_vectors = jnp.stack([grad_gain_one, grad_shift_one, grad_gain_two, grad_shift_two], axis=0)
    owned = (
        lax.psum_scatter(grad_attention, "expert", scatter_dimension=0, tiled=True),
        lax.psum_scatter(grad_router, "expert", scatter_dimension=0, tiled=True),
        lax.psum_scatter(grad_vectors, "expert", scatter_dimension=1, tiled=True),
    )
    attention_sum, router_sum, vector_sum = (
        lax.psum(owned[0].astype(jnp.bfloat16), "dp").astype(jnp.float32),
        lax.psum(owned[1].astype(jnp.bfloat16), "dp").astype(jnp.float32),
        lax.psum(owned[2].astype(jnp.bfloat16), "dp").astype(jnp.float32),
    )
    widen_sum, narrow_sum = (
        lax.psum_scatter(
            grad_widen[None].astype(jnp.bfloat16), "dp", scatter_dimension=1, tiled=True
        ).astype(jnp.float32),
        lax.psum_scatter(
            grad_narrow[None].astype(jnp.bfloat16), "dp", scatter_dimension=1, tiled=True
        ).astype(jnp.float32),
    )
    attention_new = adam_step(
        attention_weight, attention_first, attention_second, attention_sum, MATRIX_RATE, DECAY
    )
    router_new = adam_step(
        router_weight, router_first, router_second, router_sum, MATRIX_RATE, DECAY
    )
    norm_new = adam_step(norm_vectors, norm_first, norm_second, vector_sum, VECTOR_RATE, 0.0)
    widen_new = adam_step(widen_weight, widen_first, widen_second, widen_sum, MATRIX_RATE, DECAY)
    narrow_new = adam_step(
        narrow_weight, narrow_first, narrow_second, narrow_sum, MATRIX_RATE, DECAY
    )
    return (
        mixed,
        tokens_grad,
        attention_new[0],
        attention_new[1],
        attention_new[2],
        router_new[0],
        router_new[1],
        router_new[2],
        norm_new[0],
        norm_new[1],
        norm_new[2],
        widen_new[0],
        widen_new[1],
        widen_new[2],
        narrow_new[0],
        narrow_new[1],
        narrow_new[2],
    )


def solution(mesh):
    return jax.shard_map(
        local,
        mesh=mesh,
        in_specs=(
            P(("dp", "expert"), None),
            P(("dp", "expert"), None),
            P(("dp", "expert"), None),
            P("expert", None),
            P("expert", None),
            P("expert", None),
            P("expert", None),
            P("expert", None),
            P("expert", None),
            P(None, "expert"),
            P(None, "expert"),
            P(None, "expert"),
            P("expert", "dp", None),
            P("expert", "dp", None),
            P("expert", "dp", None),
            P("expert", "dp", None),
            P("expert", "dp", None),
            P("expert", "dp", None),
        ),
        out_specs=(
            P(("dp", "expert"), None),
            P(("dp", "expert"), None),
            P("expert", None),
            P("expert", None),
            P("expert", None),
            P("expert", None),
            P("expert", None),
            P("expert", None),
            P(None, "expert"),
            P(None, "expert"),
            P(None, "expert"),
            P("expert", "dp", None),
            P("expert", "dp", None),
            P("expert", "dp", None),
            P("expert", "dp", None),
            P("expert", "dp", None),
            P("expert", "dp", None),
        ),
        check_vma=False,
    )
```

profile of v0, /device:TPU:0, one launch (start us, length us, event | category | flops | bytes accessed | tf_op | source)
XLA Modules:
  0.0 1171.1 jit_solution(16998939208114620360)
XLA Ops:
  11.7 13.4 %all-gather = bf16[8,96,4]{1,2,0:T(4,128)(2,1)S(1)} all-gather(bf16[1,96,4]{1,2,0:T(4,128)(2,1)S(1)} %convert_bitcast_fusion.1), channel_id=1, replica_groups=mesh['dp'=4,'expert'=8] {'expert'}, dimensions={0}, use_global_device_ids=true | all-gather | bytes 6912 | tf_op jit(solution)/shard_map/all_gather | solution.py:118
  28.3 37.2 %all-gather.6.cloned.1.call-done = bf16[768,3072]{1,0:T(8,128)(2,1)} async-done(((bf16[96,3072]{1,0:T(8,128)(2,1)}), bf16[768,3072]{1,0:T(8,128)(2,1)}) %all-gather.6.cloned.1.call-update) | async-done | bytes 4718608 | tf_op jit(solution)/shard_map/all_gather | solution.py:116
  99.6 10.5 convolution_convert_fusion.6
  117.2 7.1 scatter_custom_fusion
  127.3 7.6 all-to-all-start
  135.9 107.1 %all-gather.1 = bf16[8,96,4]{1,2,0:T(4,128)(2,1)S(1)} all-gather(bf16[1,96,4]{1,2,0:T(4,128)(2,1)S(1)} %convert_bitcast_fusion), channel_id=1, replica_groups=mesh['dp'=4,'expert'=8] {'expert'}, dimensions={0}, use_global_device_ids=true | all-gather | bytes 6912 | tf_op jit(solution)/shard_map/all_gather | solution.py:117
  252.6 7.8 scatter_custom_fusion.1
  260.4 14.0 %all-to-all-done = bf16[8,512,768]{2,1,0:T(8,128)(2,1)} async-done(((bf16[8,512,768]{2,1,0:T(8,128)(2,1)}), bf16[8,512,768]{2,1,0:T(8,128)(2,1)}, u32[]{:S(2)}, u32[]{:S(2)}) %all-to-all-start) | async-done | bytes 6291488 | tf_op jit(solution)/shard_map/all_to_all | solution.py:71
  279.5 23.0 %all-to-all-start.2 = ((bf16[8,512,768]{2,1,0:T(8,128)(2,1)}), bf16[8,512,768]{2,1,0:T(8,128)(2,1)}, u32[]{:S(2)}, u32[]{:S(2)}) async-start(bf16[8,512,768]{2,1,0:T(8,128)(2,1)} %bitcast.113), calls=%async_computation.2 | async-start | bytes 12582912 | tf_op jit(solution)/shard_map/all_to_all | solution.py:71
  302.5 64.8 %multiply_convert_fusion = (bf16[4096,1536]{1,0:T(8,128)(2,1)}, f32[4096,1536]{1,0:T(8,128)}, f32[4096,1536]{1,0:T(8,128)}) fusion(bf16[4096,768]{1,0:T(8,128)(2,1)} %bitcast.13, bf16[1,768,1536]{2,1,0:T(8,128)(2,1)} %all-gather.8.cloned.1.call-done), kind=kOutput, calls=%fused_computation.7 | convolution fusion | flops 10072621056 | bytes 71565312 | tf_op jit(solution)/shard_map/dot_general | solution.py:174
  367.4 74.8 %all-to-all-done.2 = bf16[8,512,768]{2,1,0:T(8,128)(2,1)} async-done(((bf16[8,512,768]{2,1,0:T(8,128)(2,1)}), bf16[8,512,768]{2,1,0:T(8,128)(2,1)}, u32[]{:S(2)}, u32[]{:S(2)}) %all-to-all-start.2) | async-done | bytes 6291488 | tf_op jit(solution)/shard_map/all_to_all | solution.py:71
  442.1 16.1 %fusion.14 = bf16[1,1536,768]{2,1,0:T(8,128)(2,1)} fusion(bf16[4096,1536]{1,0:T(8,128)(2,1)} %get-tuple-element.72, bf16[4096,768]{1,0:T(8,128)(2,1)} %bitcast.21), kind=kOutput, calls=%fused_computation.50 | convolution fusion | flops 9664856064 | bytes 21233664 | tf_op jit(solution)/shard_map/rf,rd->fd/dot_general | solution.py:199
  458.3 35.6 %reduce-scatter.14.cloned.1.call-done = bf16[1,384,768]{2,1,0:T(8,128)(2,1)} async-done(((bf16[1,1536,768]{2,1,0:T(8,128)(2,1)}), bf16[1,384,768]{2,1,0:T(8,128)(2,1)}) %reduce-scatter.14.cloned.1.call-update) | async-done | bytes 589840 | tf_op jit(solution)/shard_map/reduce_scatter | solution.py:287
  497.6 37.4 %all-gather.10.cloned.1.call-done = bf16[1,1536,768]{2,1,0:T(8,128)(2,1)} async-done(((bf16[1,384,768]{2,1,0:T(8,128)(2,1)}), bf16[1,1536,768]{2,1,0:T(8,128)(2,1)}) %all-gather.10.cloned.1.call-update) | async-done | bytes 2359312 | tf_op jit(solution)/shard_map/all_gather | solution.py:122
  535.0 15.3 %convolution_convert_fusion = bf16[4096,768]{1,0:T(8,128)(2,1)} fusion(bf16[4096,1536]{1,0:T(8,128)(2,1)} %get-tuple-element.72, bf16[1,1536,768]{2,1,0:T(8,128)(2,1)} %all-gather.10.cloned.1.call-done), kind=kOutput, calls=%fused_computation.36 | convolution fusion | flops 9666822144 | bytes 21233664 | tf_op jit(solution)/shard_map/dot_general | solution.py:177
  555.3 29.8 %add_convert_fusion = bf16[4096,1536]{1,0:T(8,128)(2,1)} fusion(f32[4096,1536]{1,0:T(8,128)} %get-tuple-element.73, f32[4096,1536]{1,0:T(8,128)} %get-tuple-element.89, bf16[4096,768]{1,0:T(8,128)(2,1)} %bitcast.21, bf16[1,1536,768]{2,1,0:T(8,128)(2,1)} %all-gather.10.cloned.1.call-done), kind=kOutput, calls=%fused_computation.6 | convolution fusion | flops 9751756800 | bytes 71565312 | tf_op jit(solution)/shard_map/rd,fd->rf/dot_general | solution.py:196
  585.2 14.7 %convolution_convert_fusion.2 = bf16[8,512,768]{2,1,0:T(8,128)(2,1)} fusion(bf16[8,512,1536]{2,1,0:T(8,128)(2,1)} %bitcast.135, bf16[1,768,1536]{2,1,0:T(8,128)(2,1)S(1)} %copy-done.80), kind=kOutput, calls=%fused_computation.39 | convolution fusion | flops 9666822144 | bytes 21233664 | tf_op jit(solution)/shard_map/rf,df->rd/dot_general | solution.py:203
  599.8 94.4 %all-to-all-done.1 = bf16[8,512,768]{2,1,0:T(8,128)(2,1)} async-done(((bf16[8,512,768]{2,1,0:T(8,128)(2,1)}), bf16[8,512,768]{2,1,0:T(8,128)(2,1)}, u32[]{:S(2)}, u32[]{:S(2)}) %all-to-all-start.1) | async-done | bytes 6291488 | tf_op jit(solution)/shard_map/all_to_all | solution.py:181
  700.3 16.2 %fusion.13 = bf16[1,768,1536]{2,1,0:T(8,128)(2,1)} fusion(bf16[4096,768]{1,0:T(8,128)(2,1)} %bitcast.13, bf16[4096,1536]{1,0:T(8,128)(2,1)} %add_convert_fusion), kind=kOutput, calls=%fused_computation.49 | convolution fusion | flops 9664856064 | bytes 21233664 | tf_op jit(solution)/shard_map/rd,rf->df/dot_general | solution.py:200
  723.6 14.3 %gather_fusion = f32[1024,768]{1,0:T(8,128)S(1)} fusion(f32[4,512,768]{2,1,0:T(8,128)} %convert_reduce_fusion.1, s32[1024]{0:T(1024)S(1)} %bitcast.108), kind=kCustom, calls=%fused_computation | custom fusion | bytes 6299648 | tf_op jit(solution)/shard_map/gather | solution.py:77
  741.0 9.5 multiply_reduce_fusion.1
  750.8 87.2 %all-to-all-done.3 = bf16[8,512,768]{2,1,0:T(8,128)(2,1)} async-done(((bf16[8,512,768]{2,1,0:T(8,128)(2,1)}), bf16[8,512,768]{2,1,0:T(8,128)(2,1)}, u32[]{:S(2)}, u32[]{:S(2)}) %all-to-all-start.3) | async-done | bytes 6291488 | tf_op jit(solution)/shard_map/all_to_all | solution.py:206
  838.0 7.0 convert_reduce_fusion
  845.0 13.7 %gather_fusion.1 = f32[1024,768]{1,0:T(8,128)S(1)} fusion(f32[4,512,768]{2,1,0:T(8,128)} %convert_reduce_fusion, s32[1024]{0:T(1024)S(1)} %bitcast.109), kind=kCustom, calls=%fused_computation.1 | custom fusion | bytes 6299648 | tf_op jit(solution)/shard_map/gather | solution.py:77
  875.1 12.0 %fusion.50 = f32[12,64,904]{2,1,0:T(8,128)} fusion(bf16[512,12,64]{0,2,1:T(8,128)(2,1)S(1)} %bitcast.126, f32[12,512,904]{1,2,0:T(8,128)} %copy-done, f32[12,512]{1,0:T(8,128)S(1)} %copy-done.43, pred[512,904]{0,1:T(8,128)(4,1)S(1)} %copy-done.21), kind=kOutput, calls=%fused_computation.116 | convolution fusion | flops 733151232 | bytes 26267648 | tf_op jit(solution)/shard_map/hqk,qhd->khd/dot_general | solution.py:234
  887.1 15.4 %multiply_reduce_fusion = (f32[12,512]{1,0:T(8,128)S(1)}, f32[12,512,904]{1,2,0:T(8,128)}) fusion(f32[12,512,904]{1,2,0:T(8,128)} %copy-done, f32[12,512]{1,0:T(8,128)S(1)} %copy-done.43, pred[512,904]{0,1:T(8,128)(4,1)S(1)} %copy-done.21, bf16[512,12,64]{0,2,1:T(8,128)(2,1)S(1)} %bitcast.127, bf16[904,12,64]{0,2,1:T(8,128)(2,1)S(1)} %bitcast.122), kind=kOutput, calls=%fused_computation.22 | convolution fusion | flops 738699264 | bytes 47120384 | tf_op jit(solution)/shard_map/qhd,khd->hqk/dot_general | solution.py:237
  905.9 15.1 %multiply_convert_fusion.1 = bf16[12,512,904]{1,2,0:T(8,128)(2,1)S(1)} fusion(f32[12,512,904]{1,2,0:T(8,128)} %get-tuple-element.92, f32[12,512,904]{1,2,0:T(8,128)} %copy-done, f32[12,512]{1,0:T(8,128)S(1)} %get-tuple-element.91, f32[12,512]{1,0:T(8,128)S(1)} %copy-done.43, pred[512,904]{0,1:T(8,128)(4,1)S(1)} %copy-done.21), kind=kLoop, calls=%fused_computation.21 | loop fusion | flops 33325056 | bytes 56053760 | tf_op jit(solution)/shard_map/convert_element_type | solution.py:241
  972.7 8.1 pad_maximum_fusion
  995.9 83.9 %reduce-scatter.10.cloned.1.call-done = f32[96,3072]{1,0:T(8,128)} async-done(((f32[768,3072]{1,0:T(8,128)}), f32[96,3072]{1,0:T(8,128)}) %reduce-scatter.10.cloned.1.call-update) | async-done | bytes 1179664 | tf_op jit(solution)/shard_map/reduce_scatter | solution.py:274
  1085.4 26.3 %reduce-scatter.18.cloned.1.call-done = f32[96,4]{1,0:T(8,128)} async-done(((f32[768,4]{1,0:T(8,128)}), f32[96,4]{1,0:T(8,128)}) %reduce-scatter.18.cloned.1.call-update) | async-done | bytes 1552
  1112.5 9.9 all-reduce
  1123.7 35.1 %all-reduce.3.cloned.1.call-done = bf16[96,3072]{1,0:T(8,128)(2,1)} async-done(((bf16[96,3072]{1,0:T(8,128)(2,1)}), bf16[96,3072]{1,0:T(8,128)(2,1)}) %all-reduce.3.cloned.1.call-update) | async-done | bytes 589840 | tf_op jit(solution)/shard_map/psum | solution.py:279
  (311 shorter events, 189.6 us)
Async XLA Ops:
  8.1 57.5 %all-gather.6.cloned.1.call-start = ((), (), s32[]{:S(2)}) async-start(), calls=%async_computation.9 | async-start | bytes 5308416 | tf_op jit(solution)/shard_map/all_gather | solution.py:116
  27.7 42.0 %copy-start.40 = (f32[768]{0:T(1024)}, f32[768]{0:T(1024)S(1)}, u32[]{:S(2)}) copy-start(f32[768]{0:T(1024)S(1)} %get-tuple-element.52) | copy-start | bytes 9220
  27.7 42.0 %copy-start.46 = (f32[768]{0:T(1024)}, f32[768]{0:T(1024)S(1)}, u32[]{:S(2)}) copy-start(f32[768]{0:T(1024)S(1)} %get-tuple-element.51) | copy-start | bytes 9220
  27.7 85.9 %copy-start.52 = (f32[768]{0:T(1024)}, f32[768]{0:T(1024)S(1)}, u32[]{:S(2)}) copy-start(f32[768]{0:T(1024)S(1)} %get-tuple-element.49) | copy-start | bytes 9220
  27.9 41.8 %copy-start.44 = (f32[512]{0:T(512)}, f32[512]{0:T(512)S(1)}, u32[]{:S(2)}) copy-start(f32[512]{0:T(512)S(1)} %broadcast_multiply_fusion.1) | copy-start | bytes 6148
  28.3 41.5 %copy-start.66 = (f32[512]{0:T(512)}, f32[512]{0:T(512)S(1)}, u32[]{:S(2)}) copy-start(f32[512]{0:T(512)S(1)} %fusion.29) | copy-start | bytes 6148
  28.3 41.5 %copy-start.48 = (f32[512]{0:T(512)}, f32[512]{0:T(512)S(1)}, u32[]{:S(2)}) copy-start(f32[512]{0:T(512)S(1)} %fusion.67) | copy-start | bytes 6148
  70.7 8.8 collective-permute-start
  73.7 5.8 collective-permute-start.1
  127.3 147.1 %all-to-all-start = ((bf16[8,512,768]{2,1,0:T(8,128)(2,1)}), bf16[8,512,768]{2,1,0:T(8,128)(2,1)}, u32[]{:S(2)}, u32[]{:S(2)}) async-start(bf16[8,512,768]{2,1,0:T(8,128)(2,1)} %bitcast.112), calls=%async_computation | async-start | bytes 12582912 | tf_op jit(solution)/shard_map/all_to_all | solution.py:71
  134.9 108.2 %copy-start.14 = (bf16[512,768]{1,0:T(8,128)(2,1)S(1)}, bf16[512,768]{1,0:T(8,128)(2,1)}, u32[]{:S(2)}) copy-start(bf16[512,768]{1,0:T(8,128)(2,1)} %param.23) | copy-start | bytes 2359300
  134.9 167.6 %all-gather.8.cloned.1.call-start = ((), (), s32[]{:S(2)}) async-start(), calls=%async_computation.10 | async-start | bytes 2949120 | tf_op jit(solution)/shard_map/all_gather | solution.py:121
  279.5 162.7 %all-to-all-start.2 = ((bf16[8,512,768]{2,1,0:T(8,128)(2,1)}), bf16[8,512,768]{2,1,0:T(8,128)(2,1)}, u32[]{:S(2)}, u32[]{:S(2)}) async-start(bf16[8,512,768]{2,1,0:T(8,128)(2,1)} %bitcast.113), calls=%async_computation.2 | async-start | bytes 12582912 | tf_op jit(solution)/shard_map/all_to_all | solution.py:71
  302.5 191.5 %reduce-scatter.14.cloned.1.call-start = ((), (), s32[]{:S(2)}) async-start(), calls=%async_computation.15 | async-start | bytes 2949120 | tf_op jit(solution)/shard_map/reduce_scatter | solution.py:287
  442.1 51.8 %copy-start.37 = (f32[1,384,768]{2,1,0:T(8,128)S(1)}, f32[1,384,768]{2,1,0:T(8,128)}, u32[]{:S(2)}) copy-start(f32[1,384,768]{2,1,0:T(8,128)} %param.38) | copy-start | bytes 3538948
  458.3 76.7 %all-gather.10.cloned.1.call-start = ((), (), s32[]{:S(2)}) async-start(), calls=%async_computation.11 | async-start | bytes 2949120 | tf_op jit(solution)/shard_map/all_gather | solution.py:122
  550.3 144.0 %all-to-all-start.1 = ((bf16[8,512,768]{2,1,0:T(8,128)(2,1)}), bf16[8,512,768]{2,1,0:T(8,128)(2,1)}, u32[]{:S(2)}, u32[]{:S(2)}) async-start(bf16[8,512,768]{2,1,0:T(8,128)(2,1)} %bitcast.123), calls=%async_computation.1 | async-start | bytes 12582912 | tf_op jit(solution)/shard_map/all_to_all | solution.py:181
  599.8 99.3 %copy-start.15 = (bf16[512,768]{1,0:T(8,128)(2,1)S(1)}, bf16[512,768]{1,0:T(8,128)(2,1)}, u32[]{:S(2)}) copy-start(bf16[512,768]{1,0:T(8,128)(2,1)} %param.23) | copy-start | bytes 2359300
  694.3 143.7 %all-to-all-start.3 = ((bf16[8,512,768]{2,1,0:T(8,128)(2,1)}), bf16[8,512,768]{2,1,0:T(8,128)(2,1)}, u32[]{:S(2)}, u32[]{:S(2)}) async-start(bf16[8,512,768]{2,1,0:T(8,128)(2,1)} %convolution_convert_fusion.2), calls=%async_computation.3 | async-start | bytes 12582912 | tf_op jit(solution)/shard_map/all_to_all | solution.py:206
  699.0 281.9 %reduce-scatter.12.cloned.1.call-start = ((), (), s32[]{:S(2)}) async-start(), calls=%async_computation.14 | async-start | bytes 2949120 | tf_op jit(solution)/shard_map/reduce_scatter | solution.py:284
  716.6 271.0 %reduce-scatter.16.cloned.1.call-start = ((), (), s32[]{:S(2)}) async-start(), calls=%async_computation.16 | async-start | bytes 442368
  934.1 17.4 %collective-permute-start.2 = (bf16[196,1536]{1,0:T(8,128)(2,1)}, bf16[196,1536]{1,0:T(8,128)(2,1)}, u32[]{:S(2)}, u32[]{:S(2)}) collective-permute-start(bf16[196,1536]{1,0:T(8,128)(2,1)} %get-tuple-element.75), channel_id=1, source_target_pairs={{1,0},{2,1},{3,2},{4,3},{5,4},{6,5},{7,6},{9,8},{10,9},{11,10},{12... | collective-permute-start | bytes 1806344 | tf_op jit(solution)/shard_map/ppermute | solution.py:40
  935.7 22.8 %collective-permute-start.3 = (bf16[196,1536]{1,0:T(8,128)(2,1)}, bf16[196,1536]{1,0:T(8,128)(2,1)}, u32[]{:S(2)}, u32[]{:S(2)}) collective-permute-start(bf16[196,1536]{1,0:T(8,128)(2,1)} %get-tuple-element.74), channel_id=1, source_target_pairs={{0,1},{1,2},{2,3},{3,4},{4,5},{5,6},{6,7},{8,9},{9,10},{10,11},{11... | collective-permute-start | bytes 1806344 | tf_op jit(solution)/shard_map/ppermute | solution.py:40
  951.4 128.5 %reduce-scatter.10.cloned.1.call-start = ((), (), s32[]{:S(2)}) async-start(), calls=%async_computation.12 | async-start | bytes 10616832 | tf_op jit(solution)/shard_map/reduce_scatter | solution.py:274
  980.9 130.8 %reduce-scatter.18.cloned.1.call-start = ((), (), s32[]{:S(2)}) async-start(), calls=%async_computation.17 | async-start | bytes 442368
  994.0 88.0 %copy-start.13 = (f32[512,768]{1,0:T(8,128)S(1)}, f32[512,768]{1,0:T(8,128)}, u32[]{:S(2)}) copy-start(f32[512,768]{1,0:T(8,128)} %copy-done.11) | copy-start | bytes 4718596
  994.0 88.0 %copy-start.17 = (bf16[512,768]{1,0:T(8,128)(2,1)S(1)}, bf16[512,768]{1,0:T(8,128)(2,1)}, u32[]{:S(2)}) copy-start(bf16[512,768]{1,0:T(8,128)(2,1)} %param.23) | copy-start | bytes 2359300
  995.9 162.9 %all-reduce.3.cloned.1.call-start = ((), (), s32[]{:S(2)}) async-start(), calls=%async_computation.13 | async-start | bytes 1179648 | tf_op jit(solution)/shard_map/psum | solution.py:279
  1082.1 40.4 %copy-start.71 = (f32[4,96]{1,0:T(4,128)S(1)}, f32[4,96]{1,0:T(4,128)}, u32[]{:S(2)}) copy-start(f32[4,96]{1,0:T(4,128)} %param.31) | copy-start | bytes 4612
  1082.1 41.0 %copy-start.73 = (f32[96,4]{0,1:T(4,128)S(1)}, f32[96,4]{0,1:T(4,128)}, u32[]{:S(2)}) copy-start(f32[96,4]{0,1:T(4,128)} %param.28) | copy-start | bytes 4612
  1082.1 41.0 %copy-start.76 = (f32[96,4]{0,1:T(4,128)S(1)}, f32[96,4]{0,1:T(4,128)}, u32[]{:S(2)}) copy-start(f32[96,4]{0,1:T(4,128)} %param.30) | copy-start | bytes 4612
  1082.1 40.9 %copy-start.77 = (f32[96,4]{0,1:T(4,128)S(1)}, f32[96,4]{0,1:T(4,128)}, u32[]{:S(2)}) copy-start(f32[96,4]{0,1:T(4,128)} %param.29) | copy-start | bytes 4612
  (69 other events, 570.7 us)
Sparse Core Ops, SparseCore 0:
  11.1 54.3 all-gather.5
Sparse Core Ops, SparseCore 1:
  137.8 38.7 all-gather.7
  458.4 35.5 reduce-scatter.13
  497.7 37.3 all-gather.9
  716.7 37.5 reduce-scatter.11
  951.5 28.4 reduce-scatter.15
  982.4 97.4 reduce-scatter.9
  1082.6 28.9 reduce-scatter.17
  1115.1 43.6 all-reduce.2
where the time goes:
time: 1180 us; the launch traced here: 1170 us
  waiting for transfers between devices  526 us (45%)
  matrix products  235 us (20%)
  blocking collectives  130 us (11%)
  other arithmetic  109 us (9%)
  local copies, waits for them, and re-layouts  103 us (9%)
  starting transfers between devices  50.9 us (4%)
  between operations  17 us (1%)
    all_gather x1, blocking collectives, local(): lax.all_gather(router_weight.astype(jnp.bfloat16), 'expert', axis=0, tile...  107 us
    all_to_all x1, waiting for transfers between devices, local(): lax.all_to_all(parts_low, 'expert', split_axis=0, concat_axis=0, tiled=True)  94.4 us
    all_to_all x2, waiting for transfers between devices, to_experts(): lax.all_to_all(doubled, 'expert', split_axis=0, concat_axis=0, tiled=True)  88.8 us
    all_to_all x1, waiting for transfers between devices, local(): lax.all_to_all(grad_back.astype(jnp.bfloat16), 'expert', split_axis=0, co...  87.2 us
    reduce_scatter x1, waiting for transfers between devices, local(): lax.psum_scatter(grad_attention, 'expert', scatter_dimension=0, tiled=True)  83.9 us
    dot_general x1, matrix products, local(): jnp.dot(expert_rows, widen_low, preferred_element_type=jnp.float32)  64.8 us
    all_gather x1, waiting for transfers between devices, local(): lax.all_gather(narrow_weight.astype(jnp.bfloat16), 'dp', axis=1, tiled=True)  37.4 us
    all_gather x1, waiting for transfers between devices, local(): lax.all_gather(attention_weight.astype(jnp.bfloat16), 'expert', axis=0, t...  37.2 us
  transfers between devices with their start and end apart: 17, of which 10 were waited for; matrix products, arithmetic and copies ran while one was open for 30% of the time, Pallas kernels for 0%

commit v1 on v0

v1 whole, which is shorter than its diff:
```python
import functools

import jax
import jax.numpy as jnp
from jax import lax
from jax.experimental import pallas as pl
from jax.experimental.pallas import tpu as pltpu
from jax.sharding import PartitionSpec as P

HEADS = 12
HEAD_DIM = 64
SEQ = 197
STEP = 5

HIGHEST = lax.Precision.HIGHEST
NORM_EPS = 1e-06
SCORE_SCALE = 0.125
MASKED = -1000000000.0
BETA_ONE = 0.9
BETA_TWO = 0.999
ADAM_EPS = 1e-08
MATRIX_RATE = 0.04
VECTOR_RATE = 0.2
DECAY = 0.1

F32 = jnp.float32
BF16 = jnp.bfloat16
LANES = 128
HALO = 256
QUERY_TILE = 256
ROW_TILE = 256
VMEM_LIMIT = 56 * 1024 * 1024
EXTRA = 16
EXPERT_VMEM = 32 * 1024 * 1024


def tie_kernel(*refs):
    pass


def tie(block, *dependencies):
    anywhere = pl.BlockSpec(memory_space=pl.ANY)
    return pl.pallas_call(
        tie_kernel,
        out_shape=jax.ShapeDtypeStruct(block.shape, block.dtype),
        in_specs=[anywhere] * (1 + len(dependencies)),
        out_specs=anywhere,
        input_output_aliases={0: 0},
        name="tie",
    )(block, *dependencies)


def hop(block, distance):
    count = lax.axis_size("expert")
    return lax.ppermute(block, "expert", [(i, (i + distance) % count) for i in range(count)])


def ring(block):
    return hop(block, 2)


def pair(block):
    return lax.ppermute(block, "expert", [(i, i ^ 1) for i in range(lax.axis_size("expert"))])


def across(block, bit):
    return lax.ppermute(block, "dp", [(i, i ^ bit) for i in range(lax.axis_size("dp"))])


def place_kernel(index, block, *refs):
    refs[-1][0] = block[...]


def place(out, count, block, index):
    anywhere = [pl.BlockSpec(memory_space=pl.ANY)]
    half = (block.shape[0] // 2,) + block.shape[1:]
    return pl.pallas_call(
        place_kernel,
        grid_spec=pltpu.PrefetchScalarGridSpec(
            num_scalar_prefetch=1,
            grid=(2,),
            in_specs=[pl.BlockSpec(half, lambda i, t: (i, 0))] + ([] if out is None else anywhere),
            out_specs=pl.BlockSpec((1,) + half, lambda i, t: (t[0], i, 0)),
        ),
        out_shape=jax.ShapeDtypeStruct((count,) + block.shape, block.dtype),
        input_output_aliases={} if out is None else {2: 0},
        cost_estimate=pl.CostEstimate(
            flops=0, bytes_accessed=2 * block.size * block.dtype.itemsize, transcendentals=0
        ),
        name="place",
    )(*((index.reshape(1), block) + (() if out is None else (out,))))


def gather_dp_near(block):
    count = lax.axis_size("dp")
    if count != 4:
        return lax.all_gather(block, "dp", axis=0), None
    me = lax.axis_index("dp")
    out = place(None, count, block, me)
    for bits in (1, 2):
        out = place(out, count, across(block, bits), me ^ bits)
    return out, across(block, 3)


def gather_dp_far(out, far):
    return out if far is None else place(out, out.shape[0], far, lax.axis_index("dp") ^ 3)


def added(*parts):
    total = parts[0].astype(F32)
    for part in parts[1:]:
        total = total + part.astype(F32)
    return total


def scatter_dp_start(parts):
    one, two = lax.axis_index("dp") % 2, lax.axis_index("dp") // 2
    half = parts.shape[1] // 2
    grid = parts.reshape((2, 2) + parts.shape[1:])
    first, second = grid[:, :, :half], grid[:, :, half:]
    first_got = across(lax.dynamic_index_in_dim(first, 1 - one, 1, False), 1)
    second_got = across(lax.dynamic_index_in_dim(second, 1 - two, 0, False), 2)
    return first, second, first_got, second_got


def scatter_dp_middle(state, then):
    one, two = lax.axis_index("dp") % 2, lax.axis_index("dp") // 2
    first, second, first_got, second_got = state
    first_got, second_got = tie(first_got, then), tie(second_got, then)
    first_sum = added(lax.dynamic_index_in_dim(first, one, 1, False), first_got).astype(BF16)
    second_sum = added(lax.dynamic_index_in_dim(second, two, 0, False), second_got).astype(BF16)
    first_got = across(lax.dynamic_index_in_dim(first_sum, 1 - two, 0, False), 2)
    second_got = across(lax.dynamic_index_in_dim(second_sum, 1 - one, 0, False), 1)
    return first_sum, second_sum, first_got, second_got


def scatter_dp_end(state, then):
    one, two = lax.axis_index("dp") % 2, lax.axis_index("dp") // 2
    first_sum, second_sum, first_got, second_got = state
    first_got, second_got = tie(first_got, then), tie(second_got, then)
    first_sum = added(lax.dynamic_index_in_dim(first_sum, two, 0, False), first_got)
    second_sum = added(lax.dynamic_index_in_dim(second_sum, one, 0, False), second_got)
    return jnp.concatenate([first_sum, second_sum], axis=0)


def gather_expert(block, by_hops):
    count = lax.axis_size("expert")
    if not by_hops:
        return lax.all_gather(block, "expert", axis=0)
    chip, core = lax.axis_index("expert") // 2, lax.axis_index("expert") % 2
    given = pair(block)
    both = jnp.where(core == 0, jnp.stack([block, given]), jnp.stack([given, block]))
    blocks = [both] + [hop(both, 2 * step) for step in range(1, count // 2)]
    pieces = []
    for place in range(count // 2):
        piece = blocks[0]
        for step in range(1, count // 2):
            piece = jnp.where((place + step) % (count // 2) == chip, blocks[step], piece)
        pieces.append(piece)
    return jnp.concatenate(pieces, axis=0)


def sum_to_owner(cut, then=(None, None, None, None)):
    replicas, chips = cut.shape[1], cut.shape[2]
    chip, core = lax.axis_index("expert") // 2, lax.axis_index("expert") % 2
    me = lax.axis_index("dp")

    def held(got, place):
        return got if then[place] is None else [tie(got[0], then[place])] + got[1:]

    got = held([pair(lax.dynamic_index_in_dim(cut, 1 - core, 0, False))], 0)
    over_pair = added(lax.dynamic_index_in_dim(cut, core, 0, False), *got).astype(BF16)
    got = [
        across(lax.dynamic_index_in_dim(over_pair, me ^ bits, 0, False), bits)
        for bits in range(1, replicas)
    ]
    got = held(got, 1)
    over_dp = added(lax.dynamic_index_in_dim(over_pair, me, 0, False), *got).astype(BF16)
    got = [
        hop(lax.dynamic_index_in_dim(over_dp, (chip + step) % chips, 0, False), 2 * step)
        for step in range(1, chips)
    ]
    got = held(got, 2)
    owned = added(lax.dynamic_index_in_dim(over_dp, chip, 0, False), *got).astype(BF16)
    got = held([across(owned, bits) for bits in range(1, replicas)], 3)
    blocks = [owned] + got
    pieces = []
    for place in range(replicas):
        piece = blocks[0]
        for bits in range(1, replicas):
            piece = jnp.where(place ^ bits == me, blocks[bits], piece)
        pieces.append(piece.astype(F32))
    return jnp.concatenate(pieces, axis=0), (over_pair, over_dp, owned)


def standardised(values):
    center = values - jnp.mean(values, axis=-1, keepdims=True)
    spread = jnp.mean(center * center, axis=-1, keepdims=True)
    inverse = lax.rsqrt(spread + NORM_EPS)
    return center * inverse, inverse


def norm_pull(grad, unit, inverse, gain):
    scaled = grad * gain
    mean = jnp.mean(scaled, axis=-1, keepdims=True)
    along = jnp.mean(scaled * unit, axis=-1, keepdims=True)
    return inverse * (scaled - mean - unit * along)


def exact_gelu(values):
    return jax.nn.gelu(values, approximate=False)


def adam_step(weight, first, second, grad, rate, decay):
    new_first = BETA_ONE * first + (1.0 - BETA_ONE) * grad
    new_second = BETA_TWO * second + (1.0 - BETA_TWO) * grad * grad
    mean_hat = new_first / (1.0 - BETA_ONE**STEP)
    square_hat = new_second / (1.0 - BETA_TWO**STEP)
    updated = weight - rate * (mean_hat / (jnp.sqrt(square_hat) + ADAM_EPS) + decay * weight)
    return (new_first, new_second, updated)


def dot_nt(left, right):
    return lax.dot_general(left, right, (((1,), (1,)), ((), ())), preferred_element_type=F32)


def dot_tn(left, right):
    return lax.dot_general(left, right, (((0,), (0,)), ((), ())), preferred_element_type=F32)


def dot_nn(left, right):
    return jnp.dot(left, right, preferred_element_type=F32)


def head_lanes(head):
    lane = lax.broadcasted_iota(jnp.int32, (1, LANES), 1)
    return (lane // HEAD_DIM) == head


def attend_kernel(query_image, key_image, q_ref, k_ref, v_ref, out_ref):
    rows = out_ref.shape[0]
    window = QUERY_TILE + 2 * HALO
    for tile in range(rows // QUERY_TILE):
        low = tile * QUERY_TILE
        queries = q_ref[HALO + low : HALO + low + QUERY_TILE, :] * SCORE_SCALE
        keys = k_ref[low : low + window, :]
        values = v_ref[low : low + window, :]
        allowed = query_image[low : low + QUERY_TILE, :] == key_image[:, low : low + window]
        result = None
        for head in range(LANES // HEAD_DIM):
            lanes = head_lanes(head)
            scores = dot_nt(jnp.where(lanes, queries, 0).astype(BF16), keys)
            scores = jnp.where(allowed, scores, MASKED)
            raised = jnp.exp(scores - jnp.max(scores, axis=-1, keepdims=True))
            attend = raised * (1.0 / jnp.sum(raised, axis=-1, keepdims=True))
            found = dot_nn(attend.astype(BF16), values)
            result = found if result is None else jnp.where(lanes, found, result)
        out_ref[low : low + QUERY_TILE, :] = result.astype(BF16)


def attention(triple, query_image, key_image):
    span = triple.shape[0]
    rows = span - 2 * HALO
    width = triple.shape[1] // 3
    blocks = width // LANES
    cost = HEADS * rows * (QUERY_TILE + 2 * HALO)
    return pl.pallas_call(
        attend_kernel,
        grid=(blocks,),
        in_specs=[
            pl.BlockSpec((rows, 1), lambda i: (0, 0)),
            pl.BlockSpec((1, span), lambda i: (0, 0)),
            pl.BlockSpec((span, LANES), lambda i: (0, i)),
            pl.BlockSpec((span, LANES), lambda i: (0, blocks + i)),
            pl.BlockSpec((span, LANES), lambda i: (0, 2 * blocks + i)),
        ],
        out_specs=pl.BlockSpec((rows, LANES), lambda i: (0, i)),
        out_shape=jax.ShapeDtypeStruct((rows, width), BF16),
        compiler_params=pltpu.CompilerParams(vmem_limit_bytes=VMEM_LIMIT),
        cost_estimate=pl.CostEstimate(
            flops=cost * 512, bytes_accessed=span * width * 6, transcendentals=cost
        ),
        name="attention",
    )(query_image[:, None], key_image[None, :], triple, triple, triple)


def attend_back_kernel(query_image, key_image, q_ref, k_ref, v_ref, g_ref, out_ref, dk, dv):
    rows = g_ref.shape[0]
    span = k_ref.shape[0]
    width = out_ref.shape[1] // 3
    window = QUERY_TILE + 2 * HALO
    column = pl.program_id(0) * LANES

    def columns(part):
        return pl.ds(pl.multiple_of(part * width + column, LANES), LANES)

    dk[...] = jnp.zeros_like(dk)
    dv[...] = jnp.zeros_like(dv)
    out_ref[:HALO, columns(0)] = jnp.zeros((HALO, LANES), BF16)
    out_ref[span - HALO :, columns(0)] = jnp.zeros((HALO, LANES), BF16)
    for tile in range(rows // QUERY_TILE):
        low = tile * QUERY_TILE
        queries = q_ref[HALO + low : HALO + low + QUERY_TILE, :] * SCORE_SCALE
        grads = g_ref[low : low + QUERY_TILE, :]
        keys = k_ref[low : low + window, :]
        values = v_ref[low : low + window, :]
        allowed = key_image[low : low + window, :] == query_image[:, low : low + QUERY_TILE]
        query_grad = None
        for head in range(LANES // HEAD_DIM):
            lanes = head_lanes(head)
            own_queries = jnp.where(lanes, queries, 0).astype(BF16)
            own_grads = jnp.where(lanes, grads, 0).astype(BF16)
            scores = jnp.where(allowed, dot_nt(keys, own_queries), MASKED)
            raised = jnp.exp(scores - jnp.max(scores, axis=0, keepdims=True))
            attend = raised * (1.0 / jnp.sum(raised, axis=0, keepdims=True))
            dv[low : low + window, :] += dot_nn(attend.astype(BF16), own_grads)
            pulled = dot_nt(values, own_grads)
            inner = jnp.sum(attend * pulled, axis=0, keepdims=True)
            score_grad = (attend * (pulled - inner)).astype(BF16)
            dk[low : low + window, :] += dot_nn(score_grad, own_queries)
            found = dot_tn(score_grad, keys) * SCORE_SCALE
            query_grad = found if query_grad is None else jnp.where(lanes, found, query_grad)
        out_ref[HALO + low : HALO + low + QUERY_TILE, columns(0)] = query_grad.astype(BF16)
    out_ref[:, columns(1)] = dk[...].astype(BF16)
    out_ref[:, columns(2)] = dv[...].astype(BF16)


def attention_back(triple, grads, query_image, key_image):
    span = triple.shape[0]
    rows = span - 2 * HALO
    width = triple.shape[1] // 3
    blocks = width // LANES
    cost = HEADS * rows * (QUERY_TILE + 2 * HALO)
    return pl.pallas_call(
        attend_back_kernel,
        grid=(blocks,),
        in_specs=[
            pl.BlockSpec((1, rows), lambda i: (0, 0)),
            pl.BlockSpec((span, 1), lambda i: (0, 0)),
            pl.BlockSpec((span, LANES), lambda i: (0, i)),
            pl.BlockSpec((span, LANES), lambda i: (0, blocks + i)),
            pl.BlockSpec((span, LANES), lambda i: (0, 2 * blocks + i)),
            pl.BlockSpec((rows, LANES), lambda i: (0, i)),
        ],
        out_specs=pl.BlockSpec((span, 3 * width), lambda i: (0, 0)),
        out_shape=jax.ShapeDtypeStruct((span, 3 * width), BF16),
        scratch_shapes=[pltpu.VMEM((span, LANES), F32), pltpu.VMEM((span, LANES), F32)],
        compiler_params=pltpu.CompilerParams(vmem_limit_bytes=VMEM_LIMIT),
        cost_estimate=pl.CostEstimate(
            flops=cost * 1280, bytes_accessed=span * width * 14, transcendentals=cost
        ),
        name="attention_back",
    )(query_image[None, :], key_image[:, None], triple, triple, triple, grads)


def first_norm_kernel(below, tokens, above, vectors, out):
    low = 0
    for block in (below, tokens, above):
        unit, _ = standardised(block[...].astype(F32))
        out[low : low + block.shape[0], :] = (unit * vectors[0:1] + vectors[1:2]).astype(BF16)
        low += block.shape[0]


def first_norm(below, tokens, above, vectors):
    span, width = tokens.shape[0] + 2 * HALO, tokens.shape[1]
    return pl.pallas_call(
        first_norm_kernel,
        out_shape=jax.ShapeDtypeStruct((span, width), BF16),
        compiler_params=pltpu.CompilerParams(vmem_limit_bytes=VMEM_LIMIT),
        cost_estimate=pl.CostEstimate(
            flops=span * width * 10, bytes_accessed=span * width * 4, transcendentals=0
        ),
        name="first_norm",
    )(below, tokens, above, vectors)


def dense_back_kernel(
    layout, hidden, below, tokens, above, grads, weight, small, dense_out, back_out
):
    cores, replicas, chips, rows = layout
    width = hidden.shape[1]
    gain = jnp.zeros((1, width), F32)
    shift = jnp.zeros((1, width), F32)
    low = 0
    for block in (below, tokens, above):
        here = slice(low, low + block.shape[0])
        back = dot_nt(grads[here, :], weight[...])
        back_out[here, :] = back.astype(BF16)
        unit, _ = standardised(block[...].astype(F32))
        gain += jnp.sum(back * unit, axis=0, keepdims=True)
        shift += jnp.sum(back, axis=0, keepdims=True)
        low += block.shape[0]
    sums = jnp.concatenate(
        [
            gain,
            shift,
            jnp.zeros((6, width), F32),
        ],
        axis=0,
    )
    lane = lax.broadcasted_iota(jnp.int32, (8, LANES), 1)
    row = lax.broadcasted_iota(jnp.int32, (8, LANES), 0)
    spread = (lane == row).astype(F32)

    def store(low, block):
        for chip in range(chips):
            for core in range(cores):
                for replica in range(replicas):
                    start = ((chip * cores + core) * replicas + replica) * rows
                    piece = block[start : start + rows].astype(BF16)
                    dense_out[core, replica, chip, :, low : low + block.shape[1]] = piece

    for low in range(0, 3 * width, width):
        store(low, dot_tn(hidden[...], grads[:, low : low + width]))
    store(
        3 * width,
        lax.dot_general(
            small[...] + sums,
            spread,
            (((0,), (0,)), ((), ())),
            precision=HIGHEST,
            preferred_element_type=F32,
        ),
    )


def dense_back(hidden, below, tokens, above, grads, weight, small, layout):
    span, width = hidden.shape
    columns = 3 * width + LANES
    return pl.pallas_call(
        functools.partial(dense_back_kernel, layout),
        out_shape=[
            jax.ShapeDtypeStruct(layout + (columns,), BF16),
            jax.ShapeDtypeStruct((span, width), BF16),
        ],
        compiler_params=pltpu.CompilerParams(vmem_limit_bytes=VMEM_LIMIT),
        cost_estimate=pl.CostEstimate(
            flops=span * width * width * 12,
            bytes_accessed=span * width * 16 + width * width * 12,
            transcendentals=0,
        ),
        name="dense_back",
    )(hidden, below, tokens, above, grads, weight, small)


def small_adam_kernel(sums, *refs):
    values = [ref[...] for ref in refs[:6]]
    vectors, matrix = refs[0].shape[0], refs[3].shape[1]
    rows = sums.shape[0]
    lane = lax.broadcasted_iota(jnp.int32, (rows, rows), 1)
    row = lax.broadcasted_iota(jnp.int32, (rows, rows), 0)
    turned = lax.dot_general(
        sums[...],
        (lane == row).astype(F32),
        (((0,), (0,)), ((), ())),
        precision=HIGHEST,
        preferred_element_type=F32,
    )
    found = adam_step(*values[:3], turned[:vectors], VECTOR_RATE, 0.0)
    found += adam_step(
        *values[3:], sums[:, vectors : vectors + matrix], MATRIX_RATE, DECAY
    )
    for ref, value in zip(refs[6:], found):
        ref[...] = value


def small_adam(sums, *arrays):
    return pl.pallas_call(
        small_adam_kernel,
        out_shape=[jax.ShapeDtypeStruct(array.shape, F32) for array in arrays],
        name="small_adam",
    )(sums, *arrays)


def gelu_and_slope(values):
    inverse = 1.0 / (1.0 + (0.3275911 * 0.7071067811865476) * jnp.abs(values))
    fit = 1.061405429 * inverse - 1.453152027
    fit = fit * inverse + 1.421413741
    fit = fit * inverse - 0.284496736
    fit = fit * inverse + 0.254829592
    bell = jnp.exp(-0.5 * values * values)
    tail = (0.5 * fit) * (inverse * bell)
    share = jnp.where(values >= 0.0, 1.0 - tail, tail)
    return values * share, share + values * (bell * 0.3989422804014327)


def expert_kernel(first, target, rows_ref, grads_ref, gates, mark, place, weights, *refs):
    outs = refs if first else refs[5:]
    act_out, pre_out, part_out, rows_out, mixed_out, back_out = outs
    tile = pl.program_id(0)
    rows = rows_ref[...]
    gate = dot_tn(gates[...], mark[...])
    width = rows.shape[1]
    gate = jnp.concatenate([gate] * (width // LANES), axis=1)
    grads_float = grads_ref[...].astype(F32)
    grad_part = (gate * grads_float).astype(BF16)
    rows_out[...] = rows
    part_out[...] = grad_part
    part = None
    back = None
    replicas, parts, size = weights.shape
    quarter = parts // 4
    narrow_all = weights[:, 2 * quarter :, :].reshape(2 * size, width)
    for turn in range(2):
        here = slice(turn * size, (turn + 1) * size)
        widen = weights[:, turn * quarter : (turn + 1) * quarter, :].reshape(width, size)
        narrow = narrow_all[here, :]
        before = dot_nn(rows, widen)
        pulled = dot_nt(grad_part, narrow)
        act, slope = gelu_and_slope(before)
        act = act.astype(BF16)
        grad_pre = (pulled * slope).astype(BF16)
        act_out[:, here] = act
        pre_out[:, here] = grad_pre
        part_here = dot_nn(act, narrow)
        back_here = dot_nt(grad_pre, widen)
        part = part_here if part is None else part + part_here
        back = back_here if back is None else back + back_here
    part = part.astype(BF16).astype(F32)
    product = part * grads_float
    folded = product[:, :LANES]
    for low in range(LANES, width, LANES):
        folded = folded + product[:, low : low + LANES]
    dots = lax.dot_general(
        jnp.ones((EXTRA, LANES), F32),
        folded,
        (((1,), (1,)), ((), ())),
        precision=HIGHEST,
        preferred_element_type=F32,
    )
    high = dots.astype(BF16).astype(F32)
    dots = high * place[0] + (dots - high) * place[1]
    mixed_out[...] = (gate * part).astype(BF16)
    count = rows.shape[0]
    back_out[pl.ds(pl.multiple_of(tile * count, count), count), :] = back.astype(BF16)
    extra = slice(back_out.shape[0] - EXTRA, back_out.shape[0])
    back_out[extra, pl.ds(pl.multiple_of(tile * count, count), count)] = dots.astype(BF16)


def expert_block(place, places, target, payload, grads_block, marks, weights, kept):
    rows, width = grads_block.shape
    replicas, parts, _ = weights.shape
    hidden = parts * replicas // 2
    tiles = rows // ROW_TILE
    every = places * rows
    by_tile = pl.BlockSpec((ROW_TILE, width), lambda i, t: (i, 0))
    at = lambda i, t: (place * tiles + i, 0)
    whole = lambda i, t: (0, 0)
    first = kept is None
    kept = () if first else kept
    gate_mark, dot_mark = marks
    return pl.pallas_call(
        functools.partial(expert_kernel, first),
        grid_spec=pltpu.PrefetchScalarGridSpec(
            num_scalar_prefetch=1,
            grid=(tiles,),
            in_specs=[
                by_tile,
                by_tile,
                pl.BlockSpec((EXTRA, ROW_TILE), lambda i, t: (rows // EXTRA, i)),
                pl.BlockSpec((EXTRA, LANES), whole),
                pl.BlockSpec((2, EXTRA, 1), lambda i, t: (0, 0, 0)),
                pl.BlockSpec(
                    (replicas, parts, width), lambda i, t: (0, 0, 0), pipeline_mode=pl.Buffered(1)
                ),
            ]
            + [pl.BlockSpec(memory_space=pl.ANY)] * len(kept),
            out_specs=[
                pl.BlockSpec((ROW_TILE, hidden), at),
                pl.BlockSpec((ROW_TILE, hidden), at),
                pl.BlockSpec((ROW_TILE, width), at),
                pl.BlockSpec((ROW_TILE, width), at),
                pl.BlockSpec((ROW_TILE, width), lambda i, t: (t[0] * tiles + i, 0)),
                pl.BlockSpec((rows + EXTRA, width), whole),
            ],
        ),
        out_shape=[
            pltpu.HBM((every, hidden), BF16),
            pltpu.HBM((every, hidden), BF16),
            pltpu.HBM((every, width), BF16),
            pltpu.HBM((every, width), BF16),
            pltpu.HBM((every, width), BF16),
            jax.ShapeDtypeStruct((rows + EXTRA, width), BF16),
        ],
        input_output_aliases={7 + i: i for i in range(len(kept))},
        compiler_params=pltpu.CompilerParams(vmem_limit_bytes=EXPERT_VMEM),
        cost_estimate=pl.CostEstimate(
            flops=rows * width * hidden * 8,
            bytes_accessed=rows * (2 * hidden + 6 * width) * 2 + 4 * width * hidden,
            transcendentals=rows * hidden,
        ),
        name="expert_block",
    )(
        target.reshape(1),
        payload,
        grads_block,
        payload,
        gate_mark,
        dot_mark,
        weights,
        *kept,
    )


def split_float(values, terms):
    parts = []
    for _ in range(terms):
        part = lax.reduce_precision(values, 8, 7)
        parts.append(part.astype(BF16))
        values = values - part
    return parts


def experts_by_ring(hidden_two, gates, weights, next_grads, grads_mine):
    chips = lax.axis_size("expert") // 2
    expert_count, rows = gates.shape
    width = hidden_two.shape[1]
    chip, core = lax.axis_index("expert") // 2, lax.axis_index("expert") % 2
    number = jnp.arange(EXTRA, dtype=jnp.int32)[:, None]
    gate_mark = jnp.broadcast_to(
        (number % expert_count == chip) & (number < 3 * expert_count), (EXTRA, LANES)
    ).astype(BF16)
    slot = 2 * (core * expert_count + chip)
    dot_mark = jnp.stack([number == slot, number == slot + 1]).astype(F32)
    marks = (gate_mark, dot_mark)
    carried = jnp.pad(
        jnp.concatenate(split_float(gates, 3), axis=0),
        ((0, EXTRA - 3 * expert_count), (0, width - rows)),
    )
    kept = None
    carry = None
    backs = []
    mine = jnp.concatenate([hidden_two, carried], axis=0)
    for step in range(chips):
        other = pair(mine)
        if step + 1 < chips:
            following = ring(mine)
        source = (chip - step) % chips
        found_mine = expert_block(
            2 * step,
            2 * chips,
            2 * source + core,
            mine,
            grads_mine[step],
            marks,
            weights,
            kept,
        )
        found_other = expert_block(
            2 * step + 1,
            2 * chips,
            2 * source + 1 - core,
            other,
            pair(grads_mine[step]),
            marks,
            weights,
            found_mine[:5],
        )
        kept = found_other[:5]
        next_grads(found_other[5])
        backs.append((found_mine[5], found_other[5]))
        if step:
            terms = [backs[step][0], pair(backs[step][1])] + ([] if step == 1 else [carry])
            total = added(*terms).astype(BF16)
            carry = ring(total)
        if step + 1 < chips:
            mine = tie(following, found_other[5])
    act_all, pre_all, part_all, rows_all, outs = kept
    rows_all, act_all = tie(rows_all, total), tie(act_all, total)
    grad_widen = dot_tn(rows_all, pre_all).astype(BF16)
    grad_narrow = dot_tn(act_all, part_all).astype(BF16)
    grad_all = added(backs[0][0], pair(backs[0][1]), tie(carry, grad_widen, grad_narrow))
    outs = tie(outs, grad_all)
    grad_hidden = grad_all[:rows]
    table = grad_all[rows : rows + 4 * expert_count, :rows]
    table = jnp.sum(table.reshape(2, expert_count, 2, rows), axis=(0, 2))
    return outs, table, grad_hidden, grad_widen, grad_narrow


def slot_layout(routes, expert_count):
    flat = routes.reshape(-1)
    table = (flat[:, None] == jnp.arange(expert_count, dtype=jnp.int32)[None, :]).astype(jnp.int32)
    before = jnp.cumsum(table, axis=0) - table
    return (flat, jnp.sum(before * table, axis=1))


def to_experts(buffer):
    doubled = jnp.repeat(buffer, 2, axis=0)
    return lax.all_to_all(doubled, "expert", split_axis=0, concat_axis=0, tiled=True)


def both_halves(received, expert_ids, slot_ids):
    slices, capacity, width = received.shape
    summed = jnp.sum(received.astype(F32).reshape(slices // 2, 2, capacity, width), axis=1)
    return summed[expert_ids, slot_ids]


def experts_by_slots(hidden_two, cotangent, routes, gates_table, widen_low, narrow_low, capacity):
    expert_count = gates_table.shape[0]
    device_count = lax.axis_size("expert")
    rows_dev, width = hidden_two.shape
    chooser = (
        routes[:, :, None] == jnp.arange(expert_count, dtype=jnp.int32)[None, None, :]
    ).astype(F32)
    gates = jnp.sum(chooser * gates_table.T[:, None, :], axis=-1)
    expert_ids, slot_ids = slot_layout(routes, expert_count)
    dispatch = (
        jnp.zeros((expert_count, capacity, width), BF16)
        .at[expert_ids, slot_ids]
        .set(jnp.repeat(hidden_two, 2, axis=0))
    )
    expert_rows = to_experts(dispatch).reshape(device_count * capacity, width)
    before_act = dot_nn(expert_rows, widen_low)
    act_low = exact_gelu(before_act).astype(BF16)
    parts_low = dot_nn(act_low, narrow_low).astype(BF16).reshape(device_count, capacity, width)
    returned = lax.all_to_all(parts_low, "expert", split_axis=0, concat_axis=0, tiled=True)
    combined = both_halves(returned, expert_ids, slot_ids).reshape(rows_dev, 2, width)
    out = jnp.sum(gates[:, :, None] * combined, axis=1)
    grad_output = cotangent.astype(F32)
    grad_parts = (
        (gates[:, :, None] * grad_output[:, None, :]).astype(BF16).reshape(2 * rows_dev, width)
    )
    grad_dispatch = (
        jnp.zeros((expert_count, capacity, width), BF16).at[expert_ids, slot_ids].set(grad_parts)
    )
    grad_rows = to_experts(grad_dispatch).reshape(device_count * capacity, width)
    grad_act = dot_nt(grad_rows, narrow_low)
    grad_before = jax.vjp(exact_gelu, before_act)[1](grad_act)[0].astype(BF16)
    grad_narrow = dot_tn(act_low, grad_rows).astype(BF16)
    grad_widen = dot_tn(expert_rows, grad_before).astype(BF16)
    grad_back = dot_nt(grad_before, widen_low).reshape(device_count, capacity, width)
    grad_returned = lax.all_to_all(
        grad_back.astype(BF16), "expert", split_axis=0, concat_axis=0, tiled=True
    )
    grad_hidden = jnp.sum(
        both_halves(grad_returned, expert_ids, slot_ids).reshape(rows_dev, 2, width), axis=1
    )
    grad_gates = jnp.sum(grad_output[:, None, :] * combined, axis=-1)
    table = jnp.sum(grad_gates[:, :, None] * chooser, axis=1).T
    return out, table, grad_hidden, grad_widen, grad_narrow


def local(
    tokens,
    cotangent,
    routes,
    attention_weight,
    attention_first,
    attention_second,
    router_weight,
    router_first,
    router_second,
    norm_vectors,
    norm_first,
    norm_second,
    widen_weight,
    widen_first,
    widen_second,
    narrow_weight,
    narrow_first,
    narrow_second,
):
    device_count = lax.axis_size("expert")
    replicas = lax.axis_size("dp")
    expert_count = device_count // 2
    rows_dev, width = tokens.shape
    capacity = min(rows_dev, 4 * rows_dev // expert_count)
    by_ring = capacity == rows_dev and replicas == 4
    device = lax.axis_index("expert")

    attention_cast = attention_weight.astype(BF16)
    small_own = jnp.concatenate(
        [router_weight.astype(BF16).T, norm_vectors.astype(BF16)], axis=0
    )
    triple_weight = lax.all_gather(attention_cast[:, : 3 * width], "expert", axis=0, tiled=True)
    small_low = gather_expert(small_own, by_ring).transpose(1, 0, 2).reshape(-1, width)
    proj_weight = lax.all_gather(attention_cast[:, 3 * width :], "expert", axis=0, tiled=True)
    router_low = small_low[:expert_count]
    norm_float = small_low[expert_count:].astype(F32)

    widen_cast, narrow_cast = widen_weight[0].astype(BF16), narrow_weight[0].astype(BF16)
    if by_ring:
        half = widen_cast.shape[1] // 2
        halves = jnp.concatenate(
            [widen_cast[:, :half], widen_cast[:, half:], narrow_cast], axis=0
        )
        experts_near, experts_far = gather_dp_near(halves)
    else:
        widen_low = lax.all_gather(widen_cast, "dp", axis=0, tiled=True)
        narrow_low = lax.all_gather(narrow_cast, "dp", axis=0, tiled=True)

    grads_mine = [cotangent]

    def next_grads(dependency):
        if by_ring and len(grads_mine) < expert_count:
            grads_mine.append(ring(tie(grads_mine[-1], dependency)))

    if by_ring and expert_count > 1:
        grads_mine.append(ring(cotangent))
    next_grads(triple_weight)

    below = lax.ppermute(
        tokens[rows_dev - HALO :], "expert", [(i, i + 1) for i in range(device_count - 1)]
    )
    above = lax.ppermute(
        tokens[:HALO], "expert", [(i + 1, i) for i in range(device_count - 1)]
    )
    hidden_one = first_norm(below, tokens, above, norm_float[:2])
    triple = dot_nn(hidden_one, triple_weight).astype(BF16)
    first_row = device * rows_dev
    query_rows = first_row + jnp.arange(rows_dev, dtype=jnp.int32)
    key_rows = first_row - HALO + jnp.arange(rows_dev + 2 * HALO, dtype=jnp.int32)
    query_image = query_rows // SEQ
    inside = (key_rows >= 0) & (key_rows < rows_dev * device_count)
    key_image = jnp.where(inside, key_rows // SEQ, -1)
    heads_low = attention(triple, query_image, key_image)
    next_grads(heads_low)
    if by_ring:
        expert_weights = gather_dp_far(experts_near, experts_far)
    tokens_float = tokens.astype(F32)
    resid = tokens_float + dot_nn(heads_low, proj_weight)
    unit_two, inverse_two = standardised(resid)
    hidden_two = (unit_two * norm_float[2] + norm_float[3]).astype(BF16)

    logits = lax.dot_general(
        router_low, hidden_two, (((1,), (1,)), ((), ())), preferred_element_type=F32
    )
    experts = jnp.arange(expert_count, dtype=jnp.int32)[:, None]
    named = (routes[:, 0][None, :] == experts) | (routes[:, 1][None, :] == experts)
    peak = jnp.max(jnp.where(named, logits, -jnp.inf), axis=0, keepdims=True)
    raised = jnp.where(named, jnp.exp(jnp.where(named, logits - peak, 0.0)), 0.0)
    gates = raised / jnp.sum(raised, axis=0, keepdims=True)

    if by_ring:
        out, grad_gates, grad_hidden, grad_widen, grad_narrow = experts_by_ring(
            hidden_two, gates, expert_weights, next_grads, grads_mine
        )
    else:
        out, grad_gates, grad_hidden, grad_widen, grad_narrow = experts_by_slots(
            hidden_two, cotangent, routes, gates, widen_low, narrow_low, capacity
        )
    if by_ring:
        scattered = [
            scatter_dp_start(grad.reshape(replicas, grad.shape[0] // replicas, grad.shape[1]))
            for grad in (grad_widen, grad_narrow)
        ]

    grad_logits = gates * (grad_gates - jnp.sum(gates * grad_gates, axis=0, keepdims=True))
    grad_router = lax.dot_general(
        grad_logits,
        hidden_two.astype(F32),
        (((1,), (0,)), ((), ())),
        precision=HIGHEST,
        preferred_element_type=F32,
    )
    grad_hidden = grad_hidden + lax.dot_general(
        grad_logits,
        router_low.astype(F32),
        (((0,), (0,)), ((), ())),
        precision=HIGHEST,
        preferred_element_type=F32,
    )
    grad_gain_two = jnp.sum(grad_hidden * unit_two, axis=0)
    grad_shift_two = jnp.sum(grad_hidden, axis=0)
    grad_resid = cotangent.astype(F32) + norm_pull(
        grad_hidden, unit_two, inverse_two, norm_float[2]
    )
    grad_branch = grad_resid.astype(BF16)
    grad_heads = dot_nt(grad_branch, proj_weight).astype(BF16)
    grad_proj = dot_tn(heads_low, grad_branch).astype(BF16)

    grad_triple = attention_back(triple, grad_heads, query_image, key_image)
    by_owner = (2, replicas, expert_count, width // (device_count * replicas))
    small_rows = jnp.concatenate(
        [
            jnp.zeros((2, width), F32),
            jnp.stack([grad_gain_two, grad_shift_two]),
            grad_router,
        ],
        axis=0,
    )
    if by_ring:
        grad_dense, grad_hidden_one = dense_back(
            hidden_one,
            below,
            tokens,
            above,
            grad_triple,
            triple_weight,
            small_rows,
            by_owner,
        )
        dense_sum, (over_pair, over_dp, owned) = sum_to_owner(grad_dense)
        cut = grad_proj.reshape(expert_count, 2, replicas, -1, width).transpose(1, 2, 0, 3, 4)
        proj_sum, _ = sum_to_owner(cut, (grad_heads, grad_triple, over_pair, owned))
        scattered = [scatter_dp_middle(state, over_pair) for state in scattered]
        widen_sum, narrow_sum = [scatter_dp_end(state, over_dp) for state in scattered]
        attention_sum = jnp.concatenate([dense_sum[:, : 3 * width], proj_sum], axis=1)
        small_sum = dense_sum[:, 3 * width :]
    else:
        grad_hidden_one = dot_nt(grad_triple, triple_weight)
        extended = jnp.concatenate([below, tokens, above], axis=0).astype(F32)
        unit_one, _ = standardised(extended)
        small_rows = small_rows.at[0].set(jnp.sum(grad_hidden_one * unit_one, axis=0))
        small_rows = small_rows.at[1].set(jnp.sum(grad_hidden_one, axis=0))
        grad_hidden_one = grad_hidden_one.astype(BF16)
        grad_dense = jnp.concatenate(
            [dot_tn(hidden_one, grad_triple).astype(BF16), grad_proj, small_rows.T.astype(BF16)],
            axis=1,
        )
        widen_sum = lax.psum_scatter(
            grad_widen, "dp", scatter_dimension=0, tiled=True
        ).astype(F32)
        narrow_sum = lax.psum_scatter(
            grad_narrow, "dp", scatter_dimension=0, tiled=True
        ).astype(F32)
        dense_sum = lax.psum(
            lax.psum_scatter(grad_dense, "expert", scatter_dimension=0, tiled=True), "dp"
        ).astype(F32)
        attention_sum = dense_sum[:, : 4 * width]
        small_sum = dense_sum[:, 4 * width :]
    from_above = lax.ppermute(
        grad_hidden_one[:HALO], "expert", [(i + 1, i) for i in range(device_count - 1)]
    )
    from_below = lax.ppermute(
        grad_hidden_one[rows_dev + HALO :],
        "expert",
        [(i, i + 1) for i in range(device_count - 1)],
    )
    if by_ring:
        from_above = tie(from_above, over_dp)
    grad_own = added(
        grad_hidden_one[HALO : HALO + rows_dev],
        jnp.concatenate([from_below, from_above], axis=0),
    )
    unit_one, inverse_one = standardised(tokens_float)
    tokens_grad = grad_resid + norm_pull(grad_own, unit_one, inverse_one, norm_float[0])

    if by_ring:
        out = lax.psum_scatter(out, "expert", scatter_dimension=0, tiled=True)
        out = tie(out, owned).astype(F32)
    mixed = (resid + out).astype(BF16)
    attention_new = adam_step(
        attention_weight, attention_first, attention_second, attention_sum, MATRIX_RATE, DECAY
    )
    if by_ring:
        small_new = small_adam(
            small_sum,
            norm_vectors,
            norm_first,
            norm_second,
            router_weight,
            router_first,
            router_second,
        )
        norm_new, router_new = tuple(small_new[:3]), tuple(small_new[3:])
    else:
        norm_new = adam_step(
            norm_vectors, norm_first, norm_second, small_sum[:, :4].T, VECTOR_RATE, 0.0
        )
        router_new = adam_step(
            router_weight, router_first, router_second, small_sum[:, 4:], MATRIX_RATE, DECAY
        )
    widen_new = adam_step(
        widen_weight, widen_first, widen_second, widen_sum[None], MATRIX_RATE, DECAY
    )
    narrow_new = adam_step(
        narrow_weight, narrow_first, narrow_second, narrow_sum[None], MATRIX_RATE, DECAY
    )
    return (mixed, tokens_grad) + attention_new + router_new + norm_new + widen_new + narrow_new


def solution(mesh):
    rows = P(("dp", "expert"), None)
    dense = P("expert", None)
    vectors = P(None, "expert")
    halves = P("expert", "dp", None)
    return jax.shard_map(
        local,
        mesh=mesh,
        in_specs=(rows,) * 3 + (dense,) * 6 + (vectors,) * 3 + (halves,) * 6,
        out_specs=(rows,) * 2 + (dense,) * 6 + (vectors,) * 3 + (halves,) * 6,
        check_vma=False,
    )
```

time: 1180 us -> 511 us (0.43)
  waiting for transfers between devices: 526 us -> 103 us
  matrix products: 235 us -> 45.9 us
  Pallas kernels: 0 us -> 141 us
  blocking collectives: 130 us -> 0 us
  other arithmetic: 109 us -> 55.1 us
  local copies, waits for them, and re-layouts: 103 us -> 65.5 us
  starting transfers between devices: 50.9 us -> 76.4 us
    all_to_all x4 -> x0, waiting for transfers between devices: 270 us -> none  [the longest x1 94.4 us: local(): lax.all_to_all(parts_low, 'expert', split_axis=0, concat_axis=0, tiled=True)]
    dot_general x20 -> x9, matrix products: 233 us -> 45.9 us  [the longest x3 29.8 us: dot_tn(): lax.dot_general(left, right, (((0,), (0,)), ((), ())), preferred_element_...]
    pallas_call x0 -> x40, Pallas kernels: none -> 141 us  [the longest x8 65.5 us: expert_block(): pl.pallas_call(functools.partial(expert_kernel, first), grid_spec=pltpu.P...]
    all_gather x2 -> x0, blocking collectives: 121 us -> none  [the longest x1 107 us: local(): lax.all_gather(router_weight.astype(jnp.bfloat16), 'expert', axis=0, tile...]
    reduce_scatter x3 -> x1, waiting for transfers between devices: 120 us -> 0.01 us  [local(): out = lax.psum_scatter(out, 'expert', scatter_dimension=0, tiled=True)]
    ppermute x4 -> x60, waiting for transfers between devices: 0.01 us -> 85.2 us  [the longest x18 50.4 us: hop(): lax.ppermute(block, 'expert', [(i, (i + distance) % count) for i in range...]
    ppermute x4 -> x60, starting transfers between devices: 10.1 us -> 76.3 us  [the longest x18 35.7 us: hop(): lax.ppermute(block, 'expert', [(i, (i + distance) % count) for i in range...]
    all_gather x3 -> x2, waiting for transfers between devices: 74.7 us -> 17.3 us  [the longest x1 17.3 us: local(): lax.all_gather(attention_cast[:, :3 * width], 'expert', axis=0, tiled=True)]
  transfers between devices with their start and end apart: 17 -> 63, of which waited for: 10 -> 19; matrix products, arithmetic and copies ran while one was open for 30% -> 25% of each run, Pallas kernels for 0% -> 28%
where the time goes in v1:
time: 511 us; the launch traced here: 501 us
  Pallas kernels  141 us (28%)
  waiting for transfers between devices  103 us (20%)
  starting transfers between devices  76.4 us (15%)
  local copies, waits for them, and re-layouts  65.5 us (13%)
  other arithmetic  55.1 us (11%)
  matrix products  45.9 us (9%)
  between operations  15.1 us (3%)
    pallas_call x8, Pallas kernels, expert_block(): pl.pallas_call(functools.partial(expert_kernel, first), grid_spec=pltpu.P...  65.5 us
    ppermute x18, waiting for transfers between devices, hop(): lax.ppermute(block, 'expert', [(i, (i + distance) % count) for i in range...  50.4 us
    unnamed x217, local copies, waits for them, and re-layouts  45.7 us
    ppermute x18, starting transfers between devices, hop(): lax.ppermute(block, 'expert', [(i, (i + distance) % count) for i in range...  35.7 us
    ppermute x23, waiting for transfers between devices, across(): lax.ppermute(block, 'dp', [(i, i ^ bit) for i in range(lax.axis_size('dp'...  34.7 us
    ppermute x23, starting transfers between devices, across(): lax.ppermute(block, 'dp', [(i, i ^ bit) for i in range(lax.axis_size('dp'...  30.9 us
    pallas_call x1, Pallas kernels, attention_back(): pl.pallas_call(attend_back_kernel, grid=(blocks,), in_specs=[pl.BlockSpec...  30.6 us
    dot_general x3, matrix products, dot_tn(): lax.dot_general(left, right, (((0,), (0,)), ((), ())), preferred_element_...  29.8 us
  transfers between devices with their start and end apart: 63, of which 19 were waited for; matrix products, arithmetic and copies ran while one was open for 25% of the time, Pallas kernels for 28%

profile of v1, /device:TPU:0, one launch (start us, length us, event | category | flops | bytes accessed | tf_op | source)
XLA Modules:
  0.0 501.1 jit_solution(6257402841700121317)
XLA Ops:
  18.3 3.7 collective-permute-start.3
  30.9 13.2 %collective-permute-start.14 = (bf16[512,768]{1,0:T(8,128)(2,1)}, bf16[512,768]{1,0:T(8,128)(2,1)S(1)}, u32[]{:S(2)}, u32[]{:S(2)}) collective-permute-start(bf16[512,768]{1,0:T(8,128)(2,1)} %grads_ref.1), channel_id=1, source_target_pairs={{0,2},{1,3},{2,4},{3,5},{4,6},{5,7},{6,0},{7,1},{8,10},{9,11},{10,... | collective-permute-start | bytes 2359304 | tf_op jit(solution)/shard_map/ppermute | solution.py:55
  44.8 3.6 first_norm.1.hidden
  48.4 17.3 %all-gather.3.cloned.1.call-done.refs_1_.weight = bf16[768,2304]{1,0:T(8,128)(2,1)} async-done(((bf16[96,2304]{1,0:T(8,128)(2,1)}), bf16[768,2304]{1,0:T(8,128)(2,1)}) %all-gather.3.cloned.1.call-update) | async-done | bytes 3538960 | tf_op jit(solution)/shard_map/all_gather | solution.py:775
  65.7 8.4 %convolution_convert_fusion.q_ref.k_ref.v_ref = bf16[1024,2304]{1,0:T(8,128)(2,1)} fusion(bf16[1024,768]{1,0:T(8,128)(2,1)} %first_norm.1.hidden, bf16[768,2304]{1,0:T(8,128)(2,1)} %all-gather.3.cloned.1.call-done.refs_1_.weight), kind=kOutput, calls=%fused_computation | convolution fusion | flops 3626237952 | bytes 9830400 | tf_op jit(solution)/shard_map/dot_general | solution.py:232
  74.2 16.2 %attention.1.refs_1_ = bf16[512,768]{1,0:T(8,128)(2,1)} custom-call(s32[512,1]{1,0:T(8,128)} %add_select_fusion.1.query_image, s32[1,1024]{1,0:T(1,128)} %and_select_fusion.1.key_image, bf16[1024,2304]{1,0:T(8,128)(2,1)} %convolution_convert_fusion.q_ref.k_ref.v_ref, bf16[1024,2304]{1,0:T(8,128)(2,1)} %convolution_convert_fusion.q_ref.k_ref.v_ref, ...), custom_call_target="tpu_custom_call" | custom-call | flops 2415919104 | bytes 4718592 | tf_op jit(solution)/shard_map/attention/pallas_call | solution.py:267
  108.5 8.5 %expert_block.8 = (bf16[4096,1536]{1,0:T(8,128)(2,1)}, bf16[4096,1536]{1,0:T(8,128)(2,1)}, bf16[4096,768]{1,0:T(8,128)(2,1)}, bf16[4096,768]{1,0:T(8,128)(2,1)},...) custom-call(s32[1]{0:T(128)} %bitcast.16.target, bf16[528,768]{1,0:T(8,128)(2,1)S(1)} %pad_maximum_fusion.4.rows_ref.gates, ...), custom_call_target="tpu_custom_call" | custom-call | flops 4831838208 | bytes 12582912 | tf_op jit(solution)/shard_map/expert_block/pallas_call | solution.py:552
  117.9 8.5 %expert_block.9 = (bf16[4096,1536]{1,0:T(8,128)(2,1)}, bf16[4096,1536]{1,0:T(8,128)(2,1)}, bf16[4096,768]{1,0:T(8,128)(2,1)}, bf16[4096,768]{1,0:T(8,128)(2,1)},...) custom-call(s32[1]{0:T(128)} %bitcast.7.target, ...), custom_call_target="tpu_custom_call", output_to_operand_aliasing={{0}: (7, {}), {1}: (8, {}), {2}: (9, {}), {3}: (10, {}), {4... | custom-call | flops 4831838208 | bytes 12582912 | tf_op jit(solution)/shard_map/expert_block/pallas_call | solution.py:552
  131.7 7.5 %expert_block.10 = (bf16[4096,1536]{1,0:T(8,128)(2,1)}, bf16[4096,1536]{1,0:T(8,128)(2,1)}, bf16[4096,768]{1,0:T(8,128)(2,1)}, bf16[4096,768]{1,0:T(8,128)(2,1)}...) custom-call(s32[1]{0:T(128)} %bitcast.18.target, ...), custom_call_target="tpu_custom_call", output_to_operand_aliasing={{0}: (7, {}), {1}: (8, {}), {2}: (9, {}), {3}: (10, {}), {4... | custom-call | flops 4831838208 | bytes 12582912 | tf_op jit(solution)/shard_map/expert_block/pallas_call | solution.py:552
  145.7 8.8 %expert_block.11 = (bf16[4096,1536]{1,0:T(8,128)(2,1)}, bf16[4096,1536]{1,0:T(8,128)(2,1)}, bf16[4096,768]{1,0:T(8,128)(2,1)}, bf16[4096,768]{1,0:T(8,128)(2,1)}...) custom-call(s32[1]{0:T(128)} %bitcast.17.target, ...), custom_call_target="tpu_custom_call", output_to_operand_aliasing={{0}: (7, {}), {1}: (8, {}), {2}: (9, {}), {3}: (10, {}), {4... | custom-call | flops 4831838208 | bytes 12582912 | tf_op jit(solution)/shard_map/expert_block/pallas_call | solution.py:552
  154.7 7.7 %collective-permute-done.18.grads_ref.refs_0_ = bf16[512,768]{1,0:T(8,128)(2,1)S(1)} collective-permute-done((bf16[512,768]{1,0:T(8,128)(2,1)}, bf16[512,768]{1,0:T(8,128)(2,1)S(1)}, u32[]{:S(2)}, u32[]{:S(2)}) %collective-permute-start.18) | collective-permute-done | bytes 786464 | tf_op jit(solution)/shard_map/ppermute | solution.py:55
  162.5 17.0 %collective-permute-done.12.refs_0_ = bf16[528,768]{1,0:T(8,128)(2,1)S(1)} collective-permute-done((bf16[528,768]{1,0:T(8,128)(2,1)S(1)}, bf16[528,768]{1,0:T(8,128)(2,1)S(1)}, u32[]{:S(2)}, u32[]{:S(2)}) %collective-permute-start.12) | collective-permute-done | bytes 811040 | tf_op jit(solution)/shard_map/ppermute | solution.py:55
  183.8 7.5 %expert_block.12 = (bf16[4096,1536]{1,0:T(8,128)(2,1)}, bf16[4096,1536]{1,0:T(8,128)(2,1)}, bf16[4096,768]{1,0:T(8,128)(2,1)}, bf16[4096,768]{1,0:T(8,128)(2,1)}...) custom-call(s32[1]{0:T(128)} %bitcast.20.target, ...), custom_call_target="tpu_custom_call", output_to_operand_aliasing={{0}: (7, {}), {1}: (8, {}), {2}: (9, {}), {3}: (10, {}), {4... | custom-call | flops 4831838208 | bytes 12582912 | tf_op jit(solution)/shard_map/expert_block/pallas_call | solution.py:552
  200.0 8.5 %expert_block.13 = (bf16[4096,1536]{1,0:T(8,128)(2,1)}, bf16[4096,1536]{1,0:T(8,128)(2,1)}, bf16[4096,768]{1,0:T(8,128)(2,1)}, bf16[4096,768]{1,0:T(8,128)(2,1)}...) custom-call(s32[1]{0:T(128)} %bitcast.19.target, ...), custom_call_target="tpu_custom_call", output_to_operand_aliasing={{0}: (7, {}), {1}: (8, {}), {2}: (9, {}), {3}: (10, {}), {4... | custom-call | flops 4831838208 | bytes 12582912 | tf_op jit(solution)/shard_map/expert_block/pallas_call | solution.py:552
  210.3 9.7 %collective-permute-done.21.grads_ref = bf16[512,768]{1,0:T(8,128)(2,1)S(1)} collective-permute-done((bf16[512,768]{1,0:T(8,128)(2,1)}, bf16[512,768]{1,0:T(8,128)(2,1)S(1)}, u32[]{:S(2)}, u32[]{:S(2)}) %collective-permute-start.21) | collective-permute-done | bytes 786464 | tf_op jit(solution)/shard_map/ppermute | solution.py:55
  224.8 7.5 %expert_block.14 = (bf16[4096,1536]{1,0:T(8,128)(2,1)}, bf16[4096,1536]{1,0:T(8,128)(2,1)}, bf16[4096,768]{1,0:T(8,128)(2,1)}, bf16[4096,768]{1,0:T(8,128)(2,1)}...) custom-call(s32[1]{0:T(128)} %bitcast.21.target, ...), custom_call_target="tpu_custom_call", output_to_operand_aliasing={{0}: (7, {}), {1}: (8, {}), {2}: (9, {}), {3}: (10, {}), {4... | custom-call | flops 4831838208 | bytes 12582912 | tf_op jit(solution)/shard_map/expert_block/pallas_call | solution.py:552
  232.4 4.8 collective-permute-done.27
  239.8 8.6 %expert_block.15 = (bf16[4096,1536]{1,0:T(8,128)(2,1)}, bf16[4096,1536]{1,0:T(8,128)(2,1)}, bf16[4096,768]{1,0:T(8,128)(2,1)}, bf16[4096,768]{1,0:T(8,128)(2,1)}...) custom-call(s32[1]{0:T(128)} %bitcast.4.target, ...), custom_call_target="tpu_custom_call", output_to_operand_aliasing={{0}: (7, {}), {1}: (8, {}), {2}: (9, {}), {3}: (10, {}), {4... | custom-call | flops 4831838208 | bytes 12582912 | tf_op jit(solution)/shard_map/expert_block/pallas_call | solution.py:552
  252.9 8.6 %collective-permute-done.28 = bf16[528,768]{1,0:T(8,128)(2,1)} collective-permute-done((bf16[528,768]{1,0:T(8,128)(2,1)}, bf16[528,768]{1,0:T(8,128)(2,1)}, u32[]{:S(2)}, u32[]{:S(2)}) %collective-permute-start.28) | collective-permute-done | bytes 811040 | tf_op jit(solution)/shard_map/ppermute | solution.py:55
  264.2 15.0 %convolution_convert_fusion.1.refs_2_ = bf16[1536,768]{1,0:T(8,128)(2,1)S(1)} fusion(bf16[4096,1536]{1,0:T(8,128)(2,1)} %tie.29, bf16[4096,768]{1,0:T(8,128)(2,1)} %get-tuple-element.120), kind=kOutput, calls=%fused_computation.3 | convolution fusion | flops 9664856064 | bytes 21233664 | tf_op jit(solution)/shard_map/dot_general | solution.py:228
  283.4 13.9 %convolution_convert_fusion.2.refs_1_ = bf16[768,1536]{1,0:T(8,128)(2,1)S(1)} fusion(bf16[4096,768]{1,0:T(8,128)(2,1)S(1)} %copy-done.24, bf16[4096,1536]{1,0:T(8,128)(2,1)} %get-tuple-element.118), kind=kOutput, calls=%fused_computation.4 | convolution fusion | flops 9664856064 | bytes 21233664 | tf_op jit(solution)/shard_map/dot_general | solution.py:228
  311.1 30.6 %attention_back.1.grads.refs_1_ = bf16[1024,2304]{1,0:T(8,128)(2,1)} custom-call(s32[1,512]{1,0:T(1,128)} %and_select_fusion.2.query_image, s32[1024,1]{1,0:T(8,128)} %fusion.26.key_image, bf16[1024,2304]{1,0:T(8,128)(2,1)} %convolution_convert_fusion.q_ref.k_ref.v_ref, bf16[1024,2304]{1,0:T(8,128)(2,1)} %convolution_convert_fusion.q_ref.k_ref.v_ref, ...), custom_call_target="tpu_custom_call" | custom-call | flops 6039797760 | bytes 11010048 | tf_op jit(solution)/shard_map/attention_back/pallas_call | solution.py:334
  342.4 14.4 %dense_back.1 = (bf16[2,4,4,24,2432]{4,3,2,1,0:T(8,128)(2,1)}, bf16[1024,768]{1,0:T(8,128)(2,1)}) custom-call(bf16[1024,768]{1,0:T(8,128)(2,1)} %first_norm.1.hidden, bf16[256,768]{1,0:T(8,128)(2,1)} %copy-done.81, bf16[512,768]{1,0:T(8,128)(2,1)} %tokens.3, bf16[256,768]{1,0:T(8,128)(2,1)} %copy-done.82, bf16[1024,2304]{1,0:T(8,128)(2,1)} %attention_back.1.grads.refs_1_, ...), custom_call_target="tpu_custom_call" | custom-call | flops 7247757312 | bytes 19660800 | tf_op jit(solution)/shard_map/dense_back/pallas_call | solution.py:430
  356.8 3.0 dynamic-slice_bitcast_fusion
  383.2 3.8 fusion.refs_1_
  386.9 3.8 collective-permute-start.47
  391.0 3.2 collective-permute-start.48
  415.5 5.1 %collective-permute-done.31 = bf16[4,24,2432]{2,1,0:T(8,128)(2,1)} collective-permute-done((bf16[4,24,2432]{2,1,0:T(8,128)(2,1)}, bf16[4,24,2432]{2,1,0:T(8,128)(2,1)}, u32[]{:S(2)}, u32[]{:S(2)}) %collective-permute-start.31) | collective-permute-done | bytes 466976 | tf_op jit(solution)/shard_map/ppermute | solution.py:67
  421.2 8.5 %collective-permute-done.32 = bf16[4,24,2432]{2,1,0:T(8,128)(2,1)S(1)} collective-permute-done((bf16[4,24,2432]{2,1,0:T(8,128)(2,1)}, bf16[4,24,2432]{2,1,0:T(8,128)(2,1)S(1)}, u32[]{:S(2)}, u32[]{:S(2)}) %collective-permute-start.32) | collective-permute-done | bytes 466976 | tf_op jit(solution)/shard_map/ppermute | solution.py:67
  439.1 3.2 collective-permute-done.53.refs_0_
  444.7 6.1 %collective-permute-done.55.refs_0_ = bf16[96,1536]{1,0:T(8,128)(2,1)} collective-permute-done((bf16[96,1536]{1,0:T(8,128)(2,1)}, bf16[96,1536]{1,0:T(8,128)(2,1)}, u32[]{:S(2)}, u32[]{:S(2)}) %collective-permute-start.55) | collective-permute-done | bytes 294944 | tf_op jit(solution)/shard_map/ppermute | solution.py:67
  488.6 3.6 multiply_subtract_fusion.2
  (472 shorter events, 196.1 us)
Async XLA Ops:
  7.2 58.5 %all-gather.3.cloned.1.call-start = ((), (), s32[]{:S(2)}) async-start(), calls=%async_computation.1 | async-start | bytes 3981312 | tf_op jit(solution)/shard_map/all_gather | solution.py:775
  9.5 80.8 %all-gather.5.cloned.1.call-start = ((), (), s32[]{:S(2)}) async-start(), calls=%async_computation.2 | async-start | bytes 1327104 | tf_op jit(solution)/shard_map/all_gather | solution.py:777
  12.0 86.1 %collective-permute-start.11 = (bf16[768,768]{1,0:T(8,128)(2,1)}, bf16[768,768]{1,0:T(8,128)(2,1)}, u32[]{:S(2)}, u32[]{:S(2)}) collective-permute-start(bf16[768,768]{1,0:T(8,128)(2,1)} %pad_maximum_fusion.block), channel_id=1, source_target_pairs={{0,8},{8,0},{16,24},{24,16},{1,9},{9,1},{17,25},{25,17},{2,10},{10... | collective-permute-start | bytes 3538952 | tf_op jit(solution)/shard_map/ppermute | solution.py:67
  14.9 85.6 %collective-permute-start.10 = (bf16[768,768]{1,0:T(8,128)(2,1)}, bf16[768,768]{1,0:T(8,128)(2,1)}, u32[]{:S(2)}, u32[]{:S(2)}) collective-permute-start(bf16[768,768]{1,0:T(8,128)(2,1)} %pad_maximum_fusion.block), channel_id=1, source_target_pairs={{0,16},{8,24},{16,0},{24,8},{1,17},{9,25},{17,1},{25,9},{2,18},{10... | collective-permute-start | bytes 3538952 | tf_op jit(solution)/shard_map/ppermute | solution.py:67
  17.2 475.0 %reduce-scatter.2.cloned.1.call-start = ((), (), s32[]{:S(2)}) async-start(), calls=%async_computation.3 | async-start | bytes 7077888 | tf_op jit(solution)/shard_map/reduce_scatter | solution.py:940
  23.6 79.0 %collective-permute-start.9 = (bf16[768,768]{1,0:T(8,128)(2,1)}, bf16[768,768]{1,0:T(8,128)(2,1)}, u32[]{:S(2)}, u32[]{:S(2)}) collective-permute-start(bf16[768,768]{1,0:T(8,128)(2,1)} %pad_maximum_fusion.block), channel_id=1, source_target_pairs={{0,24},{8,16},{16,8},{24,0},{1,25},{9,17},{17,9},{25,1},{2,26},{10... | collective-permute-start | bytes 3538952 | tf_op jit(solution)/shard_map/ppermute | solution.py:67
  30.9 64.5 %collective-permute-start.14 = (bf16[512,768]{1,0:T(8,128)(2,1)}, bf16[512,768]{1,0:T(8,128)(2,1)S(1)}, u32[]{:S(2)}, u32[]{:S(2)}) collective-permute-start(bf16[512,768]{1,0:T(8,128)(2,1)} %grads_ref.1), channel_id=1, source_target_pairs={{0,2},{1,3},{2,4},{3,5},{4,6},{5,7},{6,0},{7,1},{8,10},{9,11},{10,... | collective-permute-start | bytes 2359304 | tf_op jit(solution)/shard_map/ppermute | solution.py:55
  95.0 22.9 %collective-permute-start.7 = (bf16[528,768]{1,0:T(8,128)(2,1)S(1)}, bf16[528,768]{1,0:T(8,128)(2,1)S(1)}, u32[]{:S(2)}, u32[]{:S(2)}) collective-permute-start(bf16[528,768]{1,0:T(8,128)(2,1)S(1)} %pad_maximum_fusion.4.rows_ref.gates), channel_id=1, source_target_pairs={{0,1},{1,0},{2,3},{3,2},{4,5},{5,4},{6,7},{7,6},{8,9},{9,8},{10,11... | collective-permute-start | bytes 2433032 | tf_op jit(solution)/shard_map/ppermute | solution.py:63
  95.4 22.5 %collective-permute-start.8 = (bf16[512,768]{1,0:T(8,128)(2,1)}, bf16[512,768]{1,0:T(8,128)(2,1)}, u32[]{:S(2)}, u32[]{:S(2)}) collective-permute-start(bf16[512,768]{1,0:T(8,128)(2,1)} %grads_ref.1), channel_id=1, source_target_pairs={{0,1},{1,0},{2,3},{3,2},{4,5},{5,4},{6,7},{7,6},{8,9},{9,8},{10,11... | collective-permute-start | bytes 2359304 | tf_op jit(solution)/shard_map/ppermute | solution.py:63
  98.1 42.0 %collective-permute-start.15 = (bf16[512,768]{1,0:T(8,128)(2,1)S(1)}, bf16[512,768]{1,0:T(8,128)(2,1)}, u32[]{:S(2)}, u32[]{:S(2)}) collective-permute-start(bf16[512,768]{1,0:T(8,128)(2,1)S(1)} %collective-permute-done.14.grads_ref.refs_0_), channel_id=1, source_target_pairs={{0,1},{1,0},{2,3},{3,2},{4,5},{5,4},{6,7},{7,6},{8,9},{9,8},{10,11... | collective-permute-start | bytes 2359304 | tf_op jit(solution)/shard_map/ppermute | solution.py:63
  104.8 22.5 %collective-permute-start.6 = (bf16[528,768]{1,0:T(8,128)(2,1)S(1)}, bf16[528,768]{1,0:T(8,128)(2,1)S(1)}, u32[]{:S(2)}, u32[]{:S(2)}) collective-permute-start(bf16[528,768]{1,0:T(8,128)(2,1)S(1)} %pad_maximum_fusion.4.rows_ref.gates), channel_id=1, source_target_pairs={{0,2},{1,3},{2,4},{3,5},{4,6},{5,7},{6,0},{7,1},{8,10},{9,11},{10,... | collective-permute-start | bytes 2433032 | tf_op jit(solution)/shard_map/ppermute | solution.py:55
  140.1 22.3 %collective-permute-start.18 = (bf16[512,768]{1,0:T(8,128)(2,1)}, bf16[512,768]{1,0:T(8,128)(2,1)S(1)}, u32[]{:S(2)}, u32[]{:S(2)}) collective-permute-start(bf16[512,768]{1,0:T(8,128)(2,1)} %tie.25), channel_id=1, source_target_pairs={{0,2},{1,3},{2,4},{3,5},{4,6},{5,7},{6,0},{7,1},{8,10},{9,11},{10,... | collective-permute-start | bytes 2359304 | tf_op jit(solution)/shard_map/ppermute | solution.py:55
  141.7 37.7 %collective-permute-start.12 = (bf16[528,768]{1,0:T(8,128)(2,1)S(1)}, bf16[528,768]{1,0:T(8,128)(2,1)S(1)}, u32[]{:S(2)}, u32[]{:S(2)}) collective-permute-start(bf16[528,768]{1,0:T(8,128)(2,1)S(1)} %copy-done.12), channel_id=1, source_target_pairs={{0,2},{1,3},{2,4},{3,5},{4,6},{5,7},{6,0},{7,1},{8,10},{9,11},{10,... | collective-permute-start | bytes 2433032 | tf_op jit(solution)/shard_map/ppermute | solution.py:55
  154.5 38.9 %collective-permute-start.26 = (bf16[528,768]{1,0:T(8,128)(2,1)}, bf16[528,768]{1,0:T(8,128)(2,1)}, u32[]{:S(2)}, u32[]{:S(2)}) collective-permute-start(bf16[528,768]{1,0:T(8,128)(2,1)} %get-tuple-element.89.refs_1_), channel_id=1, source_target_pairs={{0,1},{1,0},{2,3},{3,2},{4,5},{5,4},{6,7},{7,6},{8,9},{9,8},{10,11... | collective-permute-start | bytes 2433032 | tf_op jit(solution)/shard_map/ppermute | solution.py:63
  162.5 30.7 %collective-permute-start.19 = (bf16[512,768]{1,0:T(8,128)(2,1)S(1)}, bf16[512,768]{1,0:T(8,128)(2,1)}, u32[]{:S(2)}, u32[]{:S(2)}) collective-permute-start(bf16[512,768]{1,0:T(8,128)(2,1)S(1)} %collective-permute-done.18.grads_ref.refs_0_), channel_id=1, source_target_pairs={{0,1},{1,0},{2,3},{3,2},{4,5},{5,4},{6,7},{7,6},{8,9},{9,8},{10,11... | collective-permute-start | bytes 2359304 | tf_op jit(solution)/shard_map/ppermute | solution.py:63
  180.3 28.2 %collective-permute-start.16 = (bf16[528,768]{1,0:T(8,128)(2,1)}, bf16[528,768]{1,0:T(8,128)(2,1)S(1)}, u32[]{:S(2)}, u32[]{:S(2)}) collective-permute-start(bf16[528,768]{1,0:T(8,128)(2,1)} %tie.24.rows_ref.gates), channel_id=1, source_target_pairs={{0,2},{1,3},{2,4},{3,5},{4,6},{5,7},{6,0},{7,1},{8,10},{9,11},{10,... | collective-permute-start | bytes 2433032 | tf_op jit(solution)/shard_map/ppermute | solution.py:55
  193.1 26.9 %collective-permute-start.21 = (bf16[512,768]{1,0:T(8,128)(2,1)}, bf16[512,768]{1,0:T(8,128)(2,1)S(1)}, u32[]{:S(2)}, u32[]{:S(2)}) collective-permute-start(bf16[512,768]{1,0:T(8,128)(2,1)} %tie.27), channel_id=1, source_target_pairs={{0,2},{1,3},{2,4},{3,5},{4,6},{5,7},{6,0},{7,1},{8,10},{9,11},{10,... | collective-permute-start | bytes 2359304 | tf_op jit(solution)/shard_map/ppermute | solution.py:55
  196.5 40.7 %collective-permute-start.27 = (bf16[528,768]{1,0:T(8,128)(2,1)}, bf16[528,768]{1,0:T(8,128)(2,1)}, u32[]{:S(2)}, u32[]{:S(2)}) collective-permute-start(bf16[528,768]{1,0:T(8,128)(2,1)} %add_convert_fusion.2), channel_id=1, source_target_pairs={{0,2},{1,3},{2,4},{3,5},{4,6},{5,7},{6,0},{7,1},{8,10},{9,11},{10,... | collective-permute-start | bytes 2433032 | tf_op jit(solution)/shard_map/ppermute | solution.py:55
  208.5 28.6 %collective-permute-start.25 = (bf16[528,768]{1,0:T(8,128)(2,1)S(1)}, bf16[528,768]{1,0:T(8,128)(2,1)}, u32[]{:S(2)}, u32[]{:S(2)}) collective-permute-start(bf16[528,768]{1,0:T(8,128)(2,1)S(1)} %get-tuple-element.100.refs_1_), channel_id=1, source_target_pairs={{0,1},{1,0},{2,3},{3,2},{4,5},{5,4},{6,7},{7,6},{8,9},{9,8},{10,11... | collective-permute-start | bytes 2433032 | tf_op jit(solution)/shard_map/ppermute | solution.py:63
  210.3 29.4 %collective-permute-start.20 = (bf16[528,768]{1,0:T(8,128)(2,1)}, bf16[528,768]{1,0:T(8,128)(2,1)S(1)}, u32[]{:S(2)}, u32[]{:S(2)}) collective-permute-start(bf16[528,768]{1,0:T(8,128)(2,1)} %tie.26.rows_ref.gates), channel_id=1, source_target_pairs={{0,1},{1,0},{2,3},{3,2},{4,5},{5,4},{6,7},{7,6},{8,9},{9,8},{10,11... | collective-permute-start | bytes 2433032 | tf_op jit(solution)/shard_map/ppermute | solution.py:63
  252.4 48.1 %collective-permute-start.23 = (bf16[528,768]{1,0:T(8,128)(2,1)S(1)}, bf16[528,768]{1,0:T(8,128)(2,1)}, u32[]{:S(2)}, u32[]{:S(2)}) collective-permute-start(bf16[528,768]{1,0:T(8,128)(2,1)S(1)} %copy-done.16), channel_id=1, source_target_pairs={{0,1},{1,0},{2,3},{3,2},{4,5},{5,4},{6,7},{7,6},{8,9},{9,8},{10,11... | collective-permute-start | bytes 2433032 | tf_op jit(solution)/shard_map/ppermute | solution.py:63
  263.3 36.2 %collective-permute-start.29 = (bf16[528,768]{1,0:T(8,128)(2,1)S(1)}, bf16[528,768]{1,0:T(8,128)(2,1)S(1)}, u32[]{:S(2)}, u32[]{:S(2)}) collective-permute-start(bf16[528,768]{1,0:T(8,128)(2,1)S(1)} %add_convert_fusion.refs_1_), channel_id=1, source_target_pairs={{0,2},{1,3},{2,4},{3,5},{4,6},{5,7},{6,0},{7,1},{8,10},{9,11},{10,... | collective-permute-start | bytes 2433032 | tf_op jit(solution)/shard_map/ppermute | solution.py:55
  281.9 105.0 %collective-permute-start.56 = (bf16[2,192,768]{2,1,0:T(8,128)(2,1)}, bf16[2,192,768]{2,1,0:T(8,128)(2,1)}, u32[]{:S(2)}, u32[]{:S(2)}) collective-permute-start(bf16[2,192,768]{2,1,0:T(8,128)(2,1)} %dynamic-slice_bitcast_fusion.2), channel_id=1, source_target_pairs={{0,8},{8,0},{16,24},{24,16},{1,9},{9,1},{17,25},{25,17},{2,10},{10... | collective-permute-start | bytes 1769480 | tf_op jit(solution)/shard_map/ppermute | solution.py:67
  359.8 23.4 %collective-permute-start.30 = (bf16[4,4,24,2432]{3,2,1,0:T(8,128)(2,1)}, bf16[4,4,24,2432]{3,2,1,0:T(8,128)(2,1)}, u32[]{:S(2)}, u32[]{:S(2)}) collective-permute-start(bf16[4,4,24,2432]{3,2,1,0:T(8,128)(2,1)} %dynamic-slice_bitcast_fusion), channel_id=1, source_target_pairs={{0,1},{1,0},{2,3},{3,2},{4,5},{5,4},{6,7},{7,6},{8,9},{9,8},{10,11... | collective-permute-start | bytes 5603336 | tf_op jit(solution)/shard_map/ppermute | solution.py:63
  377.1 22.3 %collective-permute-start.52 = (bf16[2,96,1536]{2,1,0:T(8,128)(2,1)}, bf16[2,96,1536]{2,1,0:T(8,128)(2,1)}, u32[]{:S(2)}, u32[]{:S(2)}) collective-permute-start(bf16[2,96,1536]{2,1,0:T(8,128)(2,1)} %dynamic-slice_bitcast_fusion.4), channel_id=1, source_target_pairs={{0,8},{8,0},{16,24},{24,16},{1,9},{9,1},{17,25},{25,17},{2,10},{10... | collective-permute-start | bytes 1769480 | tf_op jit(solution)/shard_map/ppermute | solution.py:67
  379.6 24.0 %collective-permute-start.54 = (bf16[2,96,1536]{2,1,0:T(8,128)(2,1)}, bf16[2,96,1536]{2,1,0:T(8,128)(2,1)}, u32[]{:S(2)}, u32[]{:S(2)}) collective-permute-start(bf16[2,96,1536]{2,1,0:T(8,128)(2,1)} %dynamic-slice_bitcast_fusion.3), channel_id=1, source_target_pairs={{0,16},{8,24},{16,0},{24,8},{1,17},{9,25},{17,1},{25,9},{2,18},{10... | collective-permute-start | bytes 1769480 | tf_op jit(solution)/shard_map/ppermute | solution.py:67
  383.1 23.4 %collective-permute-start.46 = (bf16[24,768]{1,0:T(8,128)(2,1)}, bf16[24,768]{1,0:T(8,128)(2,1)S(1)}, u32[]{:S(2)}, u32[]{:S(2)}) collective-permute-start(bf16[24,768]{1,0:T(8,128)(2,1)} %get-tuple-element.263), channel_id=1, source_target_pairs={{0,2},{1,3},{2,4},{3,5},{4,6},{5,7},{6,0},{7,1},{8,10},{9,11},{10,... | collective-permute-start | bytes 110600 | tf_op jit(solution)/shard_map/ppermute | solution.py:55
  399.4 52.6 %collective-permute-start.38 = (bf16[256,768]{1,0:T(8,128)(2,1)}, bf16[256,768]{1,0:T(8,128)(2,1)S(1)}, u32[]{:S(2)}, u32[]{:S(2)}) collective-permute-start(bf16[256,768]{1,0:T(8,128)(2,1)} %get-tuple-element.242), channel_id=1, source_target_pairs={{1,0},{2,1},{3,2},{4,3},{5,4},{6,5},{7,6},{9,8},{10,9},{11,10},{12... | collective-permute-start | bytes 1179656 | tf_op jit(solution)/shard_map/ppermute | solution.py:922
  403.6 50.2 %collective-permute-start.37 = (bf16[256,768]{1,0:T(8,128)(2,1)}, bf16[256,768]{1,0:T(8,128)(2,1)}, u32[]{:S(2)}, u32[]{:S(2)}) collective-permute-start(bf16[256,768]{1,0:T(8,128)(2,1)} %get-tuple-element.241), channel_id=1, source_target_pairs={{0,1},{1,2},{2,3},{3,4},{4,5},{5,6},{6,7},{8,9},{9,10},{10,11},{11... | collective-permute-start | bytes 1179656 | tf_op jit(solution)/shard_map/ppermute | solution.py:925
  408.5 22.4 %collective-permute-start.33 = (bf16[4,24,2432]{2,1,0:T(8,128)(2,1)}, bf16[4,24,2432]{2,1,0:T(8,128)(2,1)S(1)}, u32[]{:S(2)}, u32[]{:S(2)}) collective-permute-start(bf16[4,24,2432]{2,1,0:T(8,128)(2,1)} %get-tuple-element.239), channel_id=1, source_target_pairs={{0,24},{8,16},{16,8},{24,0},{1,25},{9,17},{17,9},{25,1},{2,26},{10... | collective-permute-start | bytes 1400840 | tf_op jit(solution)/shard_map/ppermute | solution.py:67
  436.5 37.8 %collective-permute-start.51 = (bf16[24,768]{1,0:T(8,128)(2,1)S(1)}, bf16[24,768]{1,0:T(8,128)(2,1)S(1)}, u32[]{:S(2)}, u32[]{:S(2)}) collective-permute-start(bf16[24,768]{1,0:T(8,128)(2,1)S(1)} %fusion.42), channel_id=1, source_target_pairs={{0,8},{8,0},{16,24},{24,16},{1,9},{9,1},{17,25},{25,17},{2,10},{10... | collective-permute-start | bytes 110600 | tf_op jit(solution)/shard_map/ppermute | solution.py:67
  437.8 37.5 %collective-permute-start.49 = (bf16[24,768]{1,0:T(8,128)(2,1)S(1)}, bf16[24,768]{1,0:T(8,128)(2,1)S(1)}, u32[]{:S(2)}, u32[]{:S(2)}) collective-permute-start(bf16[24,768]{1,0:T(8,128)(2,1)S(1)} %fusion.42), channel_id=1, source_target_pairs={{0,24},{8,16},{16,8},{24,0},{1,25},{9,17},{17,9},{25,1},{2,26},{10... | collective-permute-start | bytes 110600 | tf_op jit(solution)/shard_map/ppermute | solution.py:67
  (136 other events, 923.6 us)
Sparse Core Ops, SparseCore 0:
  10.2 55.4 all-gather.2
  68.0 21.8 all-gather.4
  363.9 76.4 reduce-scatter.1

commit v2 on v1

--- a/solution.py
+++ b/solution.py
@@ -27,11 +27,21 @@
 BF16 = jnp.bfloat16
 LANES = 128
 HALO = 256
-QUERY_TILE = 256
+QUERY_TILE = 128
+KEY_WINDOW = -(-(2 * SEQ + 15) // 16) * 16
 ROW_TILE = 256
 VMEM_LIMIT = 56 * 1024 * 1024
+EARLY = 8
 EXTRA = 16
-EXPERT_VMEM = 32 * 1024 * 1024
+EXPERT_VMEM = 60 * 1024 * 1024
+
+
+def cheap(flops, bytes_accessed, transcendentals):
+    return pl.CostEstimate(
+        flops=flops // EARLY,
+        bytes_accessed=bytes_accessed // EARLY,
+        transcendentals=transcendentals // EARLY,
+    )
 
 
 def tie_kernel(*refs):
@@ -84,7 +94,7 @@
         ),
         out_shape=jax.ShapeDtypeStruct((count,) + block.shape, block.dtype),
         input_output_aliases={} if out is None else {2: 0},
-        cost_estimate=pl.CostEstimate(
+        cost_estimate=cheap(
             flops=0, bytes_accessed=2 * block.size * block.dtype.itemsize, transcendentals=0
         ),
         name="place",
@@ -123,10 +133,11 @@
     return first, second, first_got, second_got
 
 
-def scatter_dp_middle(state, then):
+def scatter_dp_middle(state, then=None):
     one, two = lax.axis_index("dp") % 2, lax.axis_index("dp") // 2
     first, second, first_got, second_got = state
-    first_got, second_got = tie(first_got, then), tie(second_got, then)
+    if then is not None:
+        first_got, second_got = tie(first_got, then), tie(second_got, then)
     first_sum = added(lax.dynamic_index_in_dim(first, one, 1, False), first_got).astype(BF16)
     second_sum = added(lax.dynamic_index_in_dim(second, two, 0, False), second_got).astype(BF16)
     first_got = across(lax.dynamic_index_in_dim(first_sum, 1 - two, 0, False), 2)
@@ -134,10 +145,11 @@
     return first_sum, second_sum, first_got, second_got
 
 
-def scatter_dp_end(state, then):
+def scatter_dp_end(state, then=None):
     one, two = lax.axis_index("dp") % 2, lax.axis_index("dp") // 2
     first_sum, second_sum, first_got, second_got = state
-    first_got, second_got = tie(first_got, then), tie(second_got, then)
+    if then is not None:
+        first_got, second_got = tie(first_got, then), tie(second_got, then)
     first_sum = added(lax.dynamic_index_in_dim(first_sum, two, 0, False), first_got)
     second_sum = added(lax.dynamic_index_in_dim(second_sum, one, 0, False), second_got)
     return jnp.concatenate([first_sum, second_sum], axis=0)
@@ -160,37 +172,26 @@
     return jnp.concatenate(pieces, axis=0)
 
 
-def sum_to_owner(cut, then=(None, None, None, None)):
-    replicas, chips = cut.shape[1], cut.shape[2]
-    chip, core = lax.axis_index("expert") // 2, lax.axis_index("expert") % 2
-    me = lax.axis_index("dp")
-
-    def held(got, place):
-        return got if then[place] is None else [tie(got[0], then[place])] + got[1:]
-
-    got = held([pair(lax.dynamic_index_in_dim(cut, 1 - core, 0, False))], 0)
-    over_pair = added(lax.dynamic_index_in_dim(cut, core, 0, False), *got).astype(BF16)
+def sum_over_chips(parts):
+    chips = parts.shape[0]
+    chip = lax.axis_index("expert") // 2
     got = [
-        across(lax.dynamic_index_in_dim(over_pair, me ^ bits, 0, False), bits)
-        for bits in range(1, replicas)
-    ]
-    got = held(got, 1)
-    over_dp = added(lax.dynamic_index_in_dim(over_pair, me, 0, False), *got).astype(BF16)
-    got = [
-        hop(lax.dynamic_index_in_dim(over_dp, (chip + step) % chips, 0, False), 2 * step)
+        hop(lax.dynamic_index_in_dim(parts, (chip + step) % chips, 0, False), 2 * step)
         for step in range(1, chips)
     ]
-    got = held(got, 2)
-    owned = added(lax.dynamic_index_in_dim(over_dp, chip, 0, False), *got).astype(BF16)
-    got = held([across(owned, bits) for bits in range(1, replicas)], 3)
-    blocks = [owned] + got
+    return added(lax.dynamic_index_in_dim(parts, chip, 0, False), *got).astype(BF16)
+
+
+def spread_over_dp(owned):
+    replicas, me = lax.axis_size("dp"), lax.axis_index("dp")
+    blocks = [owned] + [across(owned, bits) for bits in range(1, replicas)]
     pieces = []
-    for place in range(replicas):
+    for place_at in range(replicas):
         piece = blocks[0]
         for bits in range(1, replicas):
-            piece = jnp.where(place ^ bits == me, blocks[bits], piece)
+            piece = jnp.where(place_at ^ bits == me, blocks[bits], piece)
         pieces.append(piece.astype(F32))
-    return jnp.concatenate(pieces, axis=0), (over_pair, over_dp, owned)
+    return jnp.concatenate(pieces, axis=0)
 
 
 def standardised(values):
@@ -232,63 +233,79 @@
     return jnp.dot(left, right, preferred_element_type=F32)
 
 
-def head_lanes(head):
-    lane = lax.broadcasted_iota(jnp.int32, (1, LANES), 1)
-    return (lane // HEAD_DIM) == head
-
-
-def attend_kernel(query_image, key_image, q_ref, k_ref, v_ref, out_ref):
-    rows = out_ref.shape[0]
-    window = QUERY_TILE + 2 * HALO
-    for tile in range(rows // QUERY_TILE):
-        low = tile * QUERY_TILE
-        queries = q_ref[HALO + low : HALO + low + QUERY_TILE, :] * SCORE_SCALE
-        keys = k_ref[low : low + window, :]
-        values = v_ref[low : low + window, :]
-        allowed = query_image[low : low + QUERY_TILE, :] == key_image[:, low : low + window]
-        result = None
-        for head in range(LANES // HEAD_DIM):
-            lanes = head_lanes(head)
-            scores = dot_nt(jnp.where(lanes, queries, 0).astype(BF16), keys)
-            scores = jnp.where(allowed, scores, MASKED)
-            raised = jnp.exp(scores - jnp.max(scores, axis=-1, keepdims=True))
-            attend = raised * (1.0 / jnp.sum(raised, axis=-1, keepdims=True))
-            found = dot_nn(attend.astype(BF16), values)
-            result = found if result is None else jnp.where(lanes, found, result)
-        out_ref[low : low + QUERY_TILE, :] = result.astype(BF16)
-
-
-def attention(triple, query_image, key_image):
+def by_head(block):
+    first = lax.broadcasted_iota(jnp.int32, (1, LANES), 1) < HEAD_DIM
+    return jnp.concatenate(
+        [jnp.where(first, block, 0).astype(BF16), jnp.where(first, 0, block).astype(BF16)], axis=0
+    )
+
+
+def from_heads(turned):
+    rows = turned.shape[1] // 2
+    return jnp.concatenate([turned[:HEAD_DIM, :rows], turned[HEAD_DIM:, rows:]], axis=0).T
+
+
+def window_of(starts, tile):
+    return pl.ds(pl.multiple_of(starts[tile], 16), KEY_WINDOW)
+
+
+def attend_tile(tile, window, query_image, key_image, q_ref, keys):
+    low = tile * QUERY_TILE
+    queries = by_head(q_ref[HALO + low : HALO + low + QUERY_TILE, :] * SCORE_SCALE)
+    allowed = key_image[window, :] == query_image[:, low : low + QUERY_TILE]
+    allowed = jnp.concatenate([allowed, allowed], axis=1)
+    scores = jnp.where(allowed, dot_nt(keys, queries), MASKED)
+    raised = jnp.exp(scores - jnp.max(scores, axis=0, keepdims=True))
+    return queries, raised * (1.0 / jnp.sum(raised, axis=0, keepdims=True))
+
+
+def attend_kernel(starts, query_image, key_image, q_ref, k_ref, v_ref, out_ref):
+    for tile in range(out_ref.shape[0] // QUERY_TILE):
+        window = window_of(starts, tile)
+        _, attend = attend_tile(tile, window, query_image, key_image, q_ref, k_ref[window, :])
+        found = dot_tn(v_ref[window, :], attend.astype(BF16))
+        out_ref[tile * QUERY_TILE : (tile + 1) * QUERY_TILE, :] = from_heads(found).astype(BF16)
+
+
+def image_specs(span, rows, blocks):
+    return [
+        pl.BlockSpec((1, rows), lambda i, t: (0, 0)),
+        pl.BlockSpec((span, 1), lambda i, t: (0, 0)),
+        pl.BlockSpec((span, LANES), lambda i, t: (0, i)),
+        pl.BlockSpec((span, LANES), lambda i, t: (0, blocks + i)),
+        pl.BlockSpec((span, LANES), lambda i, t: (0, 2 * blocks + i)),
+    ]
+
+
+def attention(triple, starts, query_image, key_image):
     span = triple.shape[0]
     rows = span - 2 * HALO
     width = triple.shape[1] // 3
     blocks = width // LANES
-    cost = HEADS * rows * (QUERY_TILE + 2 * HALO)
+    cost = HEADS * rows * KEY_WINDOW
     return pl.pallas_call(
         attend_kernel,
-        grid=(blocks,),
-        in_specs=[
-            pl.BlockSpec((rows, 1), lambda i: (0, 0)),
-            pl.BlockSpec((1, span), lambda i: (0, 0)),
-            pl.BlockSpec((span, LANES), lambda i: (0, i)),
-            pl.BlockSpec((span, LANES), lambda i: (0, blocks + i)),
-            pl.BlockSpec((span, LANES), lambda i: (0, 2 * blocks + i)),
-        ],
-        out_specs=pl.BlockSpec((rows, LANES), lambda i: (0, i)),
+        grid_spec=pltpu.PrefetchScalarGridSpec(
+            num_scalar_prefetch=1,
+            grid=(blocks,),
+            in_specs=image_specs(span, rows, blocks),
+            out_specs=pl.BlockSpec((rows, LANES), lambda i, t: (0, i)),
+        ),
         out_shape=jax.ShapeDtypeStruct((rows, width), BF16),
         compiler_params=pltpu.CompilerParams(vmem_limit_bytes=VMEM_LIMIT),
-        cost_estimate=pl.CostEstimate(
+        cost_estimate=cheap(
             flops=cost * 512, bytes_accessed=span * width * 6, transcendentals=cost
         ),
         name="attention",
-    )(query_image[:, None], key_image[None, :], triple, triple, triple)
-
-
-def attend_back_kernel(query_image, key_image, q_ref, k_ref, v_ref, g_ref, out_ref, dk, dv):
+    )(starts, query_image[None, :], key_image[:, None], triple, triple, triple)
+
+
+def attend_back_kernel(
+    starts, query_image, key_image, q_ref, k_ref, v_ref, g_ref, out_ref, dk, dv
+):
     rows = g_ref.shape[0]
     span = k_ref.shape[0]
     width = out_ref.shape[1] // 3
-    window = QUERY_TILE + 2 * HALO
     column = pl.program_id(0) * LANES
 
     def columns(part):
@@ -300,57 +317,44 @@
     out_ref[span - HALO :, columns(0)] = jnp.zeros((HALO, LANES), BF16)
     for tile in range(rows // QUERY_TILE):
         low = tile * QUERY_TILE
-        queries = q_ref[HALO + low : HALO + low + QUERY_TILE, :] * SCORE_SCALE
-        grads = g_ref[low : low + QUERY_TILE, :]
-        keys = k_ref[low : low + window, :]
-        values = v_ref[low : low + window, :]
-        allowed = key_image[low : low + window, :] == query_image[:, low : low + QUERY_TILE]
-        query_grad = None
-        for head in range(LANES // HEAD_DIM):
-            lanes = head_lanes(head)
-            own_queries = jnp.where(lanes, queries, 0).astype(BF16)
-            own_grads = jnp.where(lanes, grads, 0).astype(BF16)
-            scores = jnp.where(allowed, dot_nt(keys, own_queries), MASKED)
-            raised = jnp.exp(scores - jnp.max(scores, axis=0, keepdims=True))
-            attend = raised * (1.0 / jnp.sum(raised, axis=0, keepdims=True))
-            dv[low : low + window, :] += dot_nn(attend.astype(BF16), own_grads)
-            pulled = dot_nt(values, own_grads)
-            inner = jnp.sum(attend * pulled, axis=0, keepdims=True)
-            score_grad = (attend * (pulled - inner)).astype(BF16)
-            dk[low : low + window, :] += dot_nn(score_grad, own_queries)
-            found = dot_tn(score_grad, keys) * SCORE_SCALE
-            query_grad = found if query_grad is None else jnp.where(lanes, found, query_grad)
+        window = window_of(starts, tile)
+        keys = k_ref[window, :]
+        queries, attend = attend_tile(tile, window, query_image, key_image, q_ref, keys)
+        grads = by_head(g_ref[low : low + QUERY_TILE, :])
+        pulled = dot_nt(v_ref[window, :], grads)
+        inner = jnp.sum(attend * pulled, axis=0, keepdims=True)
+        score_grad = (attend * (pulled - inner)).astype(BF16)
+        dv[window, :] += dot_nn(attend.astype(BF16), grads)
+        dk[window, :] += dot_nn(score_grad, queries)
+        query_grad = from_heads(dot_tn(keys, score_grad)) * SCORE_SCALE
         out_ref[HALO + low : HALO + low + QUERY_TILE, columns(0)] = query_grad.astype(BF16)
     out_ref[:, columns(1)] = dk[...].astype(BF16)
     out_ref[:, columns(2)] = dv[...].astype(BF16)
 
 
-def attention_back(triple, grads, query_image, key_image):
+def attention_back(triple, grads, starts, query_image, key_image):
     span = triple.shape[0]
     rows = span - 2 * HALO
     width = triple.shape[1] // 3
     blocks = width // LANES
-    cost = HEADS * rows * (QUERY_TILE + 2 * HALO)
+    cost = HEADS * rows * KEY_WINDOW
     return pl.pallas_call(
         attend_back_kernel,
-        grid=(blocks,),
-        in_specs=[
-            pl.BlockSpec((1, rows), lambda i: (0, 0)),
-            pl.BlockSpec((span, 1), lambda i: (0, 0)),
-            pl.BlockSpec((span, LANES), lambda i: (0, i)),
-            pl.BlockSpec((span, LANES), lambda i: (0, blocks + i)),
-            pl.BlockSpec((span, LANES), lambda i: (0, 2 * blocks + i)),
-            pl.BlockSpec((rows, LANES), lambda i: (0, i)),
-        ],
-        out_specs=pl.BlockSpec((span, 3 * width), lambda i: (0, 0)),
+        grid_spec=pltpu.PrefetchScalarGridSpec(
+            num_scalar_prefetch=1,
+            grid=(blocks,),
+            in_specs=image_specs(span, rows, blocks)
+            + [pl.BlockSpec((rows, LANES), lambda i, t: (0, i))],
+            out_specs=pl.BlockSpec((span, 3 * width), lambda i, t: (0, 0)),
+            scratch_shapes=[pltpu.VMEM((span, LANES), F32), pltpu.VMEM((span, LANES), F32)],
+        ),
         out_shape=jax.ShapeDtypeStruct((span, 3 * width), BF16),
-        scratch_shapes=[pltpu.VMEM((span, LANES), F32), pltpu.VMEM((span, LANES), F32)],
         compiler_params=pltpu.CompilerParams(vmem_limit_bytes=VMEM_LIMIT),
-        cost_estimate=pl.CostEstimate(
+        cost_estimate=cheap(
             flops=cost * 1280, bytes_accessed=span * width * 14, transcendentals=cost
         ),
         name="attention_back",
-    )(query_image[None, :], key_image[:, None], triple, triple, triple, grads)
+    )(starts, query_image[None, :], key_image[:, None], triple, triple, triple, grads)
 
 
 def first_norm_kernel(below, tokens, above, vectors, out):
@@ -367,7 +371,7 @@
         first_norm_kernel,
         out_shape=jax.ShapeDtypeStruct((span, width), BF16),
         compiler_params=pltpu.CompilerParams(vmem_limit_bytes=VMEM_LIMIT),
-        cost_estimate=pl.CostEstimate(
+        cost_estimate=cheap(
             flops=span * width * 10, bytes_accessed=span * width * 4, transcendentals=0
         ),
         name="first_norm",
@@ -375,7 +379,20 @@
 
 
 def dense_back_kernel(
-    layout, hidden, below, tokens, above, grads, weight, small, dense_out, back_out
+    layout,
+    me,
+    hidden,
+    below,
+    tokens,
+    above,
+    grads,
+    weight,
+    heads,
+    branch,
+    small,
+    give_out,
+    keep_out,
+    back_out,
 ):
     cores, replicas, chips, rows = layout
     width = hidden.shape[1]
@@ -403,17 +420,23 @@
     spread = (lane == row).astype(F32)
 
     def store(low, block):
-        for chip in range(chips):
-            for core in range(cores):
-                for replica in range(replicas):
-                    start = ((chip * cores + core) * replicas + replica) * rows
-                    piece = block[start : start + rows].astype(BF16)
-                    dense_out[core, replica, chip, :, low : low + block.shape[1]] = piece
+        for core in range(cores):
+
+            def put(out, core=core):
+                for chip in range(chips):
+                    for replica in range(replicas):
+                        start = ((chip * cores + core) * replicas + replica) * rows
+                        piece = block[start : start + rows].astype(BF16)
+                        out[replica, chip, :, low : low + block.shape[1]] = piece
+
+            pl.when(me[0] == core)(lambda: put(keep_out))
+            pl.when(me[0] != core)(lambda: put(give_out))
 
     for low in range(0, 3 * width, width):
         store(low, dot_tn(hidden[...], grads[:, low : low + width]))
+    store(3 * width, dot_tn(heads[...], branch[...]))
     store(
-        3 * width,
+        4 * width,
         lax.dot_general(
             small[...] + sums,
             spread,
@@ -424,28 +447,32 @@
     )
 
 
-def dense_back(hidden, below, tokens, above, grads, weight, small, layout):
+def dense_back(hidden, below, tokens, above, grads, weight, heads, branch, small, layout):
     span, width = hidden.shape
-    columns = 3 * width + LANES
+    columns = 4 * width + LANES
+    core = lax.axis_index("expert") % 2
     return pl.pallas_call(
         functools.partial(dense_back_kernel, layout),
         out_shape=[
-            jax.ShapeDtypeStruct(layout + (columns,), BF16),
+            jax.ShapeDtypeStruct(layout[1:] + (columns,), BF16),
+            jax.ShapeDtypeStruct(layout[1:] + (columns,), BF16),
             jax.ShapeDtypeStruct((span, width), BF16),
         ],
+        in_specs=[pl.BlockSpec(memory_space=pltpu.SMEM)]
+        + [pl.BlockSpec(memory_space=pltpu.VMEM)] * 9,
         compiler_params=pltpu.CompilerParams(vmem_limit_bytes=VMEM_LIMIT),
-        cost_estimate=pl.CostEstimate(
+        cost_estimate=cheap(
             flops=span * width * width * 12,
             bytes_accessed=span * width * 16 + width * width * 12,
             transcendentals=0,
         ),
         name="dense_back",
-    )(hidden, below, tokens, above, grads, weight, small)
+    )(core.reshape(1), hidden, below, tokens, above, grads, weight, heads, branch, small)
 
 
 def small_adam_kernel(sums, *refs):
     values = [ref[...] for ref in refs[:6]]
-    vectors, matrix = refs[0].shape[0], refs[3].shape[1]
+    vectors, matrix = refs[0].shape[0], refs[3].shape[0]
     rows = sums.shape[0]
     lane = lax.broadcasted_iota(jnp.int32, (rows, rows), 1)
     row = lax.broadcasted_iota(jnp.int32, (rows, rows), 0)
@@ -457,9 +484,7 @@
         preferred_element_type=F32,
     )
     found = adam_step(*values[:3], turned[:vectors], VECTOR_RATE, 0.0)
-    found += adam_step(
-        *values[3:], sums[:, vectors : vectors + matrix], MATRIX_RATE, DECAY
-    )
+    found += adam_step(*values[3:], turned[vectors : vectors + matrix], MATRIX_RATE, DECAY)
     for ref, value in zip(refs[6:], found):
         ref[...] = value
 
@@ -584,7 +609,7 @@
         ],
         input_output_aliases={7 + i: i for i in range(len(kept))},
         compiler_params=pltpu.CompilerParams(vmem_limit_bytes=EXPERT_VMEM),
-        cost_estimate=pl.CostEstimate(
+        cost_estimate=cheap(
             flops=rows * width * hidden * 8,
             bytes_accessed=rows * (2 * hidden + 6 * width) * 2 + 4 * width * hidden,
             transcendentals=rows * hidden,
@@ -664,13 +689,13 @@
             total = added(*terms).astype(BF16)
             carry = ring(total)
         if step + 1 < chips:
-            mine = tie(following, found_other[5])
+            mine = tie(following, found_other[5], *grads_mine[step + 1 :])
     act_all, pre_all, part_all, rows_all, outs = kept
     rows_all, act_all = tie(rows_all, total), tie(act_all, total)
     grad_widen = dot_tn(rows_all, pre_all).astype(BF16)
     grad_narrow = dot_tn(act_all, part_all).astype(BF16)
     grad_all = added(backs[0][0], pair(backs[0][1]), tie(carry, grad_widen, grad_narrow))
-    outs = tie(outs, grad_all)
+    outs = tie(outs, total)
     grad_hidden = grad_all[:rows]
     table = grad_all[rows : rows + 4 * expert_count, :rows]
     table = jnp.sum(table.reshape(2, expert_count, 2, rows), axis=(0, 2))
@@ -791,13 +816,12 @@
 
     grads_mine = [cotangent]
 
-    def next_grads(dependency):
+    def next_grads(*dependencies):
         if by_ring and len(grads_mine) < expert_count:
-            grads_mine.append(ring(tie(grads_mine[-1], dependency)))
-
-    if by_ring and expert_count > 1:
-        grads_mine.append(ring(cotangent))
-    next_grads(triple_weight)
+            grads_mine[-1] = tie(grads_mine[-1], *dependencies)
+            grads_mine.append(ring(grads_mine[-1]))
+
+    next_grads(small_low)
 
     below = lax.ppermute(
         tokens[rows_dev - HALO :], "expert", [(i, i + 1) for i in range(device_count - 1)]
@@ -805,7 +829,10 @@
     above = lax.ppermute(
         tokens[:HALO], "expert", [(i + 1, i) for i in range(device_count - 1)]
     )
+    if by_ring:
+        below = tie(below, experts_near)
     hidden_one = first_norm(below, tokens, above, norm_float[:2])
+    next_grads(hidden_one, triple_weight)
     triple = dot_nn(hidden_one, triple_weight).astype(BF16)
     first_row = device * rows_dev
     query_rows = first_row + jnp.arange(rows_dev, dtype=jnp.int32)
@@ -813,14 +840,20 @@
     query_image = query_rows // SEQ
     inside = (key_rows >= 0) & (key_rows < rows_dev * device_count)
     key_image = jnp.where(inside, key_rows // SEQ, -1)
-    heads_low = attention(triple, query_image, key_image)
-    next_grads(heads_low)
+    tile_rows = first_row + QUERY_TILE * jnp.arange(rows_dev // QUERY_TILE, dtype=jnp.int32)
+    starts = tile_rows // SEQ * SEQ - (first_row - HALO)
+    starts = jnp.minimum(starts // 16 * 16, rows_dev + 2 * HALO - KEY_WINDOW)
+    heads_low = attention(triple, starts, query_image, key_image)
     if by_ring:
         expert_weights = gather_dp_far(experts_near, experts_far)
     tokens_float = tokens.astype(F32)
     resid = tokens_float + dot_nn(heads_low, proj_weight)
     unit_two, inverse_two = standardised(resid)
     hidden_two = (unit_two * norm_float[2] + norm_float[3]).astype(BF16)
+
+    if by_ring:
+        hidden_two = tie(hidden_two, grads_mine[-1])
+    next_grads(hidden_two)
 
     logits = lax.dot_general(
         router_low, hidden_two, (((1,), (1,)), ((), ())), preferred_element_type=F32
@@ -867,9 +900,11 @@
     )
     grad_branch = grad_resid.astype(BF16)
     grad_heads = dot_nt(grad_branch, proj_weight).astype(BF16)
-    grad_proj = dot_tn(heads_low, grad_branch).astype(BF16)
-
-    grad_triple = attention_back(triple, grad_heads, query_image, key_image)
+
+    grad_triple = attention_back(triple, grad_heads, starts, query_image, key_image)
+    if by_ring:
+        scattered = [scatter_dp_middle(state, grad_triple) for state in scattered]
+        grad_triple = tie(grad_triple, *(part for state in scattered for part in state[:2]))
     by_owner = (2, replicas, expert_count, width // (device_count * replicas))
     small_rows = jnp.concatenate(
         [
@@ -880,23 +915,28 @@
         axis=0,
     )
     if by_ring:
-        grad_dense, grad_hidden_one = dense_back(
+        grad_give, grad_keep, grad_hidden_one = dense_back(
             hidden_one,
             below,
             tokens,
             above,
             grad_triple,
             triple_weight,
+            heads_low,
+            grad_branch,
             small_rows,
             by_owner,
         )
-        dense_sum, (over_pair, over_dp, owned) = sum_to_owner(grad_dense)
-        cut = grad_proj.reshape(expert_count, 2, replicas, -1, width).transpose(1, 2, 0, 3, 4)
-        proj_sum, _ = sum_to_owner(cut, (grad_heads, grad_triple, over_pair, owned))
-        scattered = [scatter_dp_middle(state, over_pair) for state in scattered]
-        widen_sum, narrow_sum = [scatter_dp_end(state, over_dp) for state in scattered]
-        attention_sum = jnp.concatenate([dense_sum[:, : 3 * width], proj_sum], axis=1)
-        small_sum = dense_sum[:, 3 * width :]
+        out = lax.psum_scatter(out, "expert", scatter_dimension=0, tiled=True)
+        over_pair = added(grad_keep, pair(tie(grad_give, out))).astype(BF16)
+        over_dp = scatter_dp_end(scatter_dp_middle(scatter_dp_start(over_pair)))
+        over_dp = over_dp.astype(BF16)
+        owned = sum_over_chips(over_dp)
+        dense_sum = spread_over_dp(owned)
+        widen_sum, narrow_sum = [scatter_dp_end(state, over_pair) for state in scattered]
+        out = tie(out, owned)
+        attention_sum = dense_sum[:, : 4 * width]
+        small_sum = dense_sum[:, 4 * width :]
     else:
         grad_hidden_one = dot_nt(grad_triple, triple_weight)
         extended = jnp.concatenate([below, tokens, above], axis=0).astype(F32)
@@ -905,7 +945,11 @@
         small_rows = small_rows.at[1].set(jnp.sum(grad_hidden_one, axis=0))
         grad_hidden_one = grad_hidden_one.astype(BF16)
         grad_dense = jnp.concatenate(
-            [dot_tn(hidden_one, grad_triple).astype(BF16), grad_proj, small_rows.T.astype(BF16)],
+            [
+                dot_tn(hidden_one, grad_triple).astype(BF16),
+                dot_tn(heads_low, grad_branch).astype(BF16),
+                small_rows.T.astype(BF16),
+            ],
             axis=1,
         )
         widen_sum = lax.psum_scatter(
@@ -937,8 +981,7 @@
     tokens_grad = grad_resid + norm_pull(grad_own, unit_one, inverse_one, norm_float[0])
 
     if by_ring:
-        out = lax.psum_scatter(out, "expert", scatter_dimension=0, tiled=True)
-        out = tie(out, owned).astype(F32)
+        out = out.astype(F32)
     mixed = (resid + out).astype(BF16)
     attention_new = adam_step(
         attention_weight, attention_first, attention_second, attention_sum, MATRIX_RATE, DECAY
@@ -949,11 +992,12 @@
             norm_vectors,
             norm_first,
             norm_second,
-            router_weight,
-            router_first,
-            router_second,
+            router_weight.T,
+            router_first.T,
+            router_second.T,
         )
-        norm_new, router_new = tuple(small_new[:3]), tuple(small_new[3:])
+        norm_new = tuple(small_new[:3])
+        router_new = tuple(array.T for array in small_new[3:])
     else:
         norm_new = adam_step(
             norm_vectors, norm_first, norm_second, small_sum[:, :4].T, VECTOR_RATE, 0.0

time: 511 us -> 443 us (0.87)
  the two profiles are of different devices: /device:TPU:0 before, /device:TPU:8 now
where the time goes in v2:
time: 443 us; the launch traced here: 435 us
  Pallas kernels  152 us (34%)
  waiting for transfers between devices  72.5 us (16%)
  starting transfers between devices  57.7 us (13%)
  other arithmetic  57.1 us (13%)
  matrix products  43.4 us (10%)
  local copies, waits for them, and re-layouts  37.2 us (8%)
  between operations  15.7 us (4%)
    pallas_call x8, Pallas kernels, expert_block(): pl.pallas_call(functools.partial(expert_kernel, first), grid_spec=pltpu.P...  83.5 us
    dot_general x2, matrix products, dot_tn(): lax.dot_general(left, right, (((0,), (0,)), ((), ())), preferred_element_...  28.4 us
    ppermute x15, waiting for transfers between devices, hop(): lax.ppermute(block, 'expert', [(i, (i + distance) % count) for i in range...  26 us
    ppermute x18, starting transfers between devices, across(): lax.ppermute(block, 'dp', [(i, i ^ bit) for i in range(lax.axis_size('dp'...  23.3 us
    ppermute x15, starting transfers between devices, hop(): lax.ppermute(block, 'expert', [(i, (i + distance) % count) for i in range...  22.4 us
    unnamed x173, local copies, waits for them, and re-layouts  21 us
    ppermute x18, waiting for transfers between devices, across(): lax.ppermute(block, 'dp', [(i, i ^ bit) for i in range(lax.axis_size('dp'...  20.6 us
    pallas_call x1, Pallas kernels, attention_back(): pl.pallas_call(attend_back_kernel, grid_spec=pltpu.PrefetchScalarGridSpec...  19.9 us
  transfers between devices with their start and end apart: 54, of which 16 were waited for; matrix products, arithmetic and copies ran while one was open for 25% of the time, Pallas kernels for 34%

profile of v2, /device:TPU:8, one launch (start us, length us, event | category | flops | bytes accessed | tf_op | source)
XLA Modules:
  0.0 435.3 jit_solution(14295650261704164883)
XLA Ops:
  15.8 2.6 collective-permute-start.6
  18.4 2.5 collective-permute-start.7
  25.0 3.6 collective-permute-start.3
  46.4 14.9 %collective-permute-done.3.above = bf16[256,768]{1,0:T(8,128)(2,1)S(1)} collective-permute-done((bf16[256,768]{1,0:T(8,128)(2,1)S(1)}, bf16[256,768]{1,0:T(8,128)(2,1)S(1)}, u32[]{:S(2)}, u32[]{:S(2)}) %collective-permute-start.3) | collective-permute-done | bytes 393248 | tf_op jit(solution)/shard_map/ppermute | solution.py:829
  62.0 3.6 first_norm.1.refs_1_.hidden
  66.8 3.2 all-gather.3.cloned.1.call-done.refs_2_.weight
  72.0 7.4 %convolution_convert_fusion.q_ref.k_ref.v_ref = bf16[1024,2304]{1,0:T(8,128)(2,1)} fusion(bf16[1024,768]{1,0:T(8,128)(2,1)S(1)} %copy-done.11, bf16[768,2304]{1,0:T(8,128)(2,1)} %all-gather.3.cloned.1.call-done.refs_2_.weight), kind=kOutput, calls=%fused_computation | convolution fusion | flops 3626237952 | bytes 9830400 | tf_op jit(solution)/shard_map/dot_general | solution.py:233
  79.4 15.0 %attention.1.heads = bf16[512,768]{1,0:T(8,128)(2,1)} custom-call(s32[4]{0:T(128)} %multiply_minimum_fusion.starts, s32[1,512]{1,0:T(1,128)} %and_select_fusion.query_image, s32[1024,1]{1,0:T(8,128)} %fusion.25.key_image, bf16[1024,2304]{1,0:T(8,128)(2,1)} %convolution_convert_fusion.q_ref.k_ref.v_ref, ...), custom_call_target="tpu_custom_call" | custom-call | flops 163577856 | bytes 589824 | tf_op jit(solution)/shard_map/attention/pallas_call | solution.py:286
  94.4 7.4 %all-gather.5.cloned.1.call-done = bf16[768,768]{1,0:T(8,128)(2,1)} async-done(((bf16[96,768]{1,0:T(8,128)(2,1)}), bf16[768,768]{1,0:T(8,128)(2,1)}) %all-gather.5.cloned.1.call-update) | async-done | bytes 1179664 | tf_op jit(solution)/shard_map/all_gather | solution.py:802
  101.9 2.4 fusion.69
  116.2 10.4 %expert_block.8 = (bf16[4096,1536]{1,0:T(8,128)(2,1)}, bf16[4096,1536]{1,0:T(8,128)(2,1)}, bf16[4096,768]{1,0:T(8,128)(2,1)}, bf16[4096,768]{1,0:T(8,128)(2,1)},...) custom-call(s32[1]{0:T(128)} %bitcast.16.target, bf16[528,768]{1,0:T(8,128)(2,1)} %copy-done.17, ...), custom_call_target="tpu_custom_call" | custom-call | flops 603979776 | bytes 1572864 | tf_op jit(solution)/shard_map/expert_block/pallas_call | solution.py:577
  126.6 10.4 %expert_block.9 = (bf16[4096,1536]{1,0:T(8,128)(2,1)}, bf16[4096,1536]{1,0:T(8,128)(2,1)}, bf16[4096,768]{1,0:T(8,128)(2,1)}, bf16[4096,768]{1,0:T(8,128)(2,1)},...) custom-call(s32[1]{0:T(128)} %bitcast.12.target, ...), custom_call_target="tpu_custom_call", output_to_operand_aliasing={{0}: (7, {}), {1}: (8, {}), {2}: (9, {}), {3}: (10, {}), {4... | custom-call | flops 603979776 | bytes 1572864 | tf_op jit(solution)/shard_map/expert_block/pallas_call | solution.py:577
  137.1 11.0 %collective-permute-done.14.refs_4_.refs_3_.refs_2_.grads_ref = bf16[512,768]{1,0:T(8,128)(2,1)S(1)} collective-permute-done((bf16[512,768]{1,0:T(8,128)(2,1)}, bf16[512,768]{1,0:T(8,128)(2,1)S(1)}, u32[]{:S(2)}, u32[]{:S(2)}) %collective-permute-start.14) | collective-permute-done | bytes 786464 | tf_op jit(solution)/shard_map/ppermute | solution.py:65
  151.4 10.4 %expert_block.10 = (bf16[4096,1536]{1,0:T(8,128)(2,1)}, bf16[4096,1536]{1,0:T(8,128)(2,1)}, bf16[4096,768]{1,0:T(8,128)(2,1)}, bf16[4096,768]{1,0:T(8,128)(2,1)}...) custom-call(s32[1]{0:T(128)} %bitcast.18.target, ...), custom_call_target="tpu_custom_call", output_to_operand_aliasing={{0}: (7, {}), {1}: (8, {}), {2}: (9, {}), {3}: (10, {}), {4... | custom-call | flops 603979776 | bytes 1572864 | tf_op jit(solution)/shard_map/expert_block/pallas_call | solution.py:577
  163.0 10.4 %expert_block.11 = (bf16[4096,1536]{1,0:T(8,128)(2,1)}, bf16[4096,1536]{1,0:T(8,128)(2,1)}, bf16[4096,768]{1,0:T(8,128)(2,1)}, bf16[4096,768]{1,0:T(8,128)(2,1)}...) custom-call(s32[1]{0:T(128)} %bitcast.17.target, ...), custom_call_target="tpu_custom_call", output_to_operand_aliasing={{0}: (7, {}), {1}: (8, {}), {2}: (9, {}), {3}: (10, {}), {4... | custom-call | flops 603979776 | bytes 1572864 | tf_op jit(solution)/shard_map/expert_block/pallas_call | solution.py:577
  176.5 10.5 %expert_block.12 = (bf16[4096,1536]{1,0:T(8,128)(2,1)}, bf16[4096,1536]{1,0:T(8,128)(2,1)}, bf16[4096,768]{1,0:T(8,128)(2,1)}, bf16[4096,768]{1,0:T(8,128)(2,1)}...) custom-call(s32[1]{0:T(128)} %bitcast.20.target, ...), custom_call_target="tpu_custom_call", output_to_operand_aliasing={{0}: (7, {}), {1}: (8, {}), {2}: (9, {}), {3}: (10, {}), {4... | custom-call | flops 603979776 | bytes 1572864 | tf_op jit(solution)/shard_map/expert_block/pallas_call | solution.py:577
  189.2 4.6 %collective-permute-start.26 = (bf16[528,768]{1,0:T(8,128)(2,1)}, bf16[528,768]{1,0:T(8,128)(2,1)S(1)}, u32[]{:S(2)}, u32[]{:S(2)}) collective-permute-start(bf16[528,768]{1,0:T(8,128)(2,1)} %add_convert_fusion.3), channel_id=1, source_target_pairs={{0,2},{1,3},{2,4},{3,5},{4,6},{5,7},{6,0},{7,1},{8,10},{9,11},{10,... | collective-permute-start | bytes 2433032 | tf_op jit(solution)/shard_map/ppermute | solution.py:65
  194.7 10.4 %expert_block.13 = (bf16[4096,1536]{1,0:T(8,128)(2,1)}, bf16[4096,1536]{1,0:T(8,128)(2,1)}, bf16[4096,768]{1,0:T(8,128)(2,1)}, bf16[4096,768]{1,0:T(8,128)(2,1)}...) custom-call(s32[1]{0:T(128)} %bitcast.19.target, ...), custom_call_target="tpu_custom_call", output_to_operand_aliasing={{0}: (7, {}), {1}: (8, {}), {2}: (9, {}), {3}: (10, {}), {4... | custom-call | flops 603979776 | bytes 1572864 | tf_op jit(solution)/shard_map/expert_block/pallas_call | solution.py:577
  206.6 10.5 %expert_block.14 = (bf16[4096,1536]{1,0:T(8,128)(2,1)}, bf16[4096,1536]{1,0:T(8,128)(2,1)}, bf16[4096,768]{1,0:T(8,128)(2,1)}, bf16[4096,768]{1,0:T(8,128)(2,1)}...) custom-call(s32[1]{0:T(128)} %bitcast.21.target, ...), custom_call_target="tpu_custom_call", output_to_operand_aliasing={{0}: (7, {}), {1}: (8, {}), {2}: (9, {}), {3}: (10, {}), {4... | custom-call | flops 603979776 | bytes 1572864 | tf_op jit(solution)/shard_map/expert_block/pallas_call | solution.py:577
  220.7 10.5 %expert_block.15 = (bf16[4096,1536]{1,0:T(8,128)(2,1)}, bf16[4096,1536]{1,0:T(8,128)(2,1)}, bf16[4096,768]{1,0:T(8,128)(2,1)}, bf16[4096,768]{1,0:T(8,128)(2,1)}...) custom-call(s32[1]{0:T(128)} %bitcast.9.target, ...), custom_call_target="tpu_custom_call", output_to_operand_aliasing={{0}: (7, {}), {1}: (8, {}), {2}: (9, {}), {3}: (10, {}), {4... | custom-call | flops 603979776 | bytes 1572864 | tf_op jit(solution)/shard_map/expert_block/pallas_call | solution.py:577
  231.5 8.7 %collective-permute-done.27 = bf16[528,768]{1,0:T(8,128)(2,1)S(1)} collective-permute-done((bf16[528,768]{1,0:T(8,128)(2,1)}, bf16[528,768]{1,0:T(8,128)(2,1)S(1)}, u32[]{:S(2)}, u32[]{:S(2)}) %collective-permute-start.27) | collective-permute-done | bytes 811040 | tf_op jit(solution)/shard_map/ppermute | solution.py:65
  243.0 14.9 %convolution_convert_fusion.1.refs_2_ = bf16[1536,768]{1,0:T(8,128)(2,1)S(1)} fusion(bf16[4096,1536]{1,0:T(8,128)(2,1)} %tie.34, bf16[4096,768]{1,0:T(8,128)(2,1)} %get-tuple-element.121), kind=kOutput, calls=%fused_computation.2 | convolution fusion | flops 9664856064 | bytes 21233664 | tf_op jit(solution)/shard_map/dot_general | solution.py:229
  265.3 13.5 %convolution_convert_fusion.2.refs_1_ = bf16[768,1536]{1,0:T(8,128)(2,1)S(1)} fusion(bf16[4096,768]{1,0:T(8,128)(2,1)S(1)} %copy-done, bf16[4096,1536]{1,0:T(8,128)(2,1)} %get-tuple-element.119), kind=kOutput, calls=%fused_computation.3 | convolution fusion | flops 9664856064 | bytes 21233664 | tf_op jit(solution)/shard_map/dot_general | solution.py:229
  291.3 19.9 %attention_back.1.refs_1_.refs_0_ = bf16[1024,2304]{1,0:T(8,128)(2,1)} custom-call(s32[4]{0:T(128)} %multiply_minimum_fusion.starts, s32[1,512]{1,0:T(1,128)} %and_select_fusion.query_image, s32[1024,1]{1,0:T(8,128)} %fusion.25.key_image, bf16[1024,2304]{1,0:T(8,128)(2,1)} %convolution_convert_fusion.q_ref.k_ref.v_ref, ...), custom_call_target="tpu_custom_call" | custom-call | flops 408944640 | bytes 1376256 | tf_op jit(solution)/shard_map/attention_back/pallas_call | solution.py:341
  323.2 19.4 %dense_back.1 = (bf16[4,4,24,3200]{3,2,1,0:T(8,128)(2,1)}, bf16[4,4,24,3200]{3,2,1,0:T(8,128)(2,1)}, bf16[1024,768]{1,0:T(8,128)(2,1)}) custom-call(s32[1]{0:T(128)} %bitcast.22.me, bf16[1024,768]{1,0:T(8,128)(2,1)} %first_norm.1.refs_1_.hidden, bf16[256,768]{1,0:T(8,128)(2,1)} %tie.24.below, bf16[512,768]{1,0:T(8,128)(2,1)} %tokens.3, ...), custom_call_target="tpu_custom_call" | custom-call | flops 905969664 | bytes 2457600 | tf_op jit(solution)/shard_map/dense_back/pallas_call | solution.py:454
  353.6 4.4 %add_convert_fusion.refs_1_ = bf16[4,4,24,3200]{3,2,1,0:T(8,128)(2,1)} fusion(bf16[4,4,24,3200]{3,2,1,0:T(8,128)(2,1)} %collective-permute-done.34, bf16[4,4,24,3200]{3,2,1,0:T(8,128)(2,1)} %get-tuple-element.122), kind=kLoop, calls=%fused_computation.1 | loop fusion | flops 4915200 | bytes 7372800 | tf_op jit(solution)/shard_map/convert_element_type | solution.py:931
  375.4 2.4 multiply_subtract_fusion.1
  377.8 8.5 %collective-permute-done.37 = bf16[2,2,24,3200]{3,2,1,0:T(8,128)(2,1)S(1)} collective-permute-done((bf16[2,2,24,3200]{3,2,1,0:T(8,128)(2,1)S(1)}, bf16[2,2,24,3200]{3,2,1,0:T(8,128)(2,1)S(1)}, u32[]{:S(2)}, u32[]{:S(2)}) %collective-permute-start.37) | collective-permute-done | bytes 614432 | tf_op jit(solution)/shard_map/ppermute | solution.py:77
  389.1 5.7 %collective-permute-done.38 = bf16[2,24,3200]{2,1,0:T(8,128)(2,1)S(1)} collective-permute-done((bf16[2,24,3200]{2,1,0:T(8,128)(2,1)S(1)}, bf16[2,24,3200]{2,1,0:T(8,128)(2,1)S(1)}, u32[]{:S(2)}, u32[]{:S(2)}) %collective-permute-start.38) | collective-permute-done | bytes 307232 | tf_op jit(solution)/shard_map/ppermute | solution.py:77
  396.4 4.9 %collective-permute-start.40 = (bf16[24,3200]{1,0:T(8,128)(2,1)}, bf16[24,3200]{1,0:T(8,128)(2,1)S(1)}, u32[]{:S(2)}, u32[]{:S(2)}) collective-permute-start(bf16[24,3200]{1,0:T(8,128)(2,1)} %get-tuple-element.168), channel_id=1, source_target_pairs={{0,4},{1,5},{2,6},{3,7},{4,0},{5,1},{6,2},{7,3},{8,12},{9,13},{10,... | collective-permute-start | bytes 460808 | tf_op jit(solution)/shard_map/ppermute | solution.py:65
  404.8 2.9 fusion.7
  409.6 3.2 collective-permute-done.41
  (409 shorter events, 149.4 us)
Async XLA Ops:
  7.2 62.8 %all-gather.3.cloned.1.call-start = ((), (), s32[]{:S(2)}) async-start(), calls=%async_computation.1 | async-start | bytes 3981312 | tf_op jit(solution)/shard_map/all_gather | solution.py:800
  9.5 92.4 %all-gather.5.cloned.1.call-start = ((), (), s32[]{:S(2)}) async-start(), calls=%async_computation.2 | async-start | bytes 1327104 | tf_op jit(solution)/shard_map/all_gather | solution.py:802
  11.0 28.7 %collective-permute-start.2 = (bf16[768,768]{1,0:T(8,128)(2,1)S(1)}, bf16[768,768]{1,0:T(8,128)(2,1)}, u32[]{:S(2)}, u32[]{:S(2)}) collective-permute-start(bf16[768,768]{1,0:T(8,128)(2,1)S(1)} %pad_maximum_fusion.block), channel_id=1, source_target_pairs={{0,8},{8,0},{16,24},{24,16},{1,9},{9,1},{17,25},{25,17},{2,10},{10... | collective-permute-start | bytes 3538952 | tf_op jit(solution)/shard_map/ppermute | solution.py:77
  12.5 30.9 %collective-permute-start.1 = (bf16[768,768]{1,0:T(8,128)(2,1)S(1)}, bf16[768,768]{1,0:T(8,128)(2,1)}, u32[]{:S(2)}, u32[]{:S(2)}) collective-permute-start(bf16[768,768]{1,0:T(8,128)(2,1)S(1)} %pad_maximum_fusion.block), channel_id=1, source_target_pairs={{0,16},{8,24},{16,0},{24,8},{1,17},{9,25},{17,1},{25,9},{2,18},{10... | collective-permute-start | bytes 3538952 | tf_op jit(solution)/shard_map/ppermute | solution.py:77
  14.9 327.7 %reduce-scatter.2.cloned.1.call-start = ((), (), s32[]{:S(2)}) async-start(), calls=%async_computation.3 | async-start | bytes 7077888 | tf_op jit(solution)/shard_map/reduce_scatter | solution.py:930
  23.1 22.5 %collective-permute-start = (bf16[256,768]{1,0:T(8,128)(2,1)S(1)}, bf16[256,768]{1,0:T(8,128)(2,1)S(1)}, u32[]{:S(2)}, u32[]{:S(2)}) collective-permute-start(bf16[256,768]{1,0:T(8,128)(2,1)S(1)} %get-tuple-element.162), channel_id=1, source_target_pairs={{0,1},{1,2},{2,3},{3,4},{4,5},{5,6},{6,7},{8,9},{9,10},{10,11},{11... | collective-permute-start | bytes 1179656 | tf_op jit(solution)/shard_map/ppermute | solution.py:826
  25.0 36.3 %collective-permute-start.3 = (bf16[256,768]{1,0:T(8,128)(2,1)S(1)}, bf16[256,768]{1,0:T(8,128)(2,1)S(1)}, u32[]{:S(2)}, u32[]{:S(2)}) collective-permute-start(bf16[256,768]{1,0:T(8,128)(2,1)S(1)} %get-tuple-element.161), channel_id=1, source_target_pairs={{1,0},{2,1},{3,2},{4,3},{5,4},{6,5},{7,6},{9,8},{10,9},{11,10},{12... | collective-permute-start | bytes 1179656 | tf_op jit(solution)/shard_map/ppermute | solution.py:829
  29.4 37.4 %collective-permute-start.8 = (bf16[512,768]{1,0:T(8,128)(2,1)}, bf16[512,768]{1,0:T(8,128)(2,1)S(1)}, u32[]{:S(2)}, u32[]{:S(2)}) collective-permute-start(bf16[512,768]{1,0:T(8,128)(2,1)} %tie.25.grads_ref), channel_id=1, source_target_pairs={{0,2},{1,3},{2,4},{3,5},{4,6},{5,7},{6,0},{7,1},{8,10},{9,11},{10,... | collective-permute-start | bytes 2359304 | tf_op jit(solution)/shard_map/ppermute | solution.py:65
  39.7 73.7 %collective-permute-start.13 = (bf16[768,768]{1,0:T(8,128)(2,1)}, bf16[768,768]{1,0:T(8,128)(2,1)}, u32[]{:S(2)}, u32[]{:S(2)}) collective-permute-start(bf16[768,768]{1,0:T(8,128)(2,1)} %copy-done.34), channel_id=1, source_target_pairs={{0,24},{8,16},{16,8},{24,0},{1,25},{9,17},{17,9},{25,1},{2,26},{10... | collective-permute-start | bytes 3538952 | tf_op jit(solution)/shard_map/ppermute | solution.py:77
  70.0 35.8 %collective-permute-start.9 = (bf16[512,768]{1,0:T(8,128)(2,1)}, bf16[512,768]{1,0:T(8,128)(2,1)S(1)}, u32[]{:S(2)}, u32[]{:S(2)}) collective-permute-start(bf16[512,768]{1,0:T(8,128)(2,1)} %tie.26.refs_2_.grads_ref), channel_id=1, source_target_pairs={{0,2},{1,3},{2,4},{3,5},{4,6},{5,7},{6,0},{7,1},{8,10},{9,11},{10,... | collective-permute-start | bytes 2359304 | tf_op jit(solution)/shard_map/ppermute | solution.py:65
  110.2 16.4 %collective-permute-start.11 = (bf16[528,768]{1,0:T(8,128)(2,1)S(1)}, bf16[528,768]{1,0:T(8,128)(2,1)}, u32[]{:S(2)}, u32[]{:S(2)}) collective-permute-start(bf16[528,768]{1,0:T(8,128)(2,1)S(1)} %pad_maximum_fusion.4.rows_ref.gates), channel_id=1, source_target_pairs={{0,1},{1,0},{2,3},{3,2},{4,5},{5,4},{6,7},{7,6},{8,9},{9,8},{10,11... | collective-permute-start | bytes 2433032 | tf_op jit(solution)/shard_map/ppermute | solution.py:73
  110.5 16.1 %collective-permute-start.12 = (bf16[512,768]{1,0:T(8,128)(2,1)S(1)}, bf16[512,768]{1,0:T(8,128)(2,1)}, u32[]{:S(2)}, u32[]{:S(2)}) collective-permute-start(bf16[512,768]{1,0:T(8,128)(2,1)S(1)} %copy-done.21), channel_id=1, source_target_pairs={{0,1},{1,0},{2,3},{3,2},{4,5},{5,4},{6,7},{7,6},{8,9},{9,8},{10,11... | collective-permute-start | bytes 2359304 | tf_op jit(solution)/shard_map/ppermute | solution.py:73
  110.7 37.3 %collective-permute-start.10 = (bf16[528,768]{1,0:T(8,128)(2,1)S(1)}, bf16[528,768]{1,0:T(8,128)(2,1)S(1)}, u32[]{:S(2)}, u32[]{:S(2)}) collective-permute-start(bf16[528,768]{1,0:T(8,128)(2,1)S(1)} %pad_maximum_fusion.4.rows_ref.gates), channel_id=1, source_target_pairs={{0,2},{1,3},{2,4},{3,5},{4,6},{5,7},{6,0},{7,1},{8,10},{9,11},{10,... | collective-permute-start | bytes 2433032 | tf_op jit(solution)/shard_map/ppermute | solution.py:65
  111.9 36.2 %collective-permute-start.14 = (bf16[512,768]{1,0:T(8,128)(2,1)}, bf16[512,768]{1,0:T(8,128)(2,1)S(1)}, u32[]{:S(2)}, u32[]{:S(2)}) collective-permute-start(bf16[512,768]{1,0:T(8,128)(2,1)} %tie.28.refs_3_.refs_2_.grads_ref), channel_id=1, source_target_pairs={{0,2},{1,3},{2,4},{3,5},{4,6},{5,7},{6,0},{7,1},{8,10},{9,11},{10,... | collective-permute-start | bytes 2359304 | tf_op jit(solution)/shard_map/ppermute | solution.py:65
  150.3 23.4 %collective-permute-start.15 = (bf16[528,768]{1,0:T(8,128)(2,1)}, bf16[528,768]{1,0:T(8,128)(2,1)S(1)}, u32[]{:S(2)}, u32[]{:S(2)}) collective-permute-start(bf16[528,768]{1,0:T(8,128)(2,1)} %tie.29.rows_ref.gates), channel_id=1, source_target_pairs={{0,2},{1,3},{2,4},{3,5},{4,6},{5,7},{6,0},{7,1},{8,10},{9,11},{10,... | collective-permute-start | bytes 2433032 | tf_op jit(solution)/shard_map/ppermute | solution.py:65
  174.6 19.2 %collective-permute-start.19 = (bf16[528,768]{1,0:T(8,128)(2,1)}, bf16[528,768]{1,0:T(8,128)(2,1)S(1)}, u32[]{:S(2)}, u32[]{:S(2)}) collective-permute-start(bf16[528,768]{1,0:T(8,128)(2,1)} %tie.30.rows_ref.gates), channel_id=1, source_target_pairs={{0,1},{1,0},{2,3},{3,2},{4,5},{5,4},{6,7},{7,6},{8,9},{9,8},{10,11... | collective-permute-start | bytes 2433032 | tf_op jit(solution)/shard_map/ppermute | solution.py:73
  174.9 18.9 %collective-permute-start.20 = (bf16[512,768]{1,0:T(8,128)(2,1)S(1)}, bf16[512,768]{1,0:T(8,128)(2,1)}, u32[]{:S(2)}, u32[]{:S(2)}) collective-permute-start(bf16[512,768]{1,0:T(8,128)(2,1)S(1)} %copy-done.10), channel_id=1, source_target_pairs={{0,1},{1,0},{2,3},{3,2},{4,5},{5,4},{6,7},{7,6},{8,9},{9,8},{10,11... | collective-permute-start | bytes 2359304 | tf_op jit(solution)/shard_map/ppermute | solution.py:73
  175.1 30.1 %collective-permute-start.18 = (bf16[528,768]{1,0:T(8,128)(2,1)}, bf16[528,768]{1,0:T(8,128)(2,1)S(1)}, u32[]{:S(2)}, u32[]{:S(2)}) collective-permute-start(bf16[528,768]{1,0:T(8,128)(2,1)} %tie.30.rows_ref.gates), channel_id=1, source_target_pairs={{0,2},{1,3},{2,4},{3,5},{4,6},{5,7},{6,0},{7,1},{8,10},{9,11},{10,... | collective-permute-start | bytes 2433032 | tf_op jit(solution)/shard_map/ppermute | solution.py:65
  189.2 27.9 %collective-permute-start.26 = (bf16[528,768]{1,0:T(8,128)(2,1)}, bf16[528,768]{1,0:T(8,128)(2,1)S(1)}, u32[]{:S(2)}, u32[]{:S(2)}) collective-permute-start(bf16[528,768]{1,0:T(8,128)(2,1)} %add_convert_fusion.3), channel_id=1, source_target_pairs={{0,2},{1,3},{2,4},{3,5},{4,6},{5,7},{6,0},{7,1},{8,10},{9,11},{10,... | collective-permute-start | bytes 2433032 | tf_op jit(solution)/shard_map/ppermute | solution.py:65
  219.5 20.7 %collective-permute-start.27 = (bf16[528,768]{1,0:T(8,128)(2,1)}, bf16[528,768]{1,0:T(8,128)(2,1)S(1)}, u32[]{:S(2)}, u32[]{:S(2)}) collective-permute-start(bf16[528,768]{1,0:T(8,128)(2,1)} %add_convert_fusion.2), channel_id=1, source_target_pairs={{0,2},{1,3},{2,4},{3,5},{4,6},{5,7},{6,0},{7,1},{8,10},{9,11},{10,... | collective-permute-start | bytes 2433032 | tf_op jit(solution)/shard_map/ppermute | solution.py:65
  241.5 42.4 %collective-permute-start.28 = (bf16[528,768]{1,0:T(8,128)(2,1)}, bf16[528,768]{1,0:T(8,128)(2,1)}, u32[]{:S(2)}, u32[]{:S(2)}) collective-permute-start(bf16[528,768]{1,0:T(8,128)(2,1)} %get-tuple-element.79.refs_1_), channel_id=1, source_target_pairs={{0,1},{1,0},{2,3},{3,2},{4,5},{5,4},{6,7},{7,6},{8,9},{9,8},{10,11... | collective-permute-start | bytes 2433032 | tf_op jit(solution)/shard_map/ppermute | solution.py:73
  242.5 39.5 %collective-permute-start.29 = (bf16[528,768]{1,0:T(8,128)(2,1)S(1)}, bf16[528,768]{1,0:T(8,128)(2,1)}, u32[]{:S(2)}, u32[]{:S(2)}) collective-permute-start(bf16[528,768]{1,0:T(8,128)(2,1)S(1)} %copy-done.12), channel_id=1, source_target_pairs={{0,2},{1,3},{2,4},{3,5},{4,6},{5,7},{6,0},{7,1},{8,10},{9,11},{10,... | collective-permute-start | bytes 2433032 | tf_op jit(solution)/shard_map/ppermute | solution.py:65
  260.2 51.0 %collective-permute-start.33 = (bf16[2,192,768]{2,1,0:T(8,128)(2,1)}, bf16[2,192,768]{2,1,0:T(8,128)(2,1)}, u32[]{:S(2)}, u32[]{:S(2)}) collective-permute-start(bf16[2,192,768]{2,1,0:T(8,128)(2,1)} %dynamic-slice_bitcast_fusion.2), channel_id=1, source_target_pairs={{0,16},{8,24},{16,0},{24,8},{1,17},{9,25},{17,1},{25,9},{2,18},{10... | collective-permute-start | bytes 1769480 | tf_op jit(solution)/shard_map/ppermute | solution.py:77
  263.2 48.1 %collective-permute-start.32 = (bf16[2,192,768]{2,1,0:T(8,128)(2,1)}, bf16[2,192,768]{2,1,0:T(8,128)(2,1)}, u32[]{:S(2)}, u32[]{:S(2)}) collective-permute-start(bf16[2,192,768]{2,1,0:T(8,128)(2,1)} %dynamic-slice_bitcast_fusion.3), channel_id=1, source_target_pairs={{0,8},{8,0},{16,24},{24,16},{1,9},{9,1},{17,25},{25,17},{2,10},{10... | collective-permute-start | bytes 1769480 | tf_op jit(solution)/shard_map/ppermute | solution.py:77
  281.2 30.1 %collective-permute-start.31 = (bf16[2,96,1536]{2,1,0:T(8,128)(2,1)}, bf16[2,96,1536]{2,1,0:T(8,128)(2,1)}, u32[]{:S(2)}, u32[]{:S(2)}) collective-permute-start(bf16[2,96,1536]{2,1,0:T(8,128)(2,1)} %dynamic-slice_bitcast_fusion.4), channel_id=1, source_target_pairs={{0,16},{8,24},{16,0},{24,8},{1,17},{9,25},{17,1},{25,9},{2,18},{10... | collective-permute-start | bytes 1769480 | tf_op jit(solution)/shard_map/ppermute | solution.py:77
  282.1 29.2 %collective-permute-start.30 = (bf16[2,96,1536]{2,1,0:T(8,128)(2,1)}, bf16[2,96,1536]{2,1,0:T(8,128)(2,1)}, u32[]{:S(2)}, u32[]{:S(2)}) collective-permute-start(bf16[2,96,1536]{2,1,0:T(8,128)(2,1)} %dynamic-slice_bitcast_fusion.5), channel_id=1, source_target_pairs={{0,8},{8,0},{16,24},{24,16},{1,9},{9,1},{17,25},{25,17},{2,10},{10... | collective-permute-start | bytes 1769480 | tf_op jit(solution)/shard_map/ppermute | solution.py:77
  345.1 18.8 %collective-permute-start.49 = (bf16[192,768]{1,0:T(8,128)(2,1)}, bf16[192,768]{1,0:T(8,128)(2,1)}, u32[]{:S(2)}, u32[]{:S(2)}) collective-permute-start(bf16[192,768]{1,0:T(8,128)(2,1)} %dynamic-slice_bitcast_fusion.9), channel_id=1, source_target_pairs={{0,16},{8,24},{16,0},{24,8},{1,17},{9,25},{17,1},{25,9},{2,18},{10... | collective-permute-start | bytes 884744 | tf_op jit(solution)/shard_map/ppermute | solution.py:77
  346.2 19.6 %collective-permute-start.50 = (bf16[192,768]{1,0:T(8,128)(2,1)}, bf16[192,768]{1,0:T(8,128)(2,1)S(1)}, u32[]{:S(2)}, u32[]{:S(2)}) collective-permute-start(bf16[192,768]{1,0:T(8,128)(2,1)} %dynamic-slice_bitcast_fusion.8), channel_id=1, source_target_pairs={{0,8},{8,0},{16,24},{24,16},{1,9},{9,1},{17,25},{25,17},{2,10},{10... | collective-permute-start | bytes 884744 | tf_op jit(solution)/shard_map/ppermute | solution.py:77
  349.0 19.3 %collective-permute-start.48 = (bf16[96,1536]{1,0:T(8,128)(2,1)}, bf16[96,1536]{1,0:T(8,128)(2,1)}, u32[]{:S(2)}, u32[]{:S(2)}) collective-permute-start(bf16[96,1536]{1,0:T(8,128)(2,1)} %dynamic-slice_bitcast_fusion.10), channel_id=1, source_target_pairs={{0,8},{8,0},{16,24},{24,16},{1,9},{9,1},{17,25},{25,17},{2,10},{10... | collective-permute-start | bytes 884744 | tf_op jit(solution)/shard_map/ppermute | solution.py:77
  351.6 50.8 %collective-permute-start.43 = (bf16[256,768]{1,0:T(8,128)(2,1)}, bf16[256,768]{1,0:T(8,128)(2,1)}, u32[]{:S(2)}, u32[]{:S(2)}) collective-permute-start(bf16[256,768]{1,0:T(8,128)(2,1)} %get-tuple-element.160), channel_id=1, source_target_pairs={{1,0},{2,1},{3,2},{4,3},{5,4},{6,5},{7,6},{9,8},{10,9},{11,10},{12... | collective-permute-start | bytes 1179656 | tf_op jit(solution)/shard_map/ppermute | solution.py:966
  360.1 42.3 %collective-permute-start.42 = (bf16[256,768]{1,0:T(8,128)(2,1)}, bf16[256,768]{1,0:T(8,128)(2,1)}, u32[]{:S(2)}, u32[]{:S(2)}) collective-permute-start(bf16[256,768]{1,0:T(8,128)(2,1)} %get-tuple-element.159), channel_id=1, source_target_pairs={{0,1},{1,2},{2,3},{3,4},{4,5},{5,6},{6,7},{8,9},{9,10},{10,11},{11... | collective-permute-start | bytes 1179656 | tf_op jit(solution)/shard_map/ppermute | solution.py:969
  371.0 16.1 %collective-permute-start.35 = (bf16[2,2,24,3200]{3,2,1,0:T(8,128)(2,1)S(1)}, bf16[2,2,24,3200]{3,2,1,0:T(8,128)(2,1)S(1)}, u32[]{:S(2)}, u32[]{:S(2)}) collective-permute-start(bf16[2,2,24,3200]{3,2,1,0:T(8,128)(2,1)S(1)} %dynamic-slice_bitcast_fusion.1), channel_id=1, source_target_pairs={{0,8},{8,0},{16,24},{24,16},{1,9},{9,1},{17,25},{25,17},{2,10},{10... | collective-permute-start | bytes 1843208 | tf_op jit(solution)/shard_map/ppermute | solution.py:77
  (108 other events, 662.6 us)
Sparse Core Ops, SparseCore 0:
  10.2 59.7 all-gather.2
  72.2 29.5 all-gather.4
  241.5 81.2 reduce-scatter.1

commit v3 on v2

--- a/solution.py
+++ b/solution.py
@@ -109,7 +109,7 @@
     out = place(None, count, block, me)
     for bits in (1, 2):
         out = place(out, count, across(block, bits), me ^ bits)
-    return out, across(block, 3)
+    return out, across(tie(block, out), 3)
 
 
 def gather_dp_far(out, far):
@@ -130,29 +130,57 @@
     first, second = grid[:, :, :half], grid[:, :, half:]
     first_got = across(lax.dynamic_index_in_dim(first, 1 - one, 1, False), 1)
     second_got = across(lax.dynamic_index_in_dim(second, 1 - two, 0, False), 2)
-    return first, second, first_got, second_got
-
-
-def scatter_dp_middle(state, then=None):
+    return grid, first_got, second_got
+
+
+def scatter_middle_kernel(place_at, first, second, first_got, second_got, *outs):
+    sums = (
+        first[0, 0].astype(F32) + first_got[0].astype(F32),
+        second[0, 0].astype(F32) + second_got[0].astype(F32),
+    )
+
+    def put(number):
+        for way in range(2):
+            outs[2 * number + way][...] = sums[way].astype(BF16)
+
+    pl.when(pl.program_id(0) == 0)(lambda: put(0))
+    pl.when(pl.program_id(0) != 0)(lambda: put(1))
+
+
+def scatter_dp_middle(state):
     one, two = lax.axis_index("dp") % 2, lax.axis_index("dp") // 2
-    first, second, first_got, second_got = state
-    if then is not None:
-        first_got, second_got = tie(first_got, then), tie(second_got, then)
-    first_sum = added(lax.dynamic_index_in_dim(first, one, 1, False), first_got).astype(BF16)
-    second_sum = added(lax.dynamic_index_in_dim(second, two, 0, False), second_got).astype(BF16)
-    first_got = across(lax.dynamic_index_in_dim(first_sum, 1 - two, 0, False), 2)
-    second_got = across(lax.dynamic_index_in_dim(second_sum, 1 - one, 0, False), 1)
-    return first_sum, second_sum, first_got, second_got
+    grid, first_got, second_got = state
+    shape = grid.shape[3:]
+    half = (grid.shape[2] // 2,) + shape
+    zeros = (0,) * len(shape)
+    outs = pl.pallas_call(
+        scatter_middle_kernel,
+        grid_spec=pltpu.PrefetchScalarGridSpec(
+            num_scalar_prefetch=1,
+            grid=(2,),
+            in_specs=[
+                pl.BlockSpec((1, 1) + half, lambda i, p: (p[1] ^ 1 ^ i, p[0], 0) + zeros),
+                pl.BlockSpec((1, 1) + half, lambda i, p: (p[1], p[0] ^ 1 ^ i, 1) + zeros),
+                pl.BlockSpec((1,) + half, lambda i, p: (p[1] ^ 1 ^ i, 0) + zeros),
+                pl.BlockSpec((1,) + half, lambda i, p: (p[0] ^ 1 ^ i, 0) + zeros),
+            ],
+            out_specs=[pl.BlockSpec(half, lambda i, p: (0,) + zeros)] * 4,
+        ),
+        out_shape=[jax.ShapeDtypeStruct(half, BF16)] * 4,
+        compiler_params=pltpu.CompilerParams(vmem_limit_bytes=VMEM_LIMIT),
+        cost_estimate=cheap(
+            flops=2 * first_got.size, bytes_accessed=6 * grid.size, transcendentals=0
+        ),
+        name="scatter_middle",
+    )(jnp.stack([one, two]), grid, grid, first_got, second_got)
+    return outs[2], outs[3], across(outs[0], 2), across(outs[1], 1)
 
 
 def scatter_dp_end(state, then=None):
-    one, two = lax.axis_index("dp") % 2, lax.axis_index("dp") // 2
     first_sum, second_sum, first_got, second_got = state
     if then is not None:
         first_got, second_got = tie(first_got, then), tie(second_got, then)
-    first_sum = added(lax.dynamic_index_in_dim(first_sum, two, 0, False), first_got)
-    second_sum = added(lax.dynamic_index_in_dim(second_sum, one, 0, False), second_got)
-    return jnp.concatenate([first_sum, second_sum], axis=0)
+    return jnp.concatenate([added(first_sum, first_got), added(second_sum, second_got)], axis=0)
 
 
 def gather_expert(block, by_hops):
@@ -376,6 +404,46 @@
         ),
         name="first_norm",
     )(below, tokens, above, vectors)
+
+
+def second_norm_kernel(
+    heads, weight, tokens, vectors, router, routes, resid_out, payload_out, gates_out
+):
+    rows, width = tokens.shape
+    resid = tokens[...].astype(F32) + dot_nn(heads[...], weight[...])
+    resid_out[...] = resid
+    unit, _ = standardised(resid)
+    hidden = (unit * vectors[0:1] + vectors[1:2]).astype(BF16)
+    payload_out[:rows, :] = hidden
+    logits = dot_nt(router[...], hidden)
+    expert = lax.broadcasted_iota(jnp.int32, logits.shape, 0)
+    named = (expert == routes[0:1]) | (expert == routes[1:2])
+    peak = jnp.max(jnp.where(named, logits, -jnp.inf), axis=0, keepdims=True)
+    raised = jnp.where(named, jnp.exp(jnp.where(named, logits - peak, 0.0)), 0.0)
+    gates = raised / jnp.sum(raised, axis=0, keepdims=True)
+    gates_out[...] = gates
+    high = gates.astype(BF16).astype(F32)
+    payload_out[rows:, :rows] = jnp.concatenate([high, gates - high], axis=0).astype(BF16)
+    payload_out[rows:, rows:] = jnp.zeros((EXTRA, width - rows), BF16)
+
+
+def second_norm(heads, weight, tokens, vectors, router, routes):
+    rows, width = tokens.shape
+    return pl.pallas_call(
+        second_norm_kernel,
+        out_shape=[
+            jax.ShapeDtypeStruct((rows, width), F32),
+            jax.ShapeDtypeStruct((rows + EXTRA, width), BF16),
+            jax.ShapeDtypeStruct((8, rows), F32),
+        ],
+        compiler_params=pltpu.CompilerParams(vmem_limit_bytes=VMEM_LIMIT),
+        cost_estimate=cheap(
+            flops=2 * rows * width * width,
+            bytes_accessed=rows * width * 10 + width * width * 2,
+            transcendentals=0,
+        ),
+        name="second_norm",
+    )(heads, weight, tokens, vectors, router, routes)
 
 
 def dense_back_kernel(
@@ -627,35 +695,19 @@
     )
 
 
-def split_float(values, terms):
-    parts = []
-    for _ in range(terms):
-        part = lax.reduce_precision(values, 8, 7)
-        parts.append(part.astype(BF16))
-        values = values - part
-    return parts
-
-
-def experts_by_ring(hidden_two, gates, weights, next_grads, grads_mine):
+def experts_by_ring(payload, expert_count, weights, next_grads, grads_mine):
     chips = lax.axis_size("expert") // 2
-    expert_count, rows = gates.shape
-    width = hidden_two.shape[1]
+    rows = payload.shape[0] - EXTRA
     chip, core = lax.axis_index("expert") // 2, lax.axis_index("expert") % 2
     number = jnp.arange(EXTRA, dtype=jnp.int32)[:, None]
-    gate_mark = jnp.broadcast_to(
-        (number % expert_count == chip) & (number < 3 * expert_count), (EXTRA, LANES)
-    ).astype(BF16)
+    gate_mark = jnp.broadcast_to(number % 8 == chip, (EXTRA, LANES)).astype(BF16)
     slot = 2 * (core * expert_count + chip)
     dot_mark = jnp.stack([number == slot, number == slot + 1]).astype(F32)
     marks = (gate_mark, dot_mark)
-    carried = jnp.pad(
-        jnp.concatenate(split_float(gates, 3), axis=0),
-        ((0, EXTRA - 3 * expert_count), (0, width - rows)),
-    )
     kept = None
     carry = None
     backs = []
-    mine = jnp.concatenate([hidden_two, carried], axis=0)
+    mine = payload
     for step in range(chips):
         other = pair(mine)
         if step + 1 < chips:
@@ -845,28 +897,32 @@
     starts = jnp.minimum(starts // 16 * 16, rows_dev + 2 * HALO - KEY_WINDOW)
     heads_low = attention(triple, starts, query_image, key_image)
     if by_ring:
-        expert_weights = gather_dp_far(experts_near, experts_far)
+        expert_weights = gather_dp_far(experts_near, tie(experts_far, heads_low))
     tokens_float = tokens.astype(F32)
-    resid = tokens_float + dot_nn(heads_low, proj_weight)
-    unit_two, inverse_two = standardised(resid)
-    hidden_two = (unit_two * norm_float[2] + norm_float[3]).astype(BF16)
-
     if by_ring:
-        hidden_two = tie(hidden_two, grads_mine[-1])
-    next_grads(hidden_two)
-
-    logits = lax.dot_general(
-        router_low, hidden_two, (((1,), (1,)), ((), ())), preferred_element_type=F32
-    )
-    experts = jnp.arange(expert_count, dtype=jnp.int32)[:, None]
-    named = (routes[:, 0][None, :] == experts) | (routes[:, 1][None, :] == experts)
-    peak = jnp.max(jnp.where(named, logits, -jnp.inf), axis=0, keepdims=True)
-    raised = jnp.where(named, jnp.exp(jnp.where(named, logits - peak, 0.0)), 0.0)
-    gates = raised / jnp.sum(raised, axis=0, keepdims=True)
+        router_rows = jnp.pad(router_low, ((0, 8 - expert_count), (0, 0)))
+        resid, payload, gates = second_norm(
+            heads_low, proj_weight, tokens, tie(norm_float[2:], expert_weights), router_rows, routes.T
+        )
+        gates = gates[:expert_count]
+        payload = tie(payload, grads_mine[-1])
+        next_grads(payload)
+        hidden_two = payload[:rows_dev]
+        unit_two, inverse_two = standardised(resid)
+    else:
+        resid = tokens_float + dot_nn(heads_low, proj_weight)
+        unit_two, inverse_two = standardised(resid)
+        hidden_two = (unit_two * norm_float[2] + norm_float[3]).astype(BF16)
+        logits = dot_nt(router_low, hidden_two)
+        experts = jnp.arange(expert_count, dtype=jnp.int32)[:, None]
+        named = (routes[:, 0][None, :] == experts) | (routes[:, 1][None, :] == experts)
+        peak = jnp.max(jnp.where(named, logits, -jnp.inf), axis=0, keepdims=True)
+        raised = jnp.where(named, jnp.exp(jnp.where(named, logits - peak, 0.0)), 0.0)
+        gates = raised / jnp.sum(raised, axis=0, keepdims=True)
 
     if by_ring:
         out, grad_gates, grad_hidden, grad_widen, grad_narrow = experts_by_ring(
-            hidden_two, gates, expert_weights, next_grads, grads_mine
+            payload, expert_count, expert_weights, next_grads, grads_mine
         )
     else:
         out, grad_gates, grad_hidden, grad_widen, grad_narrow = experts_by_slots(
@@ -903,7 +959,10 @@
 
     grad_triple = attention_back(triple, grad_heads, starts, query_image, key_image)
     if by_ring:
-        scattered = [scatter_dp_middle(state, grad_triple) for state in scattered]
+        scattered = [
+            scatter_dp_middle((grid, tie(first, grad_triple), tie(second, grad_triple)))
+            for grid, first, second in scattered
+        ]
         grad_triple = tie(grad_triple, *(part for state in scattered for part in state[:2]))
     by_owner = (2, replicas, expert_count, width // (device_count * replicas))
     small_rows = jnp.concatenate(
@@ -929,11 +988,12 @@
         )
         out = lax.psum_scatter(out, "expert", scatter_dimension=0, tiled=True)
         over_pair = added(grad_keep, pair(tie(grad_give, out))).astype(BF16)
-        over_dp = scatter_dp_end(scatter_dp_middle(scatter_dp_start(over_pair)))
+        halfway = scatter_dp_middle(scatter_dp_start(over_pair))
+        over_dp = scatter_dp_end(halfway)
         over_dp = over_dp.astype(BF16)
         owned = sum_over_chips(over_dp)
         dense_sum = spread_over_dp(owned)
-        widen_sum, narrow_sum = [scatter_dp_end(state, over_pair) for state in scattered]
+        widen_sum, narrow_sum = [scatter_dp_end(state, halfway[0]) for state in scattered]
         out = tie(out, owned)
         attention_sum = dense_sum[:, : 4 * width]
         small_sum = dense_sum[:, 4 * width :]

time: 443 us -> 439 us (level)
  the two profiles are of different devices: /device:TPU:8 before, /device:TPU:0 now
where the time goes in v3:
time: 439 us; the launch traced here: 431 us
  Pallas kernels  167 us (38%)
  waiting for transfers between devices  68.5 us (16%)
  starting transfers between devices  52.8 us (12%)
  other arithmetic  46.9 us (11%)
  local copies, waits for them, and re-layouts  40.1 us (9%)
  matrix products  40.1 us (9%)
  between operations  15.4 us (4%)
    pallas_call x8, Pallas kernels, expert_block(): pl.pallas_call(functools.partial(expert_kernel, first), grid_spec=pltpu.P...  83.5 us
    ppermute x15, waiting for transfers between devices, hop(): lax.ppermute(block, 'expert', [(i, (i + distance) % count) for i in range...  45.8 us
    dot_general x2, matrix products, dot_tn(): lax.dot_general(left, right, (((0,), (0,)), ((), ())), preferred_element_...  28.9 us
    unnamed x143, local copies, waits for them, and re-layouts  25.5 us
    ppermute x18, starting transfers between devices, across(): lax.ppermute(block, 'dp', [(i, i ^ bit) for i in range(lax.axis_size('dp'...  23.6 us
    pallas_call x1, Pallas kernels, attention_back(): pl.pallas_call(attend_back_kernel, grid_spec=pltpu.PrefetchScalarGridSpec...  19.9 us
    pallas_call x1, Pallas kernels, dense_back(): pl.pallas_call(functools.partial(dense_back_kernel, layout), out_shape=[j...  19.5 us
    ppermute x15, starting transfers between devices, hop(): lax.ppermute(block, 'expert', [(i, (i + distance) % count) for i in range...  18.6 us
  transfers between devices with their start and end apart: 54, of which 13 were waited for; matrix products, arithmetic and copies ran while one was open for 21% of the time, Pallas kernels for 38%

profile of v3, /device:TPU:0, one launch (start us, length us, event | category | flops | bytes accessed | tf_op | source)
XLA Modules:
  0.0 430.5 jit_solution(7878441463931666863)
XLA Ops:
  11.8 3.0 collective-permute-start.2
  18.7 3.6 collective-permute-start.5
  30.8 5.2 %collective-permute-start.9 = (bf16[512,768]{1,0:T(8,128)(2,1)}, bf16[512,768]{1,0:T(8,128)(2,1)S(1)}, u32[]{:S(2)}, u32[]{:S(2)}) collective-permute-start(bf16[512,768]{1,0:T(8,128)(2,1)} %tie.31.grads_ref), channel_id=1, source_target_pairs={{0,2},{1,3},{2,4},{3,5},{4,6},{5,7},{6,0},{7,1},{8,10},{9,11},{10,... | collective-permute-start | bytes 2359304 | tf_op jit(solution)/shard_map/ppermute | solution.py:65
  53.3 3.6 first_norm.1.refs_1_.hidden
  56.9 18.0 %collective-permute-done.9.refs_0_ = bf16[512,768]{1,0:T(8,128)(2,1)S(1)} collective-permute-done((bf16[512,768]{1,0:T(8,128)(2,1)}, bf16[512,768]{1,0:T(8,128)(2,1)S(1)}, u32[]{:S(2)}, u32[]{:S(2)}) %collective-permute-start.9) | collective-permute-done | bytes 786464 | tf_op jit(solution)/shard_map/ppermute | solution.py:65
  75.8 7.4 %convolution_convert_fusion.q_ref.k_ref.v_ref = bf16[1024,2304]{1,0:T(8,128)(2,1)} fusion(bf16[1024,768]{1,0:T(8,128)(2,1)S(1)} %copy-done.11, bf16[768,2304]{1,0:T(8,128)(2,1)} %all-gather.3.cloned.1.call-done.refs_2_.weight), kind=kOutput, calls=%fused_computation | convolution fusion | flops 3626237952 | bytes 9830400 | tf_op jit(solution)/shard_map/dot_general | solution.py:261
  83.3 14.8 %attention.1.refs_1_.heads = bf16[512,768]{1,0:T(8,128)(2,1)} custom-call(s32[4]{0:T(128)} %multiply_minimum_fusion.starts, s32[1,512]{1,0:T(1,128)} %and_select_fusion.query_image, s32[1024,1]{1,0:T(8,128)} %fusion.15.key_image, bf16[1024,2304]{1,0:T(8,128)(2,1)} %convolution_convert_fusion.q_ref.k_ref.v_ref, ...), custom_call_target="tpu_custom_call" | custom-call | flops 163577856 | bytes 589824 | tf_op jit(solution)/shard_map/attention/pallas_call | solution.py:314
  101.2 2.9 all-gather.5.cloned.1.call-done.weight
  104.2 4.3 %second_norm.1 = (f32[512,768]{1,0:T(8,128)}, bf16[528,768]{1,0:T(8,128)(2,1)}, f32[8,512]{1,0:T(8,128)}) custom-call(bf16[512,768]{1,0:T(8,128)(2,1)} %attention.1.refs_1_.heads, bf16[768,768]{1,0:T(8,128)(2,1)} %all-gather.5.cloned.1.call-done.weight, bf16[512,768]{1,0:T(8,128)(2,1)} %tokens.5, f32[2,768]{1,0:T(2,128)} %tie.30.vectors, ...), custom_call_target="tpu_custom_call" | custom-call | flops 75497472 | bytes 638976 | tf_op jit(solution)/shard_map/second_norm/pallas_call | solution.py:432
  113.0 10.4 %expert_block.8 = (bf16[4096,1536]{1,0:T(8,128)(2,1)}, bf16[4096,1536]{1,0:T(8,128)(2,1)}, bf16[4096,768]{1,0:T(8,128)(2,1)}, bf16[4096,768]{1,0:T(8,128)(2,1)},...) custom-call(s32[1]{0:T(128)} %bitcast.15.target, bf16[528,768]{1,0:T(8,128)(2,1)} %tie.33.rows_ref.gates.refs_1_, ...), custom_call_target="tpu_custom_call" | custom-call | flops 603979776 | bytes 1572864 | tf_op jit(solution)/shard_map/expert_block/pallas_call | solution.py:645
  124.3 10.4 %expert_block.9 = (bf16[4096,1536]{1,0:T(8,128)(2,1)}, bf16[4096,1536]{1,0:T(8,128)(2,1)}, bf16[4096,768]{1,0:T(8,128)(2,1)}, bf16[4096,768]{1,0:T(8,128)(2,1)},...) custom-call(s32[1]{0:T(128)} %bitcast.12.target, ...), custom_call_target="tpu_custom_call", output_to_operand_aliasing={{0}: (7, {}), {1}: (8, {}), {2}: (9, {}), {3}: (10, {}), {4... | custom-call | flops 603979776 | bytes 1572864 | tf_op jit(solution)/shard_map/expert_block/pallas_call | solution.py:645
  134.7 14.6 %collective-permute-done.14.refs_4_.refs_3_.refs_2_.grads_ref = bf16[512,768]{1,0:T(8,128)(2,1)S(1)} collective-permute-done((bf16[512,768]{1,0:T(8,128)(2,1)}, bf16[512,768]{1,0:T(8,128)(2,1)S(1)}, u32[]{:S(2)}, u32[]{:S(2)}) %collective-permute-start.14) | collective-permute-done | bytes 786464 | tf_op jit(solution)/shard_map/ppermute | solution.py:65
  151.8 10.4 %expert_block.10 = (bf16[4096,1536]{1,0:T(8,128)(2,1)}, bf16[4096,1536]{1,0:T(8,128)(2,1)}, bf16[4096,768]{1,0:T(8,128)(2,1)}, bf16[4096,768]{1,0:T(8,128)(2,1)}...) custom-call(s32[1]{0:T(128)} %bitcast.17.target, ...), custom_call_target="tpu_custom_call", output_to_operand_aliasing={{0}: (7, {}), {1}: (8, {}), {2}: (9, {}), {3}: (10, {}), {4... | custom-call | flops 603979776 | bytes 1572864 | tf_op jit(solution)/shard_map/expert_block/pallas_call | solution.py:645
  163.4 10.4 %expert_block.11 = (bf16[4096,1536]{1,0:T(8,128)(2,1)}, bf16[4096,1536]{1,0:T(8,128)(2,1)}, bf16[4096,768]{1,0:T(8,128)(2,1)}, bf16[4096,768]{1,0:T(8,128)(2,1)}...) custom-call(s32[1]{0:T(128)} %bitcast.16.target, ...), custom_call_target="tpu_custom_call", output_to_operand_aliasing={{0}: (7, {}), {1}: (8, {}), {2}: (9, {}), {3}: (10, {}), {4... | custom-call | flops 603979776 | bytes 1572864 | tf_op jit(solution)/shard_map/expert_block/pallas_call | solution.py:645
  175.8 10.5 %expert_block.12 = (bf16[4096,1536]{1,0:T(8,128)(2,1)}, bf16[4096,1536]{1,0:T(8,128)(2,1)}, bf16[4096,768]{1,0:T(8,128)(2,1)}, bf16[4096,768]{1,0:T(8,128)(2,1)}...) custom-call(s32[1]{0:T(128)} %bitcast.19.target, ...), custom_call_target="tpu_custom_call", output_to_operand_aliasing={{0}: (7, {}), {1}: (8, {}), {2}: (9, {}), {3}: (10, {}), {4... | custom-call | flops 603979776 | bytes 1572864 | tf_op jit(solution)/shard_map/expert_block/pallas_call | solution.py:645
  190.2 10.4 %expert_block.13 = (bf16[4096,1536]{1,0:T(8,128)(2,1)}, bf16[4096,1536]{1,0:T(8,128)(2,1)}, bf16[4096,768]{1,0:T(8,128)(2,1)}, bf16[4096,768]{1,0:T(8,128)(2,1)}...) custom-call(s32[1]{0:T(128)} %bitcast.18.target, ...), custom_call_target="tpu_custom_call", output_to_operand_aliasing={{0}: (7, {}), {1}: (8, {}), {2}: (9, {}), {3}: (10, {}), {4... | custom-call | flops 603979776 | bytes 1572864 | tf_op jit(solution)/shard_map/expert_block/pallas_call | solution.py:645
  202.1 10.5 %expert_block.14 = (bf16[4096,1536]{1,0:T(8,128)(2,1)}, bf16[4096,1536]{1,0:T(8,128)(2,1)}, bf16[4096,768]{1,0:T(8,128)(2,1)}, bf16[4096,768]{1,0:T(8,128)(2,1)}...) custom-call(s32[1]{0:T(128)} %bitcast.20.target, ...), custom_call_target="tpu_custom_call", output_to_operand_aliasing={{0}: (7, {}), {1}: (8, {}), {2}: (9, {}), {3}: (10, {}), {4... | custom-call | flops 603979776 | bytes 1572864 | tf_op jit(solution)/shard_map/expert_block/pallas_call | solution.py:645
  212.6 2.7 collective-permute-done.26
  220.1 10.5 %expert_block.15 = (bf16[4096,1536]{1,0:T(8,128)(2,1)}, bf16[4096,1536]{1,0:T(8,128)(2,1)}, bf16[4096,768]{1,0:T(8,128)(2,1)}, bf16[4096,768]{1,0:T(8,128)(2,1)}...) custom-call(s32[1]{0:T(128)} %bitcast.11.target, ...), custom_call_target="tpu_custom_call", output_to_operand_aliasing={{0}: (7, {}), {1}: (8, {}), {2}: (9, {}), {3}: (10, {}), {4... | custom-call | flops 603979776 | bytes 1572864 | tf_op jit(solution)/shard_map/expert_block/pallas_call | solution.py:645
  230.8 8.2 %collective-permute-done.27 = bf16[528,768]{1,0:T(8,128)(2,1)S(1)} collective-permute-done((bf16[528,768]{1,0:T(8,128)(2,1)}, bf16[528,768]{1,0:T(8,128)(2,1)S(1)}, u32[]{:S(2)}, u32[]{:S(2)}) %collective-permute-start.27) | collective-permute-done | bytes 811040 | tf_op jit(solution)/shard_map/ppermute | solution.py:65
  243.8 15.4 %convolution_convert_fusion.1.refs_2_ = bf16[1536,768]{1,0:T(8,128)(2,1)S(1)} fusion(bf16[4096,1536]{1,0:T(8,128)(2,1)} %tie.40, bf16[4096,768]{1,0:T(8,128)(2,1)} %get-tuple-element.138), kind=kOutput, calls=%fused_computation.2 | convolution fusion | flops 9664856064 | bytes 21233664 | tf_op jit(solution)/shard_map/dot_general | solution.py:257
  265.2 13.5 %convolution_convert_fusion.2.refs_1_ = bf16[768,1536]{1,0:T(8,128)(2,1)S(1)} fusion(bf16[4096,768]{1,0:T(8,128)(2,1)S(1)} %copy-done, bf16[4096,1536]{1,0:T(8,128)(2,1)} %get-tuple-element.136), kind=kOutput, calls=%fused_computation.3 | convolution fusion | flops 9664856064 | bytes 21233664 | tf_op jit(solution)/shard_map/dot_general | solution.py:257
  290.2 19.9 %attention_back.1.refs_1_.refs_0_ = bf16[1024,2304]{1,0:T(8,128)(2,1)} custom-call(s32[4]{0:T(128)} %multiply_minimum_fusion.starts, s32[1,512]{1,0:T(1,128)} %and_select_fusion.query_image, s32[1024,1]{1,0:T(8,128)} %fusion.15.key_image, bf16[1024,2304]{1,0:T(8,128)(2,1)} %convolution_convert_fusion.q_ref.k_ref.v_ref, ...), custom_call_target="tpu_custom_call" | custom-call | flops 408944640 | bytes 1376256 | tf_op jit(solution)/shard_map/attention_back/pallas_call | solution.py:369
  310.2 3.6 scatter_middle.4
  313.8 3.5 scatter_middle.3
  319.6 19.5 %dense_back.1 = (bf16[4,4,24,3200]{3,2,1,0:T(8,128)(2,1)}, bf16[4,4,24,3200]{3,2,1,0:T(8,128)(2,1)}, bf16[1024,768]{1,0:T(8,128)(2,1)}) custom-call(s32[1]{0:T(128)} %bitcast.23.me, bf16[1024,768]{1,0:T(8,128)(2,1)} %first_norm.1.refs_1_.hidden, bf16[256,768]{1,0:T(8,128)(2,1)} %tie.27.below, bf16[512,768]{1,0:T(8,128)(2,1)} %tokens.5, ...), custom_call_target="tpu_custom_call" | custom-call | flops 905969664 | bytes 2457600 | tf_op jit(solution)/shard_map/dense_back/pallas_call | solution.py:522
  340.4 3.6 collective-permute-done.34
  357.5 8.1 %collective-permute-done.36.second_got = bf16[2,2,24,3200]{3,2,1,0:T(8,128)(2,1)} collective-permute-done((bf16[2,2,24,3200]{3,2,1,0:T(8,128)(2,1)}, bf16[2,2,24,3200]{3,2,1,0:T(8,128)(2,1)}, u32[]{:S(2)}, u32[]{:S(2)}) %collective-permute-start.36) | collective-permute-done | bytes 614432 | tf_op jit(solution)/shard_map/ppermute | solution.py:77
  369.3 3.6 scatter_middle.5
  372.9 3.8 collective-permute-start.42
  386.3 4.6 %multiply_subtract_fusion.1 = (f32[1,192,1536]{2,1,0:T(8,128)}, f32[1,192,1536]{2,1,0:T(8,128)}, f32[1,192,1536]{2,1,0:T(8,128)}) fusion(f32[1,192,1536]{2,1,0:T(8,128)} %param.30, f32[1,96,1536]{2,1,0:T(8,128)S(1)} %add_bitcast_fusion.2, f32[1,96,1536]{2,1,0:T(8,128)} %add_bitcast_fusion.3, f32[1,192,1536]{2,1,0:T(8,128)S(1)} %copy-done.50, ...), kind=kLoop, calls=%fused_computation.41 | loop fusion | flops 4718592 | bytes 8257536 | tf_op jit(solution)/shard_map/sub | solution.py:248
  402.9 2.8 fusion.7
  (369 shorter events, 141.2 us)
Async XLA Ops:
  7.2 67.8 %all-gather.3.cloned.1.call-start = ((), (), s32[]{:S(2)}) async-start(), calls=%async_computation.1 | async-start | bytes 3981312 | tf_op jit(solution)/shard_map/all_gather | solution.py:852
  10.3 93.9 %all-gather.5.cloned.1.call-start = ((), (), s32[]{:S(2)}) async-start(), calls=%async_computation.2 | async-start | bytes 1327104 | tf_op jit(solution)/shard_map/all_gather | solution.py:854
  11.8 29.1 %collective-permute-start.2 = (bf16[768,768]{1,0:T(8,128)(2,1)S(1)}, bf16[768,768]{1,0:T(8,128)(2,1)}, u32[]{:S(2)}, u32[]{:S(2)}) collective-permute-start(bf16[768,768]{1,0:T(8,128)(2,1)S(1)} %pad_maximum_fusion.block.refs_0_), channel_id=1, source_target_pairs={{0,8},{8,0},{16,24},{24,16},{1,9},{9,1},{17,25},{25,17},{2,10},{10... | collective-permute-start | bytes 3538952 | tf_op jit(solution)/shard_map/ppermute | solution.py:77
  14.8 28.3 %collective-permute-start.1 = (bf16[768,768]{1,0:T(8,128)(2,1)S(1)}, bf16[768,768]{1,0:T(8,128)(2,1)}, u32[]{:S(2)}, u32[]{:S(2)}) collective-permute-start(bf16[768,768]{1,0:T(8,128)(2,1)S(1)} %pad_maximum_fusion.block.refs_0_), channel_id=1, source_target_pairs={{0,16},{8,24},{16,0},{24,8},{1,17},{9,25},{17,1},{25,9},{2,18},{10... | collective-permute-start | bytes 3538952 | tf_op jit(solution)/shard_map/ppermute | solution.py:77
  18.0 321.1 %reduce-scatter.2.cloned.1.call-start = ((), (), s32[]{:S(2)}) async-start(), calls=%async_computation.3 | async-start | bytes 7077888 | tf_op jit(solution)/shard_map/reduce_scatter | solution.py:989
  26.5 25.3 %collective-permute-start = (bf16[256,768]{1,0:T(8,128)(2,1)S(1)}, bf16[256,768]{1,0:T(8,128)(2,1)S(1)}, u32[]{:S(2)}, u32[]{:S(2)}) collective-permute-start(bf16[256,768]{1,0:T(8,128)(2,1)S(1)} %get-tuple-element.189), channel_id=1, source_target_pairs={{0,1},{1,2},{2,3},{3,4},{4,5},{5,6},{6,7},{8,9},{9,10},{10,11},{11... | collective-permute-start | bytes 1179656 | tf_op jit(solution)/shard_map/ppermute | solution.py:878
  28.1 24.5 %collective-permute-start.3 = (bf16[256,768]{1,0:T(8,128)(2,1)S(1)}, bf16[256,768]{1,0:T(8,128)(2,1)S(1)}, u32[]{:S(2)}, u32[]{:S(2)}) collective-permute-start(bf16[256,768]{1,0:T(8,128)(2,1)S(1)} %get-tuple-element.188), channel_id=1, source_target_pairs={{1,0},{2,1},{3,2},{4,3},{5,4},{6,5},{7,6},{9,8},{10,9},{11,10},{12... | collective-permute-start | bytes 1179656 | tf_op jit(solution)/shard_map/ppermute | solution.py:881
  30.8 44.1 %collective-permute-start.9 = (bf16[512,768]{1,0:T(8,128)(2,1)}, bf16[512,768]{1,0:T(8,128)(2,1)S(1)}, u32[]{:S(2)}, u32[]{:S(2)}) collective-permute-start(bf16[512,768]{1,0:T(8,128)(2,1)} %tie.31.grads_ref), channel_id=1, source_target_pairs={{0,2},{1,3},{2,4},{3,5},{4,6},{5,7},{6,0},{7,1},{8,10},{9,11},{10,... | collective-permute-start | bytes 2359304 | tf_op jit(solution)/shard_map/ppermute | solution.py:65
  45.2 52.9 %collective-permute-start.8 = (bf16[768,768]{1,0:T(8,128)(2,1)}, bf16[768,768]{1,0:T(8,128)(2,1)S(1)}, u32[]{:S(2)}, u32[]{:S(2)}) collective-permute-start(bf16[768,768]{1,0:T(8,128)(2,1)} %tie.28), channel_id=1, source_target_pairs={{0,24},{8,16},{16,8},{24,0},{1,25},{9,17},{17,9},{25,1},{2,26},{10... | collective-permute-start | bytes 3538952 | tf_op jit(solution)/shard_map/ppermute | solution.py:77
  75.8 32.7 %collective-permute-start.10 = (bf16[512,768]{1,0:T(8,128)(2,1)}, bf16[512,768]{1,0:T(8,128)(2,1)S(1)}, u32[]{:S(2)}, u32[]{:S(2)}) collective-permute-start(bf16[512,768]{1,0:T(8,128)(2,1)} %tie.32.refs_2_.grads_ref), channel_id=1, source_target_pairs={{0,2},{1,3},{2,4},{3,5},{4,6},{5,7},{6,0},{7,1},{8,10},{9,11},{10,... | collective-permute-start | bytes 2359304 | tf_op jit(solution)/shard_map/ppermute | solution.py:65
  110.1 39.1 %collective-permute-start.11 = (bf16[528,768]{1,0:T(8,128)(2,1)}, bf16[528,768]{1,0:T(8,128)(2,1)S(1)}, u32[]{:S(2)}, u32[]{:S(2)}) collective-permute-start(bf16[528,768]{1,0:T(8,128)(2,1)} %tie.33.rows_ref.gates.refs_1_), channel_id=1, source_target_pairs={{0,2},{1,3},{2,4},{3,5},{4,6},{5,7},{6,0},{7,1},{8,10},{9,11},{10,... | collective-permute-start | bytes 2433032 | tf_op jit(solution)/shard_map/ppermute | solution.py:65
  110.2 39.0 %collective-permute-start.14 = (bf16[512,768]{1,0:T(8,128)(2,1)}, bf16[512,768]{1,0:T(8,128)(2,1)S(1)}, u32[]{:S(2)}, u32[]{:S(2)}) collective-permute-start(bf16[512,768]{1,0:T(8,128)(2,1)} %tie.34.refs_3_.refs_2_.grads_ref), channel_id=1, source_target_pairs={{0,2},{1,3},{2,4},{3,5},{4,6},{5,7},{6,0},{7,1},{8,10},{9,11},{10,... | collective-permute-start | bytes 2359304 | tf_op jit(solution)/shard_map/ppermute | solution.py:65
  151.5 22.8 %collective-permute-start.15 = (bf16[528,768]{1,0:T(8,128)(2,1)}, bf16[528,768]{1,0:T(8,128)(2,1)S(1)}, u32[]{:S(2)}, u32[]{:S(2)}) collective-permute-start(bf16[528,768]{1,0:T(8,128)(2,1)} %tie.35.rows_ref.gates), channel_id=1, source_target_pairs={{0,2},{1,3},{2,4},{3,5},{4,6},{5,7},{6,0},{7,1},{8,10},{9,11},{10,... | collective-permute-start | bytes 2433032 | tf_op jit(solution)/shard_map/ppermute | solution.py:65
  175.8 24.9 %collective-permute-start.18 = (bf16[528,768]{1,0:T(8,128)(2,1)}, bf16[528,768]{1,0:T(8,128)(2,1)S(1)}, u32[]{:S(2)}, u32[]{:S(2)}) collective-permute-start(bf16[528,768]{1,0:T(8,128)(2,1)} %tie.36.rows_ref.gates), channel_id=1, source_target_pairs={{0,2},{1,3},{2,4},{3,5},{4,6},{5,7},{6,0},{7,1},{8,10},{9,11},{10,... | collective-permute-start | bytes 2433032 | tf_op jit(solution)/shard_map/ppermute | solution.py:65
  188.5 26.8 %collective-permute-start.26 = (bf16[528,768]{1,0:T(8,128)(2,1)}, bf16[528,768]{1,0:T(8,128)(2,1)S(1)}, u32[]{:S(2)}, u32[]{:S(2)}) collective-permute-start(bf16[528,768]{1,0:T(8,128)(2,1)} %add_convert_fusion.3), channel_id=1, source_target_pairs={{0,2},{1,3},{2,4},{3,5},{4,6},{5,7},{6,0},{7,1},{8,10},{9,11},{10,... | collective-permute-start | bytes 2433032 | tf_op jit(solution)/shard_map/ppermute | solution.py:65
  201.6 17.6 %collective-permute-start.21 = (bf16[528,768]{1,0:T(8,128)(2,1)}, bf16[528,768]{1,0:T(8,128)(2,1)S(1)}, u32[]{:S(2)}, u32[]{:S(2)}) collective-permute-start(bf16[528,768]{1,0:T(8,128)(2,1)} %tie.37.rows_ref.gates), channel_id=1, source_target_pairs={{0,1},{1,0},{2,3},{3,2},{4,5},{5,4},{6,7},{7,6},{8,9},{9,8},{10,11... | collective-permute-start | bytes 2433032 | tf_op jit(solution)/shard_map/ppermute | solution.py:73
  202.1 17.1 %collective-permute-start.22 = (bf16[512,768]{1,0:T(8,128)(2,1)S(1)}, bf16[512,768]{1,0:T(8,128)(2,1)}, u32[]{:S(2)}, u32[]{:S(2)}) collective-permute-start(bf16[512,768]{1,0:T(8,128)(2,1)S(1)} %copy-done.14), channel_id=1, source_target_pairs={{0,1},{1,0},{2,3},{3,2},{4,5},{5,4},{6,7},{7,6},{8,9},{9,8},{10,11... | collective-permute-start | bytes 2359304 | tf_op jit(solution)/shard_map/ppermute | solution.py:73
  217.7 21.4 %collective-permute-start.27 = (bf16[528,768]{1,0:T(8,128)(2,1)}, bf16[528,768]{1,0:T(8,128)(2,1)S(1)}, u32[]{:S(2)}, u32[]{:S(2)}) collective-permute-start(bf16[528,768]{1,0:T(8,128)(2,1)} %add_convert_fusion.2), channel_id=1, source_target_pairs={{0,2},{1,3},{2,4},{3,5},{4,6},{5,7},{6,0},{7,1},{8,10},{9,11},{10,... | collective-permute-start | bytes 2433032 | tf_op jit(solution)/shard_map/ppermute | solution.py:65
  242.2 41.2 %collective-permute-start.28 = (bf16[528,768]{1,0:T(8,128)(2,1)}, bf16[528,768]{1,0:T(8,128)(2,1)}, u32[]{:S(2)}, u32[]{:S(2)}) collective-permute-start(bf16[528,768]{1,0:T(8,128)(2,1)} %get-tuple-element.96.refs_1_), channel_id=1, source_target_pairs={{0,1},{1,0},{2,3},{3,2},{4,5},{5,4},{6,7},{7,6},{8,9},{9,8},{10,11... | collective-permute-start | bytes 2433032 | tf_op jit(solution)/shard_map/ppermute | solution.py:73
  242.9 39.6 %collective-permute-start.29 = (bf16[528,768]{1,0:T(8,128)(2,1)S(1)}, bf16[528,768]{1,0:T(8,128)(2,1)S(1)}, u32[]{:S(2)}, u32[]{:S(2)}) collective-permute-start(bf16[528,768]{1,0:T(8,128)(2,1)S(1)} %copy-done.12), channel_id=1, source_target_pairs={{0,2},{1,3},{2,4},{3,5},{4,6},{5,7},{6,0},{7,1},{8,10},{9,11},{10,... | collective-permute-start | bytes 2433032 | tf_op jit(solution)/shard_map/ppermute | solution.py:65
  261.4 48.7 %collective-permute-start.33 = (bf16[2,192,768]{2,1,0:T(8,128)(2,1)}, bf16[2,192,768]{2,1,0:T(8,128)(2,1)}, u32[]{:S(2)}, u32[]{:S(2)}) collective-permute-start(bf16[2,192,768]{2,1,0:T(8,128)(2,1)} %dynamic-slice_bitcast_fusion.2), channel_id=1, source_target_pairs={{0,16},{8,24},{16,0},{24,8},{1,17},{9,25},{17,1},{25,9},{2,18},{10... | collective-permute-start | bytes 1769480 | tf_op jit(solution)/shard_map/ppermute | solution.py:77
  263.8 46.4 %collective-permute-start.32 = (bf16[2,192,768]{2,1,0:T(8,128)(2,1)}, bf16[2,192,768]{2,1,0:T(8,128)(2,1)}, u32[]{:S(2)}, u32[]{:S(2)}) collective-permute-start(bf16[2,192,768]{2,1,0:T(8,128)(2,1)} %dynamic-slice_bitcast_fusion.3), channel_id=1, source_target_pairs={{0,8},{8,0},{16,24},{24,16},{1,9},{9,1},{17,25},{25,17},{2,10},{10... | collective-permute-start | bytes 1769480 | tf_op jit(solution)/shard_map/ppermute | solution.py:77
  281.0 29.1 %collective-permute-start.31 = (bf16[2,96,1536]{2,1,0:T(8,128)(2,1)}, bf16[2,96,1536]{2,1,0:T(8,128)(2,1)}, u32[]{:S(2)}, u32[]{:S(2)}) collective-permute-start(bf16[2,96,1536]{2,1,0:T(8,128)(2,1)} %dynamic-slice_bitcast_fusion.4), channel_id=1, source_target_pairs={{0,16},{8,24},{16,0},{24,8},{1,17},{9,25},{17,1},{25,9},{2,18},{10... | collective-permute-start | bytes 1769480 | tf_op jit(solution)/shard_map/ppermute | solution.py:77
  282.5 27.7 %collective-permute-start.30 = (bf16[2,96,1536]{2,1,0:T(8,128)(2,1)}, bf16[2,96,1536]{2,1,0:T(8,128)(2,1)}, u32[]{:S(2)}, u32[]{:S(2)}) collective-permute-start(bf16[2,96,1536]{2,1,0:T(8,128)(2,1)} %dynamic-slice_bitcast_fusion.5), channel_id=1, source_target_pairs={{0,8},{8,0},{16,24},{24,16},{1,9},{9,1},{17,25},{25,17},{2,10},{10... | collective-permute-start | bytes 1769480 | tf_op jit(solution)/shard_map/ppermute | solution.py:77
  348.7 17.0 %collective-permute-start.36 = (bf16[2,2,24,3200]{3,2,1,0:T(8,128)(2,1)}, bf16[2,2,24,3200]{3,2,1,0:T(8,128)(2,1)}, u32[]{:S(2)}, u32[]{:S(2)}) collective-permute-start(bf16[2,2,24,3200]{3,2,1,0:T(8,128)(2,1)} %dynamic-slice_bitcast_fusion), channel_id=1, source_target_pairs={{0,16},{8,24},{16,0},{24,8},{1,17},{9,25},{17,1},{25,9},{2,18},{10... | collective-permute-start | bytes 1843208 | tf_op jit(solution)/shard_map/ppermute | solution.py:77
  350.9 17.1 %collective-permute-start.35 = (bf16[2,2,24,3200]{3,2,1,0:T(8,128)(2,1)}, bf16[2,2,24,3200]{3,2,1,0:T(8,128)(2,1)}, u32[]{:S(2)}, u32[]{:S(2)}) collective-permute-start(bf16[2,2,24,3200]{3,2,1,0:T(8,128)(2,1)} %dynamic-slice_bitcast_fusion.1), channel_id=1, source_target_pairs={{0,8},{8,0},{16,24},{24,16},{1,9},{9,1},{17,25},{25,17},{2,10},{10... | collective-permute-start | bytes 1843208 | tf_op jit(solution)/shard_map/ppermute | solution.py:77
  352.5 20.4 %collective-permute-start.47 = (bf16[96,1536]{1,0:T(8,128)(2,1)}, bf16[96,1536]{1,0:T(8,128)(2,1)S(1)}, u32[]{:S(2)}, u32[]{:S(2)}) collective-permute-start(bf16[96,1536]{1,0:T(8,128)(2,1)} %get-tuple-element.157), channel_id=1, source_target_pairs={{0,16},{8,24},{16,0},{24,8},{1,17},{9,25},{17,1},{25,9},{2,18},{10... | collective-permute-start | bytes 884744 | tf_op jit(solution)/shard_map/ppermute | solution.py:77
  353.2 25.5 %collective-permute-start.49 = (bf16[192,768]{1,0:T(8,128)(2,1)}, bf16[192,768]{1,0:T(8,128)(2,1)}, u32[]{:S(2)}, u32[]{:S(2)}) collective-permute-start(bf16[192,768]{1,0:T(8,128)(2,1)} %get-tuple-element.159), channel_id=1, source_target_pairs={{0,16},{8,24},{16,0},{24,8},{1,17},{9,25},{17,1},{25,9},{2,18},{10... | collective-permute-start | bytes 884744 | tf_op jit(solution)/shard_map/ppermute | solution.py:77
  354.6 25.9 %collective-permute-start.50 = (bf16[192,768]{1,0:T(8,128)(2,1)}, bf16[192,768]{1,0:T(8,128)(2,1)S(1)}, u32[]{:S(2)}, u32[]{:S(2)}) collective-permute-start(bf16[192,768]{1,0:T(8,128)(2,1)} %get-tuple-element.160), channel_id=1, source_target_pairs={{0,8},{8,0},{16,24},{24,16},{1,9},{9,1},{17,25},{25,17},{2,10},{10... | collective-permute-start | bytes 884744 | tf_op jit(solution)/shard_map/ppermute | solution.py:77
  365.7 17.5 %collective-permute-start.48 = (bf16[96,1536]{1,0:T(8,128)(2,1)}, bf16[96,1536]{1,0:T(8,128)(2,1)}, u32[]{:S(2)}, u32[]{:S(2)}) collective-permute-start(bf16[96,1536]{1,0:T(8,128)(2,1)} %get-tuple-element.158), channel_id=1, source_target_pairs={{0,8},{8,0},{16,24},{24,16},{1,9},{9,1},{17,25},{25,17},{2,10},{10... | collective-permute-start | bytes 884744 | tf_op jit(solution)/shard_map/ppermute | solution.py:77
  368.0 31.9 %collective-permute-start.43 = (bf16[256,768]{1,0:T(8,128)(2,1)}, bf16[256,768]{1,0:T(8,128)(2,1)S(1)}, u32[]{:S(2)}, u32[]{:S(2)}) collective-permute-start(bf16[256,768]{1,0:T(8,128)(2,1)} %get-tuple-element.187), channel_id=1, source_target_pairs={{1,0},{2,1},{3,2},{4,3},{5,4},{6,5},{7,6},{9,8},{10,9},{11,10},{12... | collective-permute-start | bytes 1179656 | tf_op jit(solution)/shard_map/ppermute | solution.py:1026
  372.9 27.8 %collective-permute-start.42 = (bf16[256,768]{1,0:T(8,128)(2,1)}, bf16[256,768]{1,0:T(8,128)(2,1)}, u32[]{:S(2)}, u32[]{:S(2)}) collective-permute-start(bf16[256,768]{1,0:T(8,128)(2,1)} %get-tuple-element.186), channel_id=1, source_target_pairs={{0,1},{1,2},{2,3},{3,4},{4,5},{5,6},{6,7},{8,9},{9,10},{10,11},{11... | collective-permute-start | bytes 1179656 | tf_op jit(solution)/shard_map/ppermute | solution.py:1029
  (93 other events, 457.6 us)
Sparse Core Ops, SparseCore 0:
  10.4 60.4 all-gather.2
  73.1 30.9 all-gather.4
  240.4 84.4 reduce-scatter.1
